TPU v7x, 32 devices: a whole 2x2x4 slice. The times are simulated.
32 devices in a mesh: dp: 4 (over x, core), space: 8 (over z, y).
Axes of the slice: x: 2, y: 2, z: 4, core: 2. Of those that a mesh axis runs over, the one named last changes fastest.
Arguments:
- field: bfloat16 [4, 32, 32, 16, 128], P('dp', 'space'), may hold values from -6 to 6
- cotangent: bfloat16 [4, 32, 32, 16, 128], P('dp', 'space'), may hold values from -6 to 6
- weights: float32 [16, 128, 2, 128, 128], P('space', 'dp'), may hold values from -0.375 to 0.375
- first_moment: float32 [16, 128, 2, 128, 128], P('space', 'dp'), may hold values from -6 to 6
- second_moment: float32 [16, 128, 2, 128, 128], P('space', 'dp'), may hold values from 0.01 to 10
Outputs:
- field_grad: bfloat16 [4, 32, 32, 16, 128], P('dp', 'space')
- new_weights: float32 [16, 128, 2, 128, 128], P('space', 'dp')
- new_first: float32 [16, 128, 2, 128, 128], P('space', 'dp')
- new_second: float32 [16, 128, 2, 128, 128], P('space', 'dp')
All inputs are finite; a program needn't handle non-finite values.
Results may differ from a plain program's by a relative error of at most 0.024.
Values may be sent and summed in bfloat16 or wider, within the bound.
No kernel may reach another device: no remote copies, remote signals or barrier semaphores. Data moves between devices by JAX's collectives and lax.ppermute only.
A program may use at most 128 MiB of HBM per device.

v0:
```python
import math

import jax
import jax.numpy as jnp
from jax import lax
from jax.sharding import PartitionSpec as P

C = 128
MX = 16
MY = 16
MZ = 8
NY = 32
NZ = 16
STEP = 100
MYZ = 128


decay_first = 0.9
decay_second = 0.999
learn_rate = 0.001
adam_floor = 1e-08


def trig_tables(length, modes_kept, signed):
    points = jnp.arange(length, dtype=jnp.int32)
    frequency = jnp.arange(modes_kept, dtype=jnp.int32) - (modes_kept // 2 if signed else 0)
    phases = jnp.mod(points[:, None] * frequency[None, :], length).astype(jnp.float32)
    angles = phases * (2.0 * math.pi / length)
    factor = 1.0 / math.sqrt(length)
    return (
        (jnp.cos(angles) * factor).astype(jnp.bfloat16),
        (jnp.sin(angles) * factor).astype(jnp.bfloat16),
    )


def forward_table(cosine, sine_part):
    real_row = jnp.stack([cosine, -sine_part], axis=-1)
    imag_row = jnp.stack([sine_part, cosine], axis=-1)
    return jnp.stack([real_row, imag_row], axis=1)


def inverse_table(cosine, sine_part):
    real_row = jnp.stack([cosine.T, sine_part.T], axis=-1)
    imag_row = jnp.stack([-sine_part.T, cosine.T], axis=-1)
    return jnp.stack([real_row, imag_row], axis=1)


def adam_update(weights, first_moment, second_moment, weight_grads):
    new_first = decay_first * first_moment + (1.0 - decay_first) * weight_grads
    new_second = decay_second * second_moment + (1.0 - decay_second) * weight_grads * weight_grads
    first_hat = new_first / (1.0 - decay_first**STEP)
    second_hat = new_second / (1.0 - decay_second**STEP)
    new_weights = weights - learn_rate * first_hat / (jnp.sqrt(second_hat) + adam_floor)
    return (new_weights, new_first, new_second)


def on_device(field, cotangent, weights, first_moment, second_moment):
    f32 = jnp.float32
    half = jnp.bfloat16
    slab_count = lax.axis_size("space")
    batch_local = field.shape[0]
    cells_x = field.shape[1]
    total_x = cells_x * slab_count
    cos_z, sin_z = trig_tables(NZ, MZ, False)
    cos_y, sin_y = trig_tables(NY, MY, True)
    cos_x, sin_x = trig_tables(total_x, MX, True)
    table_z = jnp.stack([cos_z, -sin_z], axis=1)
    table_y = forward_table(cos_y, sin_y)
    table_x = forward_table(cos_x, sin_x)
    back_table_x = inverse_table(cos_x, sin_x)
    back_table_y = inverse_table(cos_y, sin_y)
    back_table_z = jnp.stack([cos_z.T, -sin_z.T], axis=0)

    def yz_modes(slab_field):
        first_pass = jnp.einsum(
            "bxyzc,zpk->bxypkc", slab_field, table_z, preferred_element_type=f32
        ).astype(half)
        second = jnp.einsum(
            "bxypkc,ypmq->bxmkqc", first_pass, table_y, preferred_element_type=f32
        ).astype(half)
        return second.reshape(batch_local, cells_x, MYZ, 2, C)

    field_yz = yz_modes(field)
    cot_yz = yz_modes(cotangent)
    field_x, cot_x = (
        lax.all_to_all(field_yz, "space", split_axis=2, concat_axis=1, tiled=True),
        lax.all_to_all(cot_yz, "space", split_axis=2, concat_axis=1, tiled=True),
    )

    def along_x(slab_block):
        return jnp.einsum(
            "bxpjc,xjmq->bmpqc", slab_block, table_x, preferred_element_type=f32
        ).astype(half)

    field_hat, cot_hat = (
        lax.all_to_all(
            lax.all_to_all(along_x(field_x), "space", split_axis=1, concat_axis=2, tiled=True),
            "dp",
            split_axis=2,
            concat_axis=0,
            tiled=True,
        ),
        lax.all_to_all(
            lax.all_to_all(along_x(cot_x), "space", split_axis=1, concat_axis=2, tiled=True),
            "dp",
            split_axis=2,
            concat_axis=0,
            tiled=True,
        ),
    )
    order_in = "bmpj"
    rotated = jnp.stack([cot_hat[:, :, :, 1], -cot_hat[:, :, :, 0]], axis=3)
    form_in = order_in + "c," + order_in + "o->mpco"
    grad_real = jnp.einsum(form_in, field_hat, cot_hat, preferred_element_type=f32)
    grad_imag = jnp.einsum(form_in, field_hat, rotated, preferred_element_type=f32)
    weight_grads = jnp.stack([grad_real, grad_imag], axis=2)
    half_weights = weights.astype(half)
    form_back = "mpjio," + order_in + "o->bmpi"
    back_real = jnp.einsum(form_back, half_weights, cot_hat, preferred_element_type=f32)
    back_imag = jnp.einsum(form_back, half_weights, rotated, preferred_element_type=f32)
    mode_grads = jnp.stack([back_real, back_imag], axis=3).astype(half)
    new_weights, new_first, new_second = adam_update(
        weights, first_moment, second_moment, weight_grads
    )
    pencils = lax.all_to_all(
        lax.all_to_all(mode_grads, "dp", split_axis=0, concat_axis=2, tiled=True),
        "space",
        split_axis=2,
        concat_axis=1,
        tiled=True,
    )
    back_x = jnp.einsum(
        "bmpjc,mjxq->bxpqc", pencils, back_table_x, preferred_element_type=f32
    ).astype(half)
    slab_modes = lax.all_to_all(back_x, "space", split_axis=1, concat_axis=2, tiled=True)
    unpacked = slab_modes.reshape(batch_local, cells_x, MY, MZ, 2, C)
    back_y = jnp.einsum(
        "bxmkjc,mjyq->bxyqkc", unpacked, back_table_y, preferred_element_type=f32
    ).astype(half)
    field_grad = jnp.einsum(
        "bxyqkc,qkz->bxyzc", back_y, back_table_z, preferred_element_type=f32
    ).astype(half)
    return (field_grad, new_weights, new_first, new_second)


def solution(mesh):
    placed = (
        P("dp", "space", None, None, None),
        P("dp", "space", None, None, None),
        P("space", "dp", None, None, None),
        P("space", "dp", None, None, None),
        P("space", "dp", None, None, None),
    )
    return jax.shard_map(
        on_device,
        mesh=mesh,
        in_specs=placed,
        out_specs=(
            P("dp", "space", None, None, None),
            P("space", "dp", None, None, None),
            P("space", "dp", None, None, None),
            P("space", "dp", None, None, None),
        ),
        check_vma=False,
    )
```

profile of v0, /device:TPU:0, one launch (start us, length us, event | category | flops | bytes accessed | tf_op | source)
XLA Modules:
  0.0 136.8 jit_solution(14939740274775634560)
XLA Ops:
  0.7 0.1 multiply_convert_fusion
  1.0 0.6 copy-done
  1.7 0.3 fusion.8
  2.0 0.3 fusion.16
  2.3 1.0 copy.81
  3.3 7.3 %all-to-all-start = ((bf16[1,4,128,2,128]{4,3,1,0,2:T(2,128)(2,1)}), bf16[1,4,128,2,128]{4,3,1,0,2:T(2,128)(2,1)S(1)}, u32[]{:S(2)}, u32[]{:S(2)}) async-start(bf16[1,4,128,2,128]{4,3,1,0,2:T(2,128)(2,1)} %copy.81), calls=%async_computation | async-start | bytes 524288 | tf_op jit(solution)/shard_map/all_to_all | solution.py:87
  10.6 1.3 fusion.9
  11.9 0.3 fusion.15
  12.3 1.0 copy.101
  13.2 6.3 %all-to-all-done = bf16[1,4,128,2,128]{4,3,1,0,2:T(2,128)(2,1)S(1)} async-done(((bf16[1,4,128,2,128]{4,3,1,0,2:T(2,128)(2,1)}), bf16[1,4,128,2,128]{4,3,1,0,2:T(2,128)(2,1)S(1)}, u32[]{:S(2)}, u32[]{:S(2)}) %all-to-all-start) | async-done | bytes 262176 | tf_op jit(solution)/shard_map/all_to_all | solution.py:87
  19.5 3.6 %all-to-all-start.6 = ((bf16[1,4,128,2,128]{4,3,1,0,2:T(2,128)(2,1)}), bf16[1,4,128,2,128]{4,3,1,0,2:T(2,128)(2,1)S(1)}, u32[]{:S(2)}, u32[]{:S(2)}) async-start(bf16[1,4,128,2,128]{4,3,1,0,2:T(2,128)(2,1)} %copy.101), calls=%async_computation.6 | async-start | bytes 524288 | tf_op jit(solution)/shard_map/all_to_all | solution.py:86
  23.1 0.2 copy.83
  23.3 0.2 fusion.27
  23.6 0.7 copy.84
  24.3 7.4 %all-to-all-done.6 = bf16[1,4,128,2,128]{4,3,1,0,2:T(2,128)(2,1)S(1)} async-done(((bf16[1,4,128,2,128]{4,3,1,0,2:T(2,128)(2,1)}), bf16[1,4,128,2,128]{4,3,1,0,2:T(2,128)(2,1)S(1)}, u32[]{:S(2)}, u32[]{:S(2)}) %all-to-all-start.6) | async-done | bytes 262176 | tf_op jit(solution)/shard_map/all_to_all | solution.py:86
  31.6 3.6 %all-to-all-start.1 = ((bf16[1,16,16,2,128]{4,2,3,0,1:T(8,128)(2,1)}), bf16[1,16,16,2,128]{4,2,3,0,1:T(8,128)(2,1)S(1)}, u32[]{:S(2)}, u32[]{:S(2)}) async-start(bf16[1,16,16,2,128]{4,2,3,0,1:T(8,128)(2,1)} %copy.84), calls=%async_computation.1 | async-start | bytes 262144 | tf_op jit(solution)/shard_map/all_to_all | solution.py:104
  35.4 0.2 copy.103
  35.6 0.2 fusion.26
  35.9 0.7 copy.104
  36.5 6.0 %all-to-all-done.1 = bf16[1,16,16,2,128]{4,2,3,0,1:T(8,128)(2,1)S(1)} async-done(((bf16[1,16,16,2,128]{4,2,3,0,1:T(8,128)(2,1)}), bf16[1,16,16,2,128]{4,2,3,0,1:T(8,128)(2,1)S(1)}, u32[]{:S(2)}, u32[]{:S(2)}) %all-to-all-start.1) | async-done | bytes 131104 | tf_op jit(solution)/shard_map/all_to_all | solution.py:104
  42.6 3.4 %all-to-all-start.7 = ((bf16[1,16,16,2,128]{4,2,3,0,1:T(8,128)(2,1)}), bf16[1,16,16,2,128]{4,2,3,0,1:T(8,128)(2,1)S(1)}, u32[]{:S(2)}, u32[]{:S(2)}) async-start(bf16[1,16,16,2,128]{4,2,3,0,1:T(8,128)(2,1)} %copy.104), calls=%async_computation.7 | async-start | bytes 262144 | tf_op jit(solution)/shard_map/all_to_all | solution.py:97
  46.2 0.8 copy.86
  47.0 6.3 %all-to-all-done.7 = bf16[1,16,16,2,128]{4,2,3,0,1:T(8,128)(2,1)S(1)} async-done(((bf16[1,16,16,2,128]{4,2,3,0,1:T(8,128)(2,1)}), bf16[1,16,16,2,128]{4,2,3,0,1:T(8,128)(2,1)S(1)}, u32[]{:S(2)}, u32[]{:S(2)}) %all-to-all-start.7) | async-done | bytes 131104 | tf_op jit(solution)/shard_map/all_to_all | solution.py:97
  53.2 3.3 %all-to-all-start.2 = ((bf16[1,2,128,2,128]{4,3,1,0,2:T(2,128)(2,1)}), bf16[1,2,128,2,128]{4,3,1,0,2:T(2,128)(2,1)S(1)}, u32[]{:S(2)}, u32[]{:S(2)}) async-start(bf16[1,2,128,2,128]{4,3,1,0,2:T(2,128)(2,1)} %copy.86), calls=%async_computation.2 | async-start | bytes 262144 | tf_op jit(solution)/shard_map/all_to_all | solution.py:103
  56.6 0.8 copy.106
  57.4 3.7 %all-to-all-done.2 = bf16[1,2,128,2,128]{4,3,1,0,2:T(2,128)(2,1)S(1)} async-done(((bf16[1,2,128,2,128]{4,3,1,0,2:T(2,128)(2,1)}), bf16[1,2,128,2,128]{4,3,1,0,2:T(2,128)(2,1)S(1)}, u32[]{:S(2)}, u32[]{:S(2)}) %all-to-all-start.2) | async-done | bytes 131104 | tf_op jit(solution)/shard_map/all_to_all | solution.py:103
  61.2 3.3 %all-to-all-start.8 = ((bf16[1,2,128,2,128]{4,3,1,0,2:T(2,128)(2,1)}), bf16[1,2,128,2,128]{4,3,1,0,2:T(2,128)(2,1)S(1)}, u32[]{:S(2)}, u32[]{:S(2)}) async-start(bf16[1,2,128,2,128]{4,3,1,0,2:T(2,128)(2,1)} %copy.106), calls=%async_computation.8 | async-start | bytes 262144 | tf_op jit(solution)/shard_map/all_to_all | solution.py:96
  64.5 0.2 copy.173
  64.7 4.6 %fusion.34 = bf16[4,2,32,1,128]{4,0,2,1,3:T(4,128)(2,1)S(1)} fusion(f32[2,32,2,128,128]{4,3,2,1,0:T(8,128)} %param.7, bf16[1,2,4,32,2,128]{5,4,1,3,2,0:T(2,128)(2,1)S(1)} %bitcast.248), kind=kOutput, calls=%fused_computation.42 | convolution fusion | flops 18907136 | bytes 8585216 | tf_op jit(solution)/shard_map/mpjio,bmpjo->bmpi/dot_general | solution.py:119
  69.3 4.6 %fusion.37 = bf16[4,2,32,1,128]{4,0,2,1,3:T(4,128)(2,1)S(1)} fusion(f32[2,32,2,128,128]{4,3,2,1,0:T(8,128)} %param.7, bf16[4,2,32,1,128]{4,0,3,2,1:T(4,128)(2,1)S(1)} %get-tuple-element.24, bf16[4,2,32,1,128]{4,0,3,2,1:T(4,128)(2,1)S(1)} %get-tuple-element.23), kind=kOutput, calls=%fused_computation.43 | convolution fusion | flops 19169280 | bytes 8585216 | tf_op jit(solution)/shard_map/mpjio,bmpjo->bmpi/dot_general | solution.py:120
  74.0 0.7 copy.89
  74.7 3.3 %all-to-all-start.3 = ((bf16[4,2,32,2,128]{4,2,1,3,0:T(8,128)(2,1)}), bf16[4,2,32,2,128]{4,2,1,3,0:T(8,128)(2,1)S(1)}, u32[]{:S(2)}, u32[]{:S(2)}) async-start(bf16[4,2,32,2,128]{4,2,1,3,0:T(8,128)(2,1)} %copy.89), calls=%async_computation.3 | async-start | bytes 262144 | tf_op jit(solution)/shard_map/all_to_all | solution.py:126
  78.0 2.8 %convolution_bitcast_fusion.1 = f32[2,32,1,128,128]{4,3,1,0,2:T(8,128)} fusion(bf16[1,2,4,32,2,128]{5,4,1,3,2,0:T(2,128)(2,1)S(1)} %bitcast.250, bf16[1,2,4,32,2,128]{5,4,1,3,2,0:T(2,128)(2,1)S(1)} %bitcast.249), kind=kOutput, calls=%fused_computation.8 | convolution fusion | flops 16777216 | bytes 4456448 | tf_op jit(solution)/shard_map/bmpjc,bmpjo->mpco/dot_general | solution.py:114
  80.8 1.8 %all-to-all-done.3 = bf16[4,2,32,2,128]{4,2,1,3,0:T(8,128)(2,1)S(1)} async-done(((bf16[4,2,32,2,128]{4,2,1,3,0:T(8,128)(2,1)}), bf16[4,2,32,2,128]{4,2,1,3,0:T(8,128)(2,1)S(1)}, u32[]{:S(2)}, u32[]{:S(2)}) %all-to-all-start.3) | async-done | bytes 131104 | tf_op jit(solution)/shard_map/all_to_all | solution.py:126
  82.6 0.8 copy.91
  83.4 3.4 %all-to-all-start.4 = ((bf16[1,2,128,2,128]{4,3,1,0,2:T(2,128)(2,1)}), bf16[1,2,128,2,128]{4,3,1,0,2:T(2,128)(2,1)S(1)}, u32[]{:S(2)}, u32[]{:S(2)}) async-start(bf16[1,2,128,2,128]{4,3,1,0,2:T(2,128)(2,1)} %copy.91), calls=%async_computation.4 | async-start | bytes 262144 | tf_op jit(solution)/shard_map/all_to_all | solution.py:125
  86.8 2.9 %convolution_bitcast_fusion = f32[2,32,1,128,128]{4,3,1,0,2:T(8,128)} fusion(bf16[1,2,4,32,2,128]{5,4,1,3,2,0:T(2,128)(2,1)S(1)} %bitcast.251, bf16[4,2,32,1,128]{4,0,3,2,1:T(4,128)(2,1)S(1)} %get-tuple-element.24, bf16[4,2,32,1,128]{4,0,3,2,1:T(4,128)(2,1)S(1)} %get-tuple-element.23), kind=kOutput, calls=%fused_computation.7 | convolution fusion | flops 17039360 | bytes 4456448 | tf_op jit(solution)/shard_map/bmpjc,bmpjo->mpco/dot_general | solution.py:115
  89.7 4.4 %all-to-all-done.4 = bf16[1,2,128,2,128]{4,3,1,0,2:T(2,128)(2,1)S(1)} async-done(((bf16[1,2,128,2,128]{4,3,1,0,2:T(2,128)(2,1)}), bf16[1,2,128,2,128]{4,3,1,0,2:T(2,128)(2,1)S(1)}, u32[]{:S(2)}, u32[]{:S(2)}) %all-to-all-start.4) | async-done | bytes 131104 | tf_op jit(solution)/shard_map/all_to_all | solution.py:125
  94.1 0.1 copy.93
  94.2 0.2 fusion.17
  94.5 0.8 copy.94
  95.3 3.6 %all-to-all-start.5 = ((bf16[1,32,16,2,128]{4,2,3,0,1:T(8,128)(2,1)}), bf16[1,32,16,2,128]{4,2,3,0,1:T(8,128)(2,1)S(1)}, u32[]{:S(2)}, u32[]{:S(2)}) async-start(bf16[1,32,16,2,128]{4,2,3,0,1:T(8,128)(2,1)} %copy.94), calls=%async_computation.5 | async-start | bytes 524288 | tf_op jit(solution)/shard_map/all_to_all | solution.py:135
  98.9 19.3 %copy_subtract_fusion = (f32[2,32,2,128,128]{4,3,1,0,2:T(8,128)}, f32[2,32,2,128,128]{4,3,1,0,2:T(8,128)}, f32[2,32,2,128,128]{4,3,1,0,2:T(8,128)}) fusion(f32[2,32,2,128,128]{4,3,2,1,0:T(8,128)} %param.7, f32[2,32,1,128,128]{4,3,1,0,2:T(8,128)} %convolution_bitcast_fusion, f32[2,32,1,128,128]{4,3,1,0,2:T(8,128)} %convolution_bitcast_fusion.1, ...), kind=kLoop, calls=%fused_computation.3 | loop fusion | flops 27262976 | bytes 58720256 | tf_op jit(solution)/shard_map/sub | solution.py:53
  118.2 8.9 %copy.111 = f32[2,32,2,128,128]{4,3,2,1,0:T(8,128)} copy(f32[2,32,2,128,128]{4,3,1,0,2:T(8,128)} %get-tuple-element.20) | data formatting | bytes 16777216
  127.1 4.2 %copy.112 = f32[2,32,2,128,128]{4,3,2,1,0:T(8,128)} copy(f32[2,32,2,128,128]{4,3,1,0,2:T(8,128)S(1)} %copy-done.2) | data formatting | bytes 16777216
  131.3 4.0 %copy.113 = f32[2,32,2,128,128]{4,3,2,1,0:T(8,128)} copy(f32[2,32,2,128,128]{4,3,1,0,2:T(8,128)S(1)} %bitcast.246) | data formatting | bytes 16777216
  135.3 0.3 fusion.11
  135.6 1.1 fusion.10
  (33 shorter events, 1.1 us)
Async XLA Ops:
  0.6 1.1 copy-start
  3.3 16.2 %all-to-all-start = ((bf16[1,4,128,2,128]{4,3,1,0,2:T(2,128)(2,1)}), bf16[1,4,128,2,128]{4,3,1,0,2:T(2,128)(2,1)S(1)}, u32[]{:S(2)}, u32[]{:S(2)}) async-start(bf16[1,4,128,2,128]{4,3,1,0,2:T(2,128)(2,1)} %copy.81), calls=%async_computation | async-start | bytes 524288 | tf_op jit(solution)/shard_map/all_to_all | solution.py:87
  19.5 12.2 %all-to-all-start.6 = ((bf16[1,4,128,2,128]{4,3,1,0,2:T(2,128)(2,1)}), bf16[1,4,128,2,128]{4,3,1,0,2:T(2,128)(2,1)S(1)}, u32[]{:S(2)}, u32[]{:S(2)}) async-start(bf16[1,4,128,2,128]{4,3,1,0,2:T(2,128)(2,1)} %copy.101), calls=%async_computation.6 | async-start | bytes 524288 | tf_op jit(solution)/shard_map/all_to_all | solution.py:86
  31.6 10.9 %all-to-all-start.1 = ((bf16[1,16,16,2,128]{4,2,3,0,1:T(8,128)(2,1)}), bf16[1,16,16,2,128]{4,2,3,0,1:T(8,128)(2,1)S(1)}, u32[]{:S(2)}, u32[]{:S(2)}) async-start(bf16[1,16,16,2,128]{4,2,3,0,1:T(8,128)(2,1)} %copy.84), calls=%async_computation.1 | async-start | bytes 262144 | tf_op jit(solution)/shard_map/all_to_all | solution.py:104
  42.6 10.7 %all-to-all-start.7 = ((bf16[1,16,16,2,128]{4,2,3,0,1:T(8,128)(2,1)}), bf16[1,16,16,2,128]{4,2,3,0,1:T(8,128)(2,1)S(1)}, u32[]{:S(2)}, u32[]{:S(2)}) async-start(bf16[1,16,16,2,128]{4,2,3,0,1:T(8,128)(2,1)} %copy.104), calls=%async_computation.7 | async-start | bytes 262144 | tf_op jit(solution)/shard_map/all_to_all | solution.py:97
  53.2 7.9 %all-to-all-start.2 = ((bf16[1,2,128,2,128]{4,3,1,0,2:T(2,128)(2,1)}), bf16[1,2,128,2,128]{4,3,1,0,2:T(2,128)(2,1)S(1)}, u32[]{:S(2)}, u32[]{:S(2)}) async-start(bf16[1,2,128,2,128]{4,3,1,0,2:T(2,128)(2,1)} %copy.86), calls=%async_computation.2 | async-start | bytes 262144 | tf_op jit(solution)/shard_map/all_to_all | solution.py:103
  61.2 13.5 %all-to-all-start.8 = ((bf16[1,2,128,2,128]{4,3,1,0,2:T(2,128)(2,1)}), bf16[1,2,128,2,128]{4,3,1,0,2:T(2,128)(2,1)S(1)}, u32[]{:S(2)}, u32[]{:S(2)}) async-start(bf16[1,2,128,2,128]{4,3,1,0,2:T(2,128)(2,1)} %copy.106), calls=%async_computation.8 | async-start | bytes 262144 | tf_op jit(solution)/shard_map/all_to_all | solution.py:96
  74.7 7.9 %all-to-all-start.3 = ((bf16[4,2,32,2,128]{4,2,1,3,0:T(8,128)(2,1)}), bf16[4,2,32,2,128]{4,2,1,3,0:T(8,128)(2,1)S(1)}, u32[]{:S(2)}, u32[]{:S(2)}) async-start(bf16[4,2,32,2,128]{4,2,1,3,0:T(8,128)(2,1)} %copy.89), calls=%async_computation.3 | async-start | bytes 262144 | tf_op jit(solution)/shard_map/all_to_all | solution.py:126
  83.4 10.7 %all-to-all-start.4 = ((bf16[1,2,128,2,128]{4,3,1,0,2:T(2,128)(2,1)}), bf16[1,2,128,2,128]{4,3,1,0,2:T(2,128)(2,1)S(1)}, u32[]{:S(2)}, u32[]{:S(2)}) async-start(bf16[1,2,128,2,128]{4,3,1,0,2:T(2,128)(2,1)} %copy.91), calls=%async_computation.4 | async-start | bytes 262144 | tf_op jit(solution)/shard_map/all_to_all | solution.py:125
  95.3 40.0 %all-to-all-start.5 = ((bf16[1,32,16,2,128]{4,2,3,0,1:T(8,128)(2,1)}), bf16[1,32,16,2,128]{4,2,3,0,1:T(8,128)(2,1)S(1)}, u32[]{:S(2)}, u32[]{:S(2)}) async-start(bf16[1,32,16,2,128]{4,2,3,0,1:T(8,128)(2,1)} %copy.94), calls=%async_computation.5 | async-start | bytes 524288 | tf_op jit(solution)/shard_map/all_to_all | solution.py:135
  118.2 8.9 %copy-start.2 = (f32[2,32,2,128,128]{4,3,1,0,2:T(8,128)S(1)}, f32[2,32,2,128,128]{4,3,1,0,2:T(8,128)}, u32[]{:S(2)}) copy-start(f32[2,32,2,128,128]{4,3,1,0,2:T(8,128)} %get-tuple-element.21) | copy-start | bytes 25165828
  118.2 13.1 %slice-start = ((s8[8388608]{0:T(1024)(128)(4,1)}), s8[4194304]{0:T(1024)(128)(4,1)S(1)}, s32[]{:S(2)}) async-start(s8[8388608]{0:T(1024)(128)(4,1)} %bitcast.245), calls=%async_computation.9 | async-start | bytes 8388608
  127.1 4.2 %slice-start.1 = ((s8[8388608]{0:T(1024)(128)(4,1)}), s8[4194304]{0:T(1024)(128)(4,1)S(1)}, s32[]{:S(2)}) async-start(s8[8388608]{0:T(1024)(128)(4,1)} %bitcast.245), calls=%async_computation.10 | async-start | bytes 8388608
  131.3 5.5 %copy-start.1 = (bf16[1,4,32,16,128]{4,3,2,1,0:T(8,128)(2,1)S(1)}, bf16[1,4,32,16,128]{4,3,2,1,0:T(8,128)(2,1)}, u32[]{:S(2)}) copy-start(bf16[1,4,32,16,128]{4,3,2,1,0:T(8,128)(2,1)} %param.6) | copy-start | bytes 1572868
where the time goes:
time: 138 us; the launch traced here: 137 us
  waiting for transfers between devices  35.9 us (26%)
  starting transfers between devices  34.8 us (25%)
  local copies, waits for them, and re-layouts  25.9 us (19%)
  other arithmetic  20.2 us (15%)
  matrix products  19.2 us (14%)
    sub x1, other arithmetic, adam_update(): weights - learn_rate * first_hat / (jnp.sqrt(second_hat) + adam_floor)  19.3 us
    unnamed x13, local copies, waits for them, and re-layouts  17.7 us
    all_to_all x1, waiting for transfers between devices, on_device(): lax.all_to_all(field_yz, 'space', split_axis=2, concat_axis=1, tiled=True)  7.39 us
    all_to_all x1, starting transfers between devices, on_device(): lax.all_to_all(cot_yz, 'space', split_axis=2, concat_axis=1, tiled=True)  7.28 us
    all_to_all x1, waiting for transfers between devices, on_device(): lax.all_to_all(along_x(field_x), 'space', split_axis=1, concat_axis=2, ti...  6.27 us
    all_to_all x1, waiting for transfers between devices, on_device(): lax.all_to_all(cot_yz, 'space', split_axis=2, concat_axis=1, tiled=True)  6.26 us
    all_to_all x1, waiting for transfers between devices, on_device(): lax.all_to_all(along_x(cot_x), 'space', split_axis=1, concat_axis=2, tile...  6.03 us
    dot_general x1, matrix products, on_device(): jnp.einsum(form_back, half_weights, rotated, preferred_element_type=f32)  4.58 us
  transfers between devices with their start and end apart: 9, of which 7 were waited for; matrix products, arithmetic and copies ran while one was open for 43% of the time, Pallas kernels for 0%

commit v1 on v0

v1 whole, which is shorter than its diff:
```python
import functools
import math

import jax
import jax.numpy as jnp
import ml_dtypes
import numpy as np
from jax import lax
from jax.experimental import pallas as pl
from jax.experimental.pallas import tpu as pltpu
from jax.sharding import PartitionSpec as P

C = 128
MX = 16
MY = 16
MZ = 8
NY = 32
NZ = 16
STEP = 100
MYZ = 128
QUAD = 4


decay_first = 0.9
decay_second = 0.999
learn_rate = 0.001
adam_floor = 1e-08

f32 = jnp.float32
half = jnp.bfloat16


def np_tables(length, modes_kept, signed):
    points = np.arange(length)
    frequency = np.arange(modes_kept) - (modes_kept // 2 if signed else 0)
    angles = np.mod(points[:, None] * frequency[None, :], length) * (2.0 * math.pi / length)
    factor = np.float32(1.0 / math.sqrt(length))
    cosine = (np.cos(angles).astype(np.float32) * factor).astype(ml_dtypes.bfloat16)
    sine = (np.sin(angles).astype(np.float32) * factor).astype(ml_dtypes.bfloat16)
    return cosine.astype(np.float64), sine.astype(np.float64)


def yz_table(dp_count):
    cos_z, sin_z = np_tables(NZ, MZ, False)
    cos_y, sin_y = np_tables(NY, MY, True)
    cy, sy = cos_y.T[:, None, :, None], sin_y.T[:, None, :, None]
    cz, sz = cos_z.T[None, :, None, :], sin_z.T[None, :, None, :]
    real = cy * cz - sy * sz
    imag = -(sy * cz + cy * sz)
    table = np.stack([real, imag], axis=2).reshape(MYZ, 2, NY * NZ)
    pencils = MYZ // dp_count // QUAD
    table = table.reshape(dp_count, QUAD, pencils, 2, NY * NZ).transpose(1, 0, 2, 3, 4)
    return table.reshape(QUAD, dp_count * pencils * 2, NY * NZ).astype(ml_dtypes.bfloat16)


def x_tables(total_x, halves, pencils):
    cos_x, sin_x = np_tables(total_x, MX, True)
    same = np.eye(pencils)
    span = total_x // halves
    forward, backward = [], []
    for part in range(halves):
        c, s = cos_x[part * span : (part + 1) * span], sin_x[part * span : (part + 1) * span]
        fwd = np.zeros((MX, pencils, 2, span, pencils, 2))
        fwd[:, :, 0, :, :, 0] = np.einsum("xm,pr->mpxr", c, same)
        fwd[:, :, 0, :, :, 1] = np.einsum("xm,pr->mpxr", s, same)
        fwd[:, :, 1, :, :, 0] = np.einsum("xm,pr->mpxr", -s, same)
        fwd[:, :, 1, :, :, 1] = np.einsum("xm,pr->mpxr", c, same)
        bwd = np.zeros((span, pencils, 2, MX, pencils, 2))
        bwd[:, :, 0, :, :, 0] = np.einsum("xm,pr->xpmr", c, same)
        bwd[:, :, 0, :, :, 1] = np.einsum("xm,pr->xpmr", -s, same)
        bwd[:, :, 1, :, :, 0] = np.einsum("xm,pr->xpmr", s, same)
        bwd[:, :, 1, :, :, 1] = np.einsum("xm,pr->xpmr", c, same)
        forward.append(fwd.reshape(MX * pencils * 2, span * pencils * 2))
        backward.append(bwd.reshape(span * pencils * 2, MX * pencils * 2))
    return np.stack(forward).astype(ml_dtypes.bfloat16), np.stack(backward).astype(ml_dtypes.bfloat16)


def gather_tables(batch, halves, modes, pencils):
    plain = np.zeros((modes, pencils, batch, 2, batch, halves, modes, pencils, 2))
    turned = np.zeros_like(plain)
    for m in range(modes):
        for p in range(pencils):
            for b in range(batch):
                plain[m, p, b, 0, b, :, m, p, 0] = 1.0
                plain[m, p, b, 1, b, :, m, p, 1] = 1.0
                turned[m, p, b, 0, b, :, m, p, 1] = 1.0
                turned[m, p, b, 1, b, :, m, p, 0] = -1.0
    rows = modes * pencils * batch * 2
    both = np.stack([plain.reshape(rows, -1), turned.reshape(rows, -1)])
    return both.astype(ml_dtypes.bfloat16)


def scatter_table(batch, modes, pencils):
    order = np.arange(modes * pencils * batch * 2).reshape(modes * pencils, batch, 2).transpose(1, 0, 2).reshape(-1)
    return np.eye(order.size)[order].astype(ml_dtypes.bfloat16)


def dot(a, b, dims=((1,), (0,))):
    return lax.dot_general(a, b, (dims, ((), ())), preferred_element_type=f32)


def yz_kernel(place, field, cotangent, table, *blocks):
    rows = table.shape[1]
    mixed = jnp.concatenate([table[place[0] ^ r] for r in range(QUAD)], axis=0)
    for which, source in enumerate((field, cotangent)):
        for x in range(0, source.shape[0], 2):
            pair = jnp.concatenate([source[x], source[x + 1]], axis=1)
            result = dot(mixed, pair).astype(half)
            for r in range(QUAD):
                piece = result[r * rows : (r + 1) * rows]
                blocks[r][which, x] = piece[:, :C]
                blocks[r][which, x + 1] = piece[:, C:]


def x_kernel(place, *refs):
    pieces, (table, out, held) = refs[:QUAD], refs[QUAD:]
    for r in range(QUAD):
        held[place[0] ^ r] = pieces[r][...]
    matrix = table[place[1]]
    fields, cells, rows = held.shape[1:4]
    height = matrix.shape[1] // QUAD // cells
    owners = rows // height
    spaces = out.shape[0] // owners
    for d in range(owners):
        columns = [
            jnp.concatenate(
                [held[q, f, x, d * height : (d + 1) * height, :] for q in range(QUAD) for x in range(cells)], axis=0
            )
            for f in range(fields)
        ]
        result = dot(matrix, jnp.concatenate(columns, axis=1)).astype(half)
        for f in range(fields):
            out[d * spaces : (d + 1) * spaces, f] = result[:, f * C : (f + 1) * C].reshape(spaces, -1, C)


def modes_kernel(arrived, weights, gather, scatter, sent, inputs, pairs):
    batch, halves, _, _, rows, _ = arrived.shape
    modes, _, pencils = weights.shape[:3]
    field = arrived[:, :, 0, 0].reshape(-1, C)
    cot = arrived[:, :, 0, 1].reshape(-1, C)
    both = dot(gather[0], jnp.concatenate([field, cot], axis=1))
    turned = dot(gather[1], cot)
    inputs[0] = both[:, :C].astype(half)
    pair = jnp.concatenate([both[:, C:], turned], axis=1).astype(half)
    pairs[0] = pair
    height = batch * 2
    results = []
    for m in range(modes):
        for p in range(0, pencils, 2):
            at = (m * pencils + p) * height
            columns = jnp.concatenate(
                [jnp.concatenate([weights[m, 0, p + k, 0], weights[m, 0, p + k, 1]], axis=1) for k in range(2)], axis=0
            ).astype(half)
            result = dot(pair[at : at + 2 * height], columns, ((1,), (1,)))
            results += [result[:height, :C], result[height:, C:]]
    grads = jnp.concatenate(results, axis=0).astype(half)
    spread = dot(scatter[...], grads).astype(half).reshape(batch, rows, C)
    for h in range(halves):
        sent[:, h, 0] = spread


def adam_kernel(inputs, pairs, weights, first, second, new_weights, new_first, new_second):
    count = weights.shape[0]
    height = inputs.shape[0] // count
    scale_first = learn_rate / (1.0 - decay_first**STEP)
    scale_second = 1.0 / (1.0 - decay_second**STEP)
    for k in range(count):
        u = inputs[k * height : (k + 1) * height, :]
        g = pairs[k * height : (k + 1) * height, :]
        grads = dot(u, g, ((0,), (0,)))
        for part in range(2):
            grad = grads[:, part * C : (part + 1) * C]
            m = decay_first * first[k, part] + (1.0 - decay_first) * grad
            v = decay_second * second[k, part] + (1.0 - decay_second) * grad * grad
            new_first[k, part] = m
            new_second[k, part] = v
            new_weights[k, part] = weights[k, part] - scale_first * m / (jnp.sqrt(v * scale_second) + adam_floor)


def back_x_kernel(place, arrived, table, *blocks):
    matrix = table[place[1]]
    cells, owners, height, _ = blocks[0].shape
    spaces = arrived.shape[0] // owners
    span = cells * height
    held = blocks[QUAD]
    for d in range(0, owners, 2):
        columns = jnp.concatenate(
            [arrived[k * spaces : (k + 1) * spaces].reshape(-1, C) for k in (d, d + 1)], axis=1
        )
        result = dot(matrix, columns).astype(half)
        for q in range(QUAD):
            piece = result[q * span : (q + 1) * span].reshape(cells, height, 2 * C)
            held[q, :, d] = piece[:, :, :C]
            held[q, :, d + 1] = piece[:, :, C:]
    for r in range(QUAD):
        blocks[r][...] = held[place[0] ^ r]


def back_yz_kernel(place, *refs):
    pieces, (table, out, held) = refs[:QUAD], refs[QUAD:]
    for r in range(QUAD):
        held[place[0] ^ r] = pieces[r][...]
    matrix = table[...]
    for x in range(0, out.shape[0], 2):
        columns = jnp.concatenate([held[:, k].reshape(-1, C) for k in (x, x + 1)], axis=1)
        result = dot(matrix, columns).astype(half)
        out[x] = result[:, :C]
        out[x + 1] = result[:, C:]


VMEM = pl.BlockSpec(memory_space=pltpu.VMEM)
SMEM = pl.BlockSpec(memory_space=pltpu.SMEM)
MIB = 1 << 20


def params(mib, **more):
    return pltpu.CompilerParams(vmem_limit_bytes=mib * MIB, **more)


def exchange(blocks, count):
    moved = [
        lax.ppermute(blocks[r], "space", [(s, s ^ r) for s in range(count)]) for r in range(1, QUAD)
    ]
    return [blocks[0]] + moved


def fast(field, cotangent, weights, first_moment, second_moment):
    spaces = lax.axis_size("space")
    owners = lax.axis_size("dp")
    cells = field.shape[1]
    total_x = cells * spaces
    halves = spaces // QUAD
    pencils = MYZ // owners // QUAD
    modes = MX // spaces
    height = pencils * 2
    s = lax.axis_index("space").astype(jnp.int32)
    place = jnp.stack([s % QUAD, s // QUAD])
    table_yz = yz_table(owners)
    table_x, back_table_x = x_tables(total_x, halves, pencils)
    back_table_yz = np.ascontiguousarray(table_yz.reshape(MYZ * 2, NY * NZ).T)
    gather = gather_tables(owners, halves, modes, pencils)
    scatter = scatter_table(owners, modes, pencils)

    blocks = pl.pallas_call(
        yz_kernel,
        out_shape=[jax.ShapeDtypeStruct((2, cells, owners * height, C), half)] * QUAD,
        in_specs=[SMEM, VMEM, VMEM, VMEM],
        out_specs=[VMEM] * QUAD,
        compiler_params=params(16),
        name="yz_modes",
    )(place, field.reshape(cells, NY * NZ, C), cotangent.reshape(cells, NY * NZ, C), jnp.asarray(table_yz))
    blocks = exchange(blocks, spaces)

    rows = modes * height
    partial = pl.pallas_call(
        x_kernel,
        out_shape=jax.ShapeDtypeStruct((owners * spaces, 2, rows, C), half),
        in_specs=[SMEM] + [VMEM] * (QUAD + 1),
        out_specs=VMEM,
        scratch_shapes=[pltpu.VMEM((QUAD, 2, cells, owners * height, C), half)],
        compiler_params=params(16),
        name="x_modes",
    )(place, *blocks, jnp.asarray(table_x))
    arrived = lax.all_to_all(partial, ("dp", "space"), 0, 0, tiled=True)
    arrived = arrived.reshape(owners, halves, QUAD, 2, rows, C)

    mode_rows = rows * owners
    whole = lambda *shape: pl.BlockSpec(shape, lambda q: (0,) * len(shape))
    sent, inputs, pairs = pl.pallas_call(
        modes_kernel,
        grid=(QUAD,),
        out_shape=[
            jax.ShapeDtypeStruct((owners, halves, QUAD, rows, C), half),
            jax.ShapeDtypeStruct((QUAD, mode_rows, C), half),
            jax.ShapeDtypeStruct((QUAD, mode_rows, 2 * C), half),
        ],
        in_specs=[
            pl.BlockSpec((owners, halves, 1, 2, rows, C), lambda q: (0, 0, q, 0, 0, 0)),
            pl.BlockSpec((modes, 1, pencils, 2, C, C), lambda q: (0, q, 0, 0, 0, 0)),
            whole(*gather.shape),
            whole(*scatter.shape),
        ],
        out_specs=[
            pl.BlockSpec((owners, halves, 1, rows, C), lambda q: (0, 0, q, 0, 0)),
            pl.BlockSpec((1, mode_rows, C), lambda q: (q, 0, 0)),
            pl.BlockSpec((1, mode_rows, 2 * C), lambda q: (q, 0, 0)),
        ],
        compiler_params=params(24),
        name="mode_grads",
    )(arrived, weights.reshape(modes, QUAD, pencils, 2, C, C), jnp.asarray(gather), jnp.asarray(scatter))

    returned = lax.all_to_all(
        sent.reshape(owners * spaces, rows, C), ("dp", "space"), 0, 0, tiled=True
    )

    chunk = pencils // 2
    steps = modes * QUAD * 2
    big = pl.BlockSpec((None, None, chunk, 2, C, C), lambda i: (i // (2 * QUAD), i // 2 % QUAD, i % 2, 0, 0, 0))
    per = chunk * owners * 2
    small = lambda width: pl.BlockSpec(
        (None, per, width), lambda i: (i // 2 % QUAD, i // (2 * QUAD) * 2 + i % 2, 0)
    )
    split = (modes, QUAD, pencils, 2, C, C)
    elements = weights.size
    new_weights, new_first, new_second = pl.pallas_call(
        adam_kernel,
        grid=(steps,),
        out_shape=[jax.ShapeDtypeStruct(split, f32)] * 3,
        in_specs=[small(C), small(2 * C), big, big, big],
        out_specs=[big] * 3,
        compiler_params=params(24),
        cost_estimate=pl.CostEstimate(
            flops=16 * elements, bytes_accessed=24 * elements, transcendentals=elements
        ),
        name="adam",
    )(inputs, pairs, weights.reshape(split), first_moment.reshape(split), second_moment.reshape(split))

    blocks = pl.pallas_call(
        back_x_kernel,
        out_shape=[jax.ShapeDtypeStruct((cells, owners, height, C), half)] * QUAD,
        in_specs=[SMEM, VMEM, VMEM],
        out_specs=[VMEM] * QUAD,
        scratch_shapes=[pltpu.VMEM((QUAD, cells, owners, height, C), half)],
        compiler_params=params(16),
        name="back_x",
    )(place, returned, jnp.asarray(back_table_x))
    blocks = exchange(blocks, spaces)
    field_grad = pl.pallas_call(
        back_yz_kernel,
        out_shape=jax.ShapeDtypeStruct((cells, NY * NZ, C), half),
        in_specs=[SMEM] + [VMEM] * (QUAD + 1),
        out_specs=VMEM,
        scratch_shapes=[pltpu.VMEM((QUAD, cells, owners, height, C), half)],
        compiler_params=params(16),
        name="back_yz",
    )(place, *blocks, jnp.asarray(back_table_yz))
    return (
        field_grad.reshape(field.shape),
        new_weights.reshape(weights.shape),
        new_first.reshape(weights.shape),
        new_second.reshape(weights.shape),
    )


def trig_tables(length, modes_kept, signed):
    cosine, sine_part = np_tables(length, modes_kept, signed)
    return jnp.asarray(cosine, half), jnp.asarray(sine_part, half)


def forward_table(cosine, sine_part):
    real_row = jnp.stack([cosine, -sine_part], axis=-1)
    imag_row = jnp.stack([sine_part, cosine], axis=-1)
    return jnp.stack([real_row, imag_row], axis=1)


def inverse_table(cosine, sine_part):
    real_row = jnp.stack([cosine.T, sine_part.T], axis=-1)
    imag_row = jnp.stack([-sine_part.T, cosine.T], axis=-1)
    return jnp.stack([real_row, imag_row], axis=1)


def adam_update(weights, first_moment, second_moment, weight_grads):
    new_first = decay_first * first_moment + (1.0 - decay_first) * weight_grads
    new_second = decay_second * second_moment + (1.0 - decay_second) * weight_grads * weight_grads
    first_hat = new_first / (1.0 - decay_first**STEP)
    second_hat = new_second / (1.0 - decay_second**STEP)
    new_weights = weights - learn_rate * first_hat / (jnp.sqrt(second_hat) + adam_floor)
    return (new_weights, new_first, new_second)


def general(field, cotangent, weights, first_moment, second_moment):
    slab_count = lax.axis_size("space")
    batch_local = field.shape[0]
    cells_x = field.shape[1]
    total_x = cells_x * slab_count
    cos_z, sin_z = trig_tables(NZ, MZ, False)
    cos_y, sin_y = trig_tables(NY, MY, True)
    cos_x, sin_x = trig_tables(total_x, MX, True)
    table_z = jnp.stack([cos_z, -sin_z], axis=1)
    table_y = forward_table(cos_y, sin_y)
    table_x = forward_table(cos_x, sin_x)
    back_table_x = inverse_table(cos_x, sin_x)
    back_table_y = inverse_table(cos_y, sin_y)
    back_table_z = jnp.stack([cos_z.T, -sin_z.T], axis=0)
    product = functools.partial(jnp.einsum, preferred_element_type=f32)

    def swap(values, axis, split, concat):
        return lax.all_to_all(values, axis, split_axis=split, concat_axis=concat, tiled=True)

    def to_modes(slab_field):
        first_pass = product("bxyzc,zpk->bxypkc", slab_field, table_z).astype(half)
        second = product("bxypkc,ypmq->bxmkqc", first_pass, table_y).astype(half)
        second = second.reshape(batch_local, cells_x, MYZ, 2, C)
        along = product("bxpjc,xjmq->bmpqc", swap(second, "space", 2, 1), table_x).astype(half)
        return swap(swap(along, "space", 1, 2), "dp", 2, 0)

    field_hat = to_modes(field)
    cot_hat = to_modes(cotangent)
    rotated = jnp.stack([cot_hat[:, :, :, 1], -cot_hat[:, :, :, 0]], axis=3)
    form_in = "bmpjc,bmpjo->mpco"
    weight_grads = jnp.stack([product(form_in, field_hat, cot_hat), product(form_in, field_hat, rotated)], axis=2)
    half_weights = weights.astype(half)
    form_back = "mpjio,bmpjo->bmpi"
    mode_grads = jnp.stack(
        [product(form_back, half_weights, cot_hat), product(form_back, half_weights, rotated)], axis=3
    ).astype(half)
    updated = adam_update(weights, first_moment, second_moment, weight_grads)
    pencils = swap(swap(mode_grads, "dp", 0, 2), "space", 2, 1)
    back_x = product("bmpjc,mjxq->bxpqc", pencils, back_table_x).astype(half)
    unpacked = swap(back_x, "space", 1, 2).reshape(batch_local, cells_x, MY, MZ, 2, C)
    back_y = product("bxmkjc,mjyq->bxyqkc", unpacked, back_table_y).astype(half)
    field_grad = product("bxyqkc,qkz->bxyzc", back_y, back_table_z).astype(half)
    return (field_grad, *updated)


def solution(mesh):
    owners, spaces = mesh.shape["dp"], mesh.shape["space"]
    grid = P("dp", "space", None, None, None)
    held = P("space", "dp", None, None, None)

    def on_device(field, *rest):
        fits = spaces % QUAD == 0 and MX % spaces == 0 and MYZ % (owners * QUAD * 8) == 0 and owners % 2 == 0
        fits = fits and field.shape[0] == 1 and field.shape[1] % 2 == 0
        return (fast if fits else general)(field, *rest)

    return jax.shard_map(
        on_device,
        mesh=mesh,
        in_specs=(grid, grid, held, held, held),
        out_specs=(grid, held, held, held),
        check_vma=False,
    )
```

time: 138 us -> 87.2 us (0.63)
  blocking collectives: 0 us -> 34.9 us
  waiting for transfers between devices: 35.9 us -> 5.99 us
  starting transfers between devices: 34.8 us -> 8.16 us
  Pallas kernels: 0 us -> 21.1 us
  other arithmetic: 20.2 us -> 0.08 us
  matrix products: 19.2 us -> 0 us
  local copies, waits for them, and re-layouts: 25.9 us -> 15.8 us
    all_to_all x9 -> x0, waiting for transfers between devices: 35.9 us -> none  [the longest x1 7.39 us: on_device(): lax.all_to_all(field_yz, 'space', split_axis=2, concat_axis=1, tiled=True)]
    all_to_all x0 -> x2, blocking collectives: none -> 34.9 us  [the longest x1 22.2 us: fast(): arrived = lax.all_to_all(partial, ('dp', 'space'), 0, 0, tiled=True)]
    all_to_all x9 -> x0, starting transfers between devices: 34.8 us -> none  [the longest x1 7.28 us: on_device(): lax.all_to_all(cot_yz, 'space', split_axis=2, concat_axis=1, tiled=True)]
    pallas_call x0 -> x6, Pallas kernels: none -> 21.1 us  [the longest x1 13.7 us: fast(): pl.pallas_call(adam_kernel, grid=(steps,), out_shape=[jax.ShapeDtypeStruc...]
    sub x2 -> x0, other arithmetic: 19.3 us -> none  [the longest x1 19.3 us: adam_update(): weights - learn_rate * first_hat / (jnp.sqrt(second_hat) + adam_floor)]
    dot_general x13 -> x0, matrix products: 19.2 us -> none  [the longest x1 4.58 us: on_device(): jnp.einsum(form_back, half_weights, rotated, preferred_element_type=f32)]
    ppermute x0 -> x6, starting transfers between devices: none -> 8.16 us  [exchange(): lax.ppermute(blocks[r], 'space', [(s, s ^ r) for s in range(count)])]
    ppermute x0 -> x6, waiting for transfers between devices: none -> 5.99 us  [exchange(): lax.ppermute(blocks[r], 'space', [(s, s ^ r) for s in range(count)])]
  transfers between devices with their start and end apart: 9 -> 6, of which waited for: 7 -> 3; matrix products, arithmetic and copies ran while one was open for 43% -> 0% of each run, Pallas kernels for 0% -> 16%
where the time goes in v1:
time: 87.2 us; the launch traced here: 86.7 us
  blocking collectives  34.9 us (40%)
  Pallas kernels  21.1 us (24%)
  local copies, waits for them, and re-layouts  15.8 us (18%)
  starting transfers between devices  8.16 us (9%)
  waiting for transfers between devices  5.99 us (7%)
    all_to_all x1, blocking collectives, fast(): arrived = lax.all_to_all(partial, ('dp', 'space'), 0, 0, tiled=True)  22.2 us
    unnamed x24, local copies, waits for them, and re-layouts  15.8 us
    pallas_call x1, Pallas kernels, fast(): pl.pallas_call(adam_kernel, grid=(steps,), out_shape=[jax.ShapeDtypeStruc...  13.7 us
    all_to_all x1, blocking collectives, fast(): lax.all_to_all(sent.reshape(owners * spaces, rows, C), ('dp', 'space'), 0...  12.7 us
    ppermute x6, starting transfers between devices, exchange(): lax.ppermute(blocks[r], 'space', [(s, s ^ r) for s in range(count)])  8.16 us
    ppermute x6, waiting for transfers between devices, exchange(): lax.ppermute(blocks[r], 'space', [(s, s ^ r) for s in range(count)])  5.99 us
    pallas_call x1, Pallas kernels, fast(): pl.pallas_call(modes_kernel, grid=(QUAD,), out_shape=[jax.ShapeDtypeStruc...  3.12 us
  transfers between devices with their start and end apart: 6, of which 3 were waited for; matrix products, arithmetic and copies ran while one was open for 0% of the time, Pallas kernels for 16%

profile of v1, /device:TPU:0, one launch (start us, length us, event | category | flops | bytes accessed | tf_op | source)
XLA Modules:
  0.0 86.7 jit_solution(16189067374254407736)
XLA Ops:
  0.6 0.1 pad_add_fusion.place
  0.7 0.0 copy-start.4
  0.7 1.0 %copy-done.4 = bf16[1,4,32,16,128]{4,3,2,1,0:T(8,128)(2,1)S(1)} copy-done((bf16[1,4,32,16,128]{4,3,2,1,0:T(8,128)(2,1)S(1)}, bf16[1,4,32,16,128]{4,3,2,1,0:T(8,128)(2,1)}, u32[]{:S(2)}) %copy-start.4) | copy-done | bytes 524312
  1.8 0.0 copy-start.5
  1.8 1.0 %copy-done.5 = bf16[1,4,32,16,128]{4,3,2,1,0:T(8,128)(2,1)S(1)} copy-done((bf16[1,4,32,16,128]{4,3,2,1,0:T(8,128)(2,1)S(1)}, bf16[1,4,32,16,128]{4,3,2,1,0:T(8,128)(2,1)}, u32[]{:S(2)}) %copy-start.5) | copy-done | bytes 524312
  2.8 0.0 copy-start.7
  2.8 0.9 %copy-done.7 = bf16[4,64,512]{2,1,0:T(8,128)(2,1)S(1)} copy-done((bf16[4,64,512]{2,1,0:T(8,128)(2,1)S(1)}, bf16[4,64,512]{2,1,0:T(8,128)(2,1)}, u32[]{:S(2)}) %copy-start.7) | copy-done | bytes 262168
  3.8 0.0 copy-start.8
  3.8 1.0 %yz_modes.1 = (bf16[2,4,64,128]{3,2,1,0:T(8,128)(2,1)S(1)}, bf16[2,4,64,128]{3,2,1,0:T(8,128)(2,1)S(1)}, bf16[2,4,64,128]{3,2,1,0:T(8,128)(2,1)S(1)}, bf16[2,4,64,128]{3,2,1,0:T(8,128)(2,1)S(1)}) custom-call(s32[2]{0:T(128)S(1)} %pad_add_fusion.place, bf16[4,512,128]{2,1,0:T(8,128)(2,1)S(1)} %bitcast.18, bf16[4,512,128]{2,1,0:T(8,128)(2,1)S(1)} %bitcast.19, ...), custom_call_target="tpu_custom_call" | custom-call | tf_op jit(solution)/shard_map/yz_modes/pallas_call | solution.py:244
  4.7 3.0 %collective-permute-start = (bf16[2,4,64,128]{3,2,1,0:T(8,128)(2,1)S(1)}, bf16[2,4,64,128]{3,2,1,0:T(8,128)(2,1)S(1)}, u32[]{:S(2)}, u32[]{:S(2)}) collective-permute-start(bf16[2,4,64,128]{3,2,1,0:T(8,128)(2,1)S(1)} %get-tuple-element.19), channel_id=1, source_target_pairs={{0,1},{1,0},{2,3},{3,2},{4,5},{5,4},{6,7},{7,6},{8,9},{9,8},{10,11... | collective-permute-start | bytes 393224 | tf_op jit(solution)/shard_map/ppermute | solution.py:222
  7.8 1.6 %collective-permute-start.1 = (bf16[2,4,64,128]{3,2,1,0:T(8,128)(2,1)S(1)}, bf16[2,4,64,128]{3,2,1,0:T(8,128)(2,1)S(1)}, u32[]{:S(2)}, u32[]{:S(2)}) collective-permute-start(bf16[2,4,64,128]{3,2,1,0:T(8,128)(2,1)S(1)} %get-tuple-element.20), channel_id=1, source_target_pairs={{0,2},{1,3},{2,0},{3,1},{4,6},{5,7},{6,4},{7,5},{8,10},{9,11},{10,... | collective-permute-start | bytes 393224 | tf_op jit(solution)/shard_map/ppermute | solution.py:222
  9.4 0.0 collective-permute-start.2
  9.4 1.9 %collective-permute-done.refs_1_ = bf16[2,4,64,128]{3,2,1,0:T(8,128)(2,1)S(1)} collective-permute-done((bf16[2,4,64,128]{3,2,1,0:T(8,128)(2,1)S(1)}, bf16[2,4,64,128]{3,2,1,0:T(8,128)(2,1)S(1)}, u32[]{:S(2)}, u32[]{:S(2)}) %collective-permute-start) | collective-permute-done | bytes 131104 | tf_op jit(solution)/shard_map/ppermute | solution.py:222
  11.3 2.9 %collective-permute-done.1.refs_2_ = bf16[2,4,64,128]{3,2,1,0:T(8,128)(2,1)S(1)} collective-permute-done((bf16[2,4,64,128]{3,2,1,0:T(8,128)(2,1)S(1)}, bf16[2,4,64,128]{3,2,1,0:T(8,128)(2,1)S(1)}, u32[]{:S(2)}, u32[]{:S(2)}) %collective-permute-start.1) | collective-permute-done | bytes 131104 | tf_op jit(solution)/shard_map/ppermute | solution.py:222
  14.1 1.2 %collective-permute-done.2.refs_3_ = bf16[2,4,64,128]{3,2,1,0:T(8,128)(2,1)S(1)} collective-permute-done((bf16[2,4,64,128]{3,2,1,0:T(8,128)(2,1)S(1)}, bf16[2,4,64,128]{3,2,1,0:T(8,128)(2,1)S(1)}, u32[]{:S(2)}, u32[]{:S(2)}) %collective-permute-start.2) | collective-permute-done | bytes 131104 | tf_op jit(solution)/shard_map/ppermute | solution.py:222
  15.3 0.0 copy-start.6
  15.3 0.9 %copy-done.6 = bf16[2,256,256]{2,1,0:T(8,128)(2,1)S(1)} copy-done((bf16[2,256,256]{2,1,0:T(8,128)(2,1)S(1)}, bf16[2,256,256]{2,1,0:T(8,128)(2,1)}, u32[]{:S(2)}) %copy-start.6) | copy-done | bytes 262168
  16.3 0.9 %x_modes.1 = bf16[32,2,32,128]{3,2,1,0:T(8,128)(2,1)S(1)} custom-call(s32[2]{0:T(128)S(1)} %pad_add_fusion.place, bf16[2,4,64,128]{3,2,1,0:T(8,128)(2,1)S(1)} %get-tuple-element.18.refs_0_, bf16[2,4,64,128]{3,2,1,0:T(8,128)(2,1)S(1)} %collective-permute-done.refs_1_, bf16[2,4,64,128]{3,2,1,0:T(8,128)(2,1)S(1)} %collective-permute-done.1.refs_2_, ...), custom_call_target="tpu_custom_call" | custom-call | tf_op jit(solution)/shard_map/x_modes/pallas_call | solution.py:255
  17.2 22.2 %all_to_all.10 = bf16[32,2,32,128]{3,2,1,0:T(8,128)(2,1)S(1)} all-to-all(bf16[32,2,32,128]{3,2,1,0:T(8,128)(2,1)S(1)} %x_modes.1), channel_id=1, replica_groups=mesh['dp'=4,'space'=8] {'dp','space'}, dimensions={0} | all-to-all | bytes 1048576 | tf_op jit(solution)/shard_map/all_to_all | solution.py:264
  39.3 0.0 copy-start
  39.3 3.4 %copy-done = f32[2,32,2,128,128]{4,3,2,1,0:T(8,128)S(1)} copy-done((f32[2,32,2,128,128]{4,3,2,1,0:T(8,128)S(1)}, f32[2,32,2,128,128]{4,3,2,1,0:T(8,128)}, u32[]{:S(2)}) %copy-start) | copy-done | bytes 8388632
  42.7 0.0 copy-start.10
  42.7 0.9 %copy-done.10 = bf16[2,128,256]{2,1,0:T(8,128)(2,1)S(1)} copy-done((bf16[2,128,256]{2,1,0:T(8,128)(2,1)S(1)}, bf16[2,128,256]{2,1,0:T(8,128)(2,1)}, u32[]{:S(2)}) %copy-start.10) | copy-done | bytes 131096
  43.6 0.0 copy-start.11
  43.6 0.8 copy-done.11
  44.4 0.0 copy-start.1
  44.4 3.1 %mode_grads.1 = (bf16[4,2,4,32,128]{4,3,2,1,0:T(8,128)(2,1)S(1)}, bf16[4,128,128]{2,1,0:T(8,128)(2,1)S(1)}, bf16[4,128,256]{2,1,0:T(8,128)(2,1)S(1)}) custom-call(bf16[4,2,4,2,32,128]{5,4,3,2,1,0:T(8,128)(2,1)S(1)} %bitcast.17, f32[2,4,8,2,128,128]{5,4,3,2,1,0:T(8,128)S(1)} %bitcast.13, bf16[2,128,256]{2,1,0:T(8,128)(2,1)S(1)} %copy-done.10, ...), custom_call_target="tpu_custom_call" | custom-call | tf_op jit(solution)/shard_map/mode_grads/pallas_call | solution.py:269
  47.5 12.7 %all_to_all.11.arrived = bf16[32,32,128]{2,1,0:T(8,128)(2,1)S(1)} all-to-all(bf16[32,32,128]{2,1,0:T(8,128)(2,1)S(1)} %bitcast.20), channel_id=1, replica_groups=mesh['dp'=4,'space'=8] {'dp','space'}, dimensions={0} | all-to-all | bytes 524288 | tf_op jit(solution)/shard_map/all_to_all | solution.py:292
  60.2 0.0 copy-done.8
  60.2 0.8 back_x.1
  61.0 1.1 %collective-permute-start.3 = (bf16[4,4,16,128]{3,2,1,0:T(8,128)(2,1)S(1)}, bf16[4,4,16,128]{3,2,1,0:T(8,128)(2,1)S(1)}, u32[]{:S(2)}, u32[]{:S(2)}) collective-permute-start(bf16[4,4,16,128]{3,2,1,0:T(8,128)(2,1)S(1)} %get-tuple-element.24), channel_id=1, source_target_pairs={{0,1},{1,0},{2,3},{3,2},{4,5},{5,4},{6,7},{7,6},{8,9},{9,8},{10,11... | collective-permute-start | bytes 196616 | tf_op jit(solution)/shard_map/ppermute | solution.py:222
  62.1 0.0 collective-permute-start.4
  62.1 2.5 %collective-permute-start.5 = (bf16[4,4,16,128]{3,2,1,0:T(8,128)(2,1)S(1)}, bf16[4,4,16,128]{3,2,1,0:T(8,128)(2,1)S(1)}, u32[]{:S(2)}, u32[]{:S(2)}) collective-permute-start(bf16[4,4,16,128]{3,2,1,0:T(8,128)(2,1)S(1)} %get-tuple-element.26), channel_id=1, source_target_pairs={{0,3},{1,2},{2,1},{3,0},{4,7},{5,6},{6,5},{7,4},{8,11},{9,10},{10,... | collective-permute-start | bytes 196616 | tf_op jit(solution)/shard_map/ppermute | solution.py:222
  64.6 0.0 copy-done.1
  64.6 0.0 copy-start.2
  64.6 3.4 %copy-done.2 = f32[2,32,2,128,128]{4,3,2,1,0:T(8,128)S(1)} copy-done((f32[2,32,2,128,128]{4,3,2,1,0:T(8,128)S(1)}, f32[2,32,2,128,128]{4,3,2,1,0:T(8,128)}, u32[]{:S(2)}) %copy-start.2) | copy-done | bytes 8388632
  68.0 0.0 copy-start.3
  68.0 3.4 %copy-done.3 = f32[2,32,2,128,128]{4,3,2,1,0:T(8,128)S(1)} copy-done((f32[2,32,2,128,128]{4,3,2,1,0:T(8,128)S(1)}, f32[2,32,2,128,128]{4,3,2,1,0:T(8,128)}, u32[]{:S(2)}) %copy-start.3) | copy-done | bytes 8388632
  71.4 0.0 copy-start.9
  71.4 13.7 %adam.1 = (f32[2,4,8,2,128,128]{5,4,3,2,1,0:T(8,128)}, f32[2,4,8,2,128,128]{5,4,3,2,1,0:T(8,128)}, f32[2,4,8,2,128,128]{5,4,3,2,1,0:T(8,128)}) custom-call(bf16[4,128,128]{2,1,0:T(8,128)(2,1)S(1)} %get-tuple-element.27.inputs, bf16[4,128,256]{2,1,0:T(8,128)(2,1)S(1)} %get-tuple-element.28.pairs, f32[2,4,8,2,128,128]{5,4,3,2,1,0:T(8,128)S(1)} %bitcast.14, ...), custom_call_target="tpu_custom_call" | custom-call | flops 33554432 | bytes 50331648 | tf_op jit(solution)/shard_map/adam/pallas_call | solution.py:305
  85.0 0.0 collective-permute-done.3.refs_1_
  85.0 0.0 collective-permute-done.4.refs_2_
  85.0 0.0 collective-permute-done.5.refs_3_
  85.0 0.0 copy-done.9
  85.0 1.6 %back_yz.1 = bf16[4,512,128]{2,1,0:T(8,128)(2,1)} custom-call(s32[2]{0:T(128)S(1)} %pad_add_fusion.place, bf16[4,4,16,128]{3,2,1,0:T(8,128)(2,1)S(1)} %get-tuple-element.23.refs_0_, bf16[4,4,16,128]{3,2,1,0:T(8,128)(2,1)S(1)} %collective-permute-done.3.refs_1_, bf16[4,4,16,128]{3,2,1,0:T(8,128)(2,1)S(1)} %collective-permute-done.4.refs_2_, ...), custom_call_target="tpu_custom_call" | custom-call | tf_op jit(solution)/shard_map/back_yz/pallas_call | solution.py:328
Async XLA Ops:
  0.7 1.0 %copy-start.4 = (bf16[1,4,32,16,128]{4,3,2,1,0:T(8,128)(2,1)S(1)}, bf16[1,4,32,16,128]{4,3,2,1,0:T(8,128)(2,1)}, u32[]{:S(2)}) copy-start(bf16[1,4,32,16,128]{4,3,2,1,0:T(8,128)(2,1)} %param.11) | copy-start | bytes 1572868
  1.8 1.0 %copy-start.5 = (bf16[1,4,32,16,128]{4,3,2,1,0:T(8,128)(2,1)S(1)}, bf16[1,4,32,16,128]{4,3,2,1,0:T(8,128)(2,1)}, u32[]{:S(2)}) copy-start(bf16[1,4,32,16,128]{4,3,2,1,0:T(8,128)(2,1)} %param.12) | copy-start | bytes 1572868
  2.8 0.9 %copy-start.7 = (bf16[4,64,512]{2,1,0:T(8,128)(2,1)S(1)}, bf16[4,64,512]{2,1,0:T(8,128)(2,1)}, u32[]{:S(2)}) copy-start(bf16[4,64,512]{2,1,0:T(8,128)(2,1)} %constant.42.clone.table) | copy-start | bytes 786436
  3.8 56.5 %copy-start.8 = (bf16[2,256,256]{2,1,0:T(8,128)(2,1)S(1)}, bf16[2,256,256]{2,1,0:T(8,128)(2,1)}, u32[]{:S(2)}) copy-start(bf16[2,256,256]{2,1,0:T(8,128)(2,1)} %constant.46.clone.table) | copy-start | bytes 786436
  4.7 6.5 %collective-permute-start = (bf16[2,4,64,128]{3,2,1,0:T(8,128)(2,1)S(1)}, bf16[2,4,64,128]{3,2,1,0:T(8,128)(2,1)S(1)}, u32[]{:S(2)}, u32[]{:S(2)}) collective-permute-start(bf16[2,4,64,128]{3,2,1,0:T(8,128)(2,1)S(1)} %get-tuple-element.19), channel_id=1, source_target_pairs={{0,1},{1,0},{2,3},{3,2},{4,5},{5,4},{6,7},{7,6},{8,9},{9,8},{10,11... | collective-permute-start | bytes 393224 | tf_op jit(solution)/shard_map/ppermute | solution.py:222
  7.8 6.4 %collective-permute-start.1 = (bf16[2,4,64,128]{3,2,1,0:T(8,128)(2,1)S(1)}, bf16[2,4,64,128]{3,2,1,0:T(8,128)(2,1)S(1)}, u32[]{:S(2)}, u32[]{:S(2)}) collective-permute-start(bf16[2,4,64,128]{3,2,1,0:T(8,128)(2,1)S(1)} %get-tuple-element.20), channel_id=1, source_target_pairs={{0,2},{1,3},{2,0},{3,1},{4,6},{5,7},{6,4},{7,5},{8,10},{9,11},{10,... | collective-permute-start | bytes 393224 | tf_op jit(solution)/shard_map/ppermute | solution.py:222
  9.4 6.0 %collective-permute-start.2 = (bf16[2,4,64,128]{3,2,1,0:T(8,128)(2,1)S(1)}, bf16[2,4,64,128]{3,2,1,0:T(8,128)(2,1)S(1)}, u32[]{:S(2)}, u32[]{:S(2)}) collective-permute-start(bf16[2,4,64,128]{3,2,1,0:T(8,128)(2,1)S(1)} %get-tuple-element.21), channel_id=1, source_target_pairs={{0,3},{1,2},{2,1},{3,0},{4,7},{5,6},{6,5},{7,4},{8,11},{9,10},{10,... | collective-permute-start | bytes 393224 | tf_op jit(solution)/shard_map/ppermute | solution.py:222
  15.3 1.0 %copy-start.6 = (bf16[2,256,256]{2,1,0:T(8,128)(2,1)S(1)}, bf16[2,256,256]{2,1,0:T(8,128)(2,1)}, u32[]{:S(2)}) copy-start(bf16[2,256,256]{2,1,0:T(8,128)(2,1)} %constant.43.clone.refs_4_) | copy-start | bytes 786436
  39.3 3.4 %copy-start = (f32[2,32,2,128,128]{4,3,2,1,0:T(8,128)S(1)}, f32[2,32,2,128,128]{4,3,2,1,0:T(8,128)}, u32[]{:S(2)}) copy-start(f32[2,32,2,128,128]{4,3,2,1,0:T(8,128)} %param.13) | copy-start | bytes 25165828
  42.7 0.9 %copy-start.10 = (bf16[2,128,256]{2,1,0:T(8,128)(2,1)S(1)}, bf16[2,128,256]{2,1,0:T(8,128)(2,1)}, u32[]{:S(2)}) copy-start(bf16[2,128,256]{2,1,0:T(8,128)(2,1)} %constant.44.clone.gather) | copy-start | bytes 393220
  43.6 0.8 copy-start.11
  44.4 20.2 %copy-start.1 = (f32[2,32,2,128,128]{4,3,2,1,0:T(8,128)S(1)}, f32[2,32,2,128,128]{4,3,2,1,0:T(8,128)}, u32[]{:S(2)}) copy-start(f32[2,32,2,128,128]{4,3,2,1,0:T(8,128)} %param.13) | copy-start | bytes 25165828
  61.0 24.0 %collective-permute-start.3 = (bf16[4,4,16,128]{3,2,1,0:T(8,128)(2,1)S(1)}, bf16[4,4,16,128]{3,2,1,0:T(8,128)(2,1)S(1)}, u32[]{:S(2)}, u32[]{:S(2)}) collective-permute-start(bf16[4,4,16,128]{3,2,1,0:T(8,128)(2,1)S(1)} %get-tuple-element.24), channel_id=1, source_target_pairs={{0,1},{1,0},{2,3},{3,2},{4,5},{5,4},{6,7},{7,6},{8,9},{9,8},{10,11... | collective-permute-start | bytes 196616 | tf_op jit(solution)/shard_map/ppermute | solution.py:222
  62.1 22.9 %collective-permute-start.4 = (bf16[4,4,16,128]{3,2,1,0:T(8,128)(2,1)S(1)}, bf16[4,4,16,128]{3,2,1,0:T(8,128)(2,1)S(1)}, u32[]{:S(2)}, u32[]{:S(2)}) collective-permute-start(bf16[4,4,16,128]{3,2,1,0:T(8,128)(2,1)S(1)} %get-tuple-element.25), channel_id=1, source_target_pairs={{0,2},{1,3},{2,0},{3,1},{4,6},{5,7},{6,4},{7,5},{8,10},{9,11},{10,... | collective-permute-start | bytes 196616 | tf_op jit(solution)/shard_map/ppermute | solution.py:222
  62.1 22.9 %collective-permute-start.5 = (bf16[4,4,16,128]{3,2,1,0:T(8,128)(2,1)S(1)}, bf16[4,4,16,128]{3,2,1,0:T(8,128)(2,1)S(1)}, u32[]{:S(2)}, u32[]{:S(2)}) collective-permute-start(bf16[4,4,16,128]{3,2,1,0:T(8,128)(2,1)S(1)} %get-tuple-element.26), channel_id=1, source_target_pairs={{0,3},{1,2},{2,1},{3,0},{4,7},{5,6},{6,5},{7,4},{8,11},{9,10},{10,... | collective-permute-start | bytes 196616 | tf_op jit(solution)/shard_map/ppermute | solution.py:222
  64.6 3.4 %copy-start.2 = (f32[2,32,2,128,128]{4,3,2,1,0:T(8,128)S(1)}, f32[2,32,2,128,128]{4,3,2,1,0:T(8,128)}, u32[]{:S(2)}) copy-start(f32[2,32,2,128,128]{4,3,2,1,0:T(8,128)} %param.14) | copy-start | bytes 25165828
  68.0 3.4 %copy-start.3 = (f32[2,32,2,128,128]{4,3,2,1,0:T(8,128)S(1)}, f32[2,32,2,128,128]{4,3,2,1,0:T(8,128)}, u32[]{:S(2)}) copy-start(f32[2,32,2,128,128]{4,3,2,1,0:T(8,128)} %param.15) | copy-start | bytes 25165828
  71.4 13.7 %copy-start.9 = (bf16[512,256]{1,0:T(8,128)(2,1)S(1)}, bf16[512,256]{1,0:T(8,128)(2,1)}, u32[]{:S(2)}) copy-start(bf16[512,256]{1,0:T(8,128)(2,1)} %constant.47.clone.refs_4_) | copy-start | bytes 786436

commit v2 on v1

v2 whole, which is shorter than its diff:
```python
import functools
import math

import jax
import jax.numpy as jnp
import ml_dtypes
import numpy as np
from jax import lax
from jax.experimental import pallas as pl
from jax.experimental.pallas import tpu as pltpu
from jax.sharding import PartitionSpec as P

C = 128
MX = 16
MY = 16
MZ = 8
NY = 32
NZ = 16
STEP = 100
MYZ = 128
QUAD = 4


decay_first = 0.9
decay_second = 0.999
learn_rate = 0.001
adam_floor = 1e-08

f32 = jnp.float32
half = jnp.bfloat16


def np_tables(length, modes_kept, signed):
    points = np.arange(length)
    frequency = np.arange(modes_kept) - (modes_kept // 2 if signed else 0)
    angles = np.mod(points[:, None] * frequency[None, :], length) * (2.0 * math.pi / length)
    factor = np.float32(1.0 / math.sqrt(length))
    cosine = (np.cos(angles).astype(np.float32) * factor).astype(ml_dtypes.bfloat16)
    sine = (np.sin(angles).astype(np.float32) * factor).astype(ml_dtypes.bfloat16)
    return cosine.astype(np.float64), sine.astype(np.float64)


def yz_table(dp_count):
    cos_z, sin_z = np_tables(NZ, MZ, False)
    cos_y, sin_y = np_tables(NY, MY, True)
    cy, sy = cos_y.T[:, None, :, None], sin_y.T[:, None, :, None]
    cz, sz = cos_z.T[None, :, None, :], sin_z.T[None, :, None, :]
    real = cy * cz - sy * sz
    imag = -(sy * cz + cy * sz)
    table = np.stack([real, imag], axis=2).reshape(MYZ, 2, NY * NZ)
    pencils = MYZ // dp_count // QUAD
    table = table.reshape(dp_count, QUAD, pencils, 2, NY * NZ).transpose(1, 0, 2, 3, 4)
    return table.reshape(QUAD, dp_count * pencils * 2, NY * NZ).astype(ml_dtypes.bfloat16)


def x_tables(total_x, halves, pencils):
    cos_x, sin_x = np_tables(total_x, MX, True)
    same = np.eye(pencils)
    span = total_x // halves
    forward, backward = [], []
    for part in range(halves):
        c, s = cos_x[part * span : (part + 1) * span], sin_x[part * span : (part + 1) * span]
        fwd = np.zeros((MX, pencils, 2, span, pencils, 2))
        fwd[:, :, 0, :, :, 0] = np.einsum("xm,pr->mpxr", c, same)
        fwd[:, :, 0, :, :, 1] = np.einsum("xm,pr->mpxr", s, same)
        fwd[:, :, 1, :, :, 0] = np.einsum("xm,pr->mpxr", -s, same)
        fwd[:, :, 1, :, :, 1] = np.einsum("xm,pr->mpxr", c, same)
        bwd = np.zeros((span, pencils, 2, MX, pencils, 2))
        bwd[:, :, 0, :, :, 0] = np.einsum("xm,pr->xpmr", c, same)
        bwd[:, :, 0, :, :, 1] = np.einsum("xm,pr->xpmr", -s, same)
        bwd[:, :, 1, :, :, 0] = np.einsum("xm,pr->xpmr", s, same)
        bwd[:, :, 1, :, :, 1] = np.einsum("xm,pr->xpmr", c, same)
        forward.append(fwd.reshape(MX * pencils * 2, span * pencils * 2))
        backward.append(bwd.reshape(span * pencils * 2, MX * pencils * 2))
    return np.stack(forward).astype(ml_dtypes.bfloat16), np.stack(backward).astype(ml_dtypes.bfloat16)


def gather_tables(batch, halves, modes, pencils):
    plain = np.zeros((modes, pencils, batch, 2, batch, halves, modes, pencils, 2))
    turned = np.zeros_like(plain)
    for m in range(modes):
        for p in range(pencils):
            for b in range(batch):
                plain[m, p, b, 0, b, :, m, p, 0] = 1.0
                plain[m, p, b, 1, b, :, m, p, 1] = 1.0
                turned[m, p, b, 0, b, :, m, p, 1] = 1.0
                turned[m, p, b, 1, b, :, m, p, 0] = -1.0
    rows = modes * pencils * batch * 2
    both = np.stack([plain.reshape(rows, -1), turned.reshape(rows, -1)])
    return both.astype(ml_dtypes.bfloat16)


def scatter_table(batch, modes, pencils):
    order = np.arange(modes * pencils * batch * 2).reshape(modes * pencils, batch, 2).transpose(1, 0, 2).reshape(-1)
    return np.eye(order.size)[order].astype(ml_dtypes.bfloat16)


def dot(a, b, dims=((1,), (0,))):
    return lax.dot_general(a, b, (dims, ((), ())), preferred_element_type=f32)


def yz_kernel(place, field, cotangent, table, *refs):
    blocks, (mixed, cells_in, sems) = refs[:QUAD], refs[QUAD:]
    rows = table.shape[1]
    cells = field.shape[0]
    loads = [
        pltpu.make_async_copy(table.at[place[0] ^ r], mixed.at[pl.ds(r * rows, rows)], sems.at[r]) for r in range(QUAD)
    ]
    for which, source in enumerate((field, cotangent)):
        for x in range(0, cells, 2):
            loads.append(
                pltpu.make_async_copy(source.at[x : x + 2], cells_in.at[which, x : x + 2], sems.at[len(loads)])
            )
    for load in loads:
        load.start()
    for load in loads[:QUAD]:
        load.wait()
    matrix = mixed[...]
    at = QUAD
    for which in range(2):
        for x in range(0, cells, 2):
            loads[at].wait()
            at += 1
            pair = jnp.concatenate([cells_in[which, x], cells_in[which, x + 1]], axis=1)
            result = dot(matrix, pair).astype(half)
            for r in range(QUAD):
                piece = result[r * rows : (r + 1) * rows]
                blocks[r][which, x] = piece[:, :C]
                blocks[r][which, x + 1] = piece[:, C:]


def x_transform(place, which, pieces, table, held):
    for r in range(QUAD):
        held[place[0] ^ r] = pieces[r][which]
    matrix = table[place[1]]
    cells, rows = held.shape[1:3]
    height = matrix.shape[1] // QUAD // cells
    results = []
    for d in range(0, rows // height, 2):
        columns = [
            jnp.concatenate(
                [held[q, x, k * height : (k + 1) * height, :] for q in range(QUAD) for x in range(cells)], axis=0
            )
            for k in (d, d + 1)
        ]
        result = dot(matrix, jnp.concatenate(columns, axis=1)).astype(half)
        results += [result[:, :C], result[:, C:]]
    return results


def x_field_kernel(place, *refs):
    pieces, (table, own, other, held, split) = refs[:QUAD], refs[QUAD:]
    for d, result in enumerate(x_transform(place, 0, pieces, table, held)):
        split[:, d * QUAD : (d + 1) * QUAD] = result.reshape(split.shape[0], QUAD, -1, C)
    own[...] = split[place[1]]
    other[...] = split[1 - place[1]]


def x_cot_kernel(place, *refs):
    pieces, (table, _, out, held) = refs[:QUAD], refs[QUAD:]
    results = x_transform(place, 1, pieces, table, held)
    spaces = out.shape[0] // len(results)
    for d, result in enumerate(results):
        out[d * spaces : (d + 1) * spaces] = result.reshape(spaces, -1, C)


def join_kernel(cot_in, own, come, after, cot_out, summed):
    del cot_in, after, cot_out
    summed[...] = (own[...].astype(f32) + come[...].astype(f32)).astype(half)


def start_all(loads):
    for load in loads:
        load.start()


def stage_weights_kernel(after, weights, *refs):
    count = (len(refs) - 3) // 2
    sources, weights_held, held = refs[:count], refs[count], refs[count + 1 : 2 * count + 1]
    rounded, sems = refs[2 * count + 1 :]
    del after
    pieces = 8
    modes, pencils = weights.shape[:2]
    each = modes * pencils // pieces
    loads = []
    for k in range(pieces):
        m, p = k * each // pencils, k * each % pencils
        loads.append(
            pltpu.make_async_copy(weights.at[m, p : p + each], weights_held.at[m, p : p + each], sems.at[k])
        )
    for source, target in zip(sources, held):
        loads.append(pltpu.make_async_copy(source, target, sems.at[len(loads)]))
    start_all(loads)
    for k in range(pieces):
        loads[k].wait()
        m, p = k * each // pencils, k * each % pencils

        def body(i, carry):
            for part in range(2):
                rounded[m, p + i, :, part * C : (part + 1) * C] = weights_held[m, p + i, part].astype(half)
            return carry

        lax.fori_loop(0, each, body, 0)
    for load in loads[pieces:]:
        load.wait()


def stage_moments_kernel(after, first, second, first_held, second_held, sems):
    del after
    loads = []
    pencils = first.shape[1]
    each = pencils // 4
    for source, target in ((first, first_held), (second, second_held)):
        for m in range(target.shape[0]):
            for p in range(0, pencils, each):
                loads.append(
                    pltpu.make_async_copy(source.at[m, p : p + each], target.at[m, p : p + each], sems.at[len(loads)])
                )
    start_all(loads)
    for load in loads:
        load.wait()


def modes_kernel(arrived, field, weights, gather, scatter, sent, pairs):
    batch, halves, quad, rows, _ = arrived.shape
    modes, pencils = weights.shape[0], weights.shape[1] // quad
    height = batch * 2
    sent[:, :, 1] = field[...].reshape(batch, quad, rows, C)
    for q in range(quad):
        cot = arrived[:, :, q].reshape(-1, C)
        pair = jnp.concatenate([dot(gather[0], cot), dot(gather[1], cot)], axis=1).astype(half)
        pairs[q] = pair
        results = []
        for m in range(modes):
            for p in range(0, pencils, 2):
                at = (m * pencils + p) * height
                first = q * pencils + p
                columns = weights[m, first : first + 2].reshape(2 * C, 2 * C)
                result = dot(pair[at : at + 2 * height], columns, ((1,), (1,)))
                results += [result[:height, :C], result[height:, C:]]
        grads = jnp.concatenate(results, axis=0).astype(half)
        sent[:, q, 0] = dot(scatter[0], grads).astype(half).reshape(batch, rows, C)


def sort_kernel(arrived, gather, back, inputs):
    batch, quad = arrived.shape[:2]
    back[...] = arrived[:, :, 0].reshape(back.shape)
    for q in range(quad):
        inputs[q] = dot(gather[1], arrived[:, q, 1].reshape(-1, C)).astype(half)


def adam_kernel(mode, inputs, pairs, weights, first, second, *refs):
    new_weights, new_first, new_second, token, held, sems = refs[-6:]
    new = (new_weights, new_first, new_second)
    modes, pencils = weights.shape[:2]
    steps, count = held.shape[1:3]
    height = inputs.shape[1] // (modes * (pencils // QUAD))
    per_quad = steps // QUAD
    scale_first = learn_rate / (1.0 - decay_first**STEP)
    scale_second = 1.0 / (1.0 - decay_second**STEP)

    def copies(i):
        return [
            pltpu.make_async_copy(held.at[o, i], new[o].at[mode, pl.ds(i * count, count)], sems.at[i, o])
            for o in range(3)
        ]

    def body(i, carry):
        rows = count * height
        row = pl.multiple_of((mode * per_quad + i % per_quad) * rows, rows)
        us = inputs[i // per_quad, pl.ds(row, rows), :]
        gs = pairs[i // per_quad, pl.ds(row, rows), :]
        for k in range(count):
            u = us[k * height : (k + 1) * height]
            g = gs[k * height : (k + 1) * height]
            grads = dot(u, g, ((0,), (0,)))
            p = i * count + k
            for part in range(2):
                grad = grads[:, part * C : (part + 1) * C]
                m = decay_first * first[mode, p, part] + (1.0 - decay_first) * grad
                v = decay_second * second[mode, p, part] + ((1.0 - decay_second) * grad) * grad
                held[1, i, k, part] = m
                held[2, i, k, part] = v
                level = v * scale_second
                inverse = lax.rsqrt(level)
                floored = level * inverse + adam_floor
                inverse = inverse * (2.0 - floored * inverse)
                held[0, i, k, part] = weights[mode, p, part] - (scale_first * m) * inverse
        for copy in copies(i):
            copy.start()
        return carry

    def finish(i, carry):
        for copy in copies(i):
            copy.wait()
        return carry

    lax.fori_loop(0, steps, body, 0)
    lax.fori_loop(0, steps, finish, 0)
    token[...] = jnp.zeros_like(token)


def back_x_kernel(place, own, come, table, after, *refs):
    blocks, (arrived, held) = refs[:QUAD], refs[QUAD:]
    arrived[place[1]] = own[...]
    arrived[1 - place[1]] = come[...]
    matrix = table[place[1]]
    cells, owners, height, _ = blocks[0].shape
    halves = arrived.shape[0]
    span = cells * height
    for d in range(0, owners, 2):
        columns = [
            jnp.concatenate([arrived[h, k * QUAD : (k + 1) * QUAD].reshape(-1, C) for h in range(halves)], axis=0)
            for k in (d, d + 1)
        ]
        result = dot(matrix, jnp.concatenate(columns, axis=1)).astype(half)
        for q in range(QUAD):
            piece = result[q * span : (q + 1) * span].reshape(cells, height, 2 * C)
            held[q, :, d] = piece[:, :, :C]
            held[q, :, d + 1] = piece[:, :, C:]
    for r in range(QUAD):
        blocks[r][...] = held[place[0] ^ r]


def back_yz_kernel(place, *refs):
    pieces, (table, after, out, held) = refs[:QUAD], refs[QUAD:]
    for r in range(QUAD):
        held[place[0] ^ r] = pieces[r][...]
    matrix = table[...]
    for x in range(0, out.shape[0], 2):
        columns = jnp.concatenate([held[:, k].reshape(-1, C) for k in (x, x + 1)], axis=1)
        result = dot(matrix, columns).astype(half)
        out[x] = result[:, :C]
        out[x + 1] = result[:, C:]


VMEM = pl.BlockSpec(memory_space=pltpu.VMEM)
SMEM = pl.BlockSpec(memory_space=pltpu.SMEM)
HBM = pl.BlockSpec(memory_space=pltpu.HBM)
ANY = pl.BlockSpec(memory_space=pl.ANY)
MIB = 1 << 20


def params(mib, **more):
    return pltpu.CompilerParams(vmem_limit_bytes=mib * MIB, **more)


def cost(size):
    return pl.CostEstimate(flops=0, bytes_accessed=size, transcendentals=0)


def in_hbm(values):
    return pltpu.with_memory_space_constraint(values, pltpu.HBM)


def exchange(blocks):
    moved = [lax.ppermute(blocks[r], "quad", [(q, q ^ r) for q in range(QUAD)]) for r in range(1, QUAD)]
    return [blocks[0]] + moved


def swap_halves(values):
    return lax.ppermute(values, "half", [(0, 1), (1, 0)])


def fast(field, cotangent, weights, first_moment, second_moment):
    halves = lax.axis_size("half")
    spaces = halves * QUAD
    owners = lax.axis_size("dp")
    cells = field.shape[1]
    total_x = cells * spaces
    pencils = MYZ // owners // QUAD
    modes = MX // spaces
    height = pencils * 2
    place = jnp.stack([lax.axis_index("quad"), lax.axis_index("half")]).astype(jnp.int32)
    table_yz = yz_table(owners)
    table_x, back_table_x = x_tables(total_x, halves, pencils)
    back_table_yz = np.ascontiguousarray(table_yz.reshape(MYZ * 2, NY * NZ).T)
    gather = gather_tables(owners, halves, modes, pencils)
    scatter = scatter_table(owners, modes, pencils)
    scatter = np.stack([scatter, scatter.T])
    vmem = lambda values: pltpu.VMEM(values.shape, values.dtype)

    flat = (cells, NY * NZ, C)
    blocks = pl.pallas_call(
        yz_kernel,
        out_shape=[pltpu.VMEM((2, cells, owners * height, C), half)] * QUAD,
        in_specs=[SMEM] + [HBM] * 3,
        out_specs=[VMEM] * QUAD,
        scratch_shapes=[
            pltpu.VMEM((MYZ * 2, NY * NZ), half),
            pltpu.VMEM((2,) + flat, half),
            pltpu.SemaphoreType.DMA((QUAD + cells,)),
        ],
        compiler_params=params(8),
        name="yz_modes",
    )(place, in_hbm(field.reshape(flat)), in_hbm(cotangent.reshape(flat)), in_hbm(jnp.asarray(table_yz)))

    split = (modes, QUAD * pencils, 2, C, C)
    big, first, second = weights.reshape(split), first_moment.reshape(split), second_moment.reshape(split)
    staged = [jnp.asarray(t) for t in (table_x, gather, scatter, back_table_x, back_table_yz)]
    weights_held, table_x, gather, scatter, back_table_x, back_table_yz, rounded = pl.pallas_call(
        stage_weights_kernel,
        out_shape=[vmem(big)] + [vmem(t) for t in staged] + [pltpu.VMEM((modes, QUAD * pencils, C, 2 * C), half)],
        in_specs=[ANY] + [HBM] * (1 + len(staged)),
        out_specs=[VMEM] * (2 + len(staged)),
        scratch_shapes=[pltpu.SemaphoreType.DMA((8 + len(staged),))],
        compiler_params=params(8),
        cost_estimate=cost(weights.size * 8),
        name="stage_weights",
    )(blocks[0], in_hbm(big), *[in_hbm(t) for t in staged])
    blocks = exchange(blocks)

    rows = modes * height
    per_half = (owners * QUAD, rows, C)
    gathered = pltpu.VMEM((QUAD, cells, owners * height, C), half)
    field_own, field_other = pl.pallas_call(
        x_field_kernel,
        out_shape=[pltpu.VMEM(per_half, half)] * 2,
        in_specs=[SMEM] + [VMEM] * (QUAD + 1),
        out_specs=[VMEM] * 2,
        scratch_shapes=[gathered, pltpu.VMEM((halves,) + per_half, half)],
        compiler_params=params(8),
        name="x_modes_field",
    )(place, *blocks, table_x)
    field_come = swap_halves(field_other)
    cot_part = pl.pallas_call(
        x_cot_kernel,
        out_shape=pltpu.VMEM((owners * spaces, rows, C), half),
        in_specs=[SMEM] + [VMEM] * (QUAD + 1) + [ANY],
        out_specs=VMEM,
        scratch_shapes=[gathered],
        compiler_params=params(8),
        name="x_modes_cot",
    )(place, *blocks, table_x, field_other)
    first_held, second_held = pl.pallas_call(
        stage_moments_kernel,
        out_shape=[vmem(first), vmem(second)],
        in_specs=[ANY] + [HBM] * 2,
        out_specs=[VMEM] * 2,
        scratch_shapes=[pltpu.SemaphoreType.DMA((8 * modes,))],
        compiler_params=params(8),
        cost_estimate=cost(weights.size * 8),
        name="stage_moments",
    )(field_other, in_hbm(first), in_hbm(second))
    cot_part, field_sum = pl.pallas_call(
        join_kernel,
        out_shape=[pltpu.VMEM((owners * spaces, rows, C), half), pltpu.VMEM(per_half, half)],
        in_specs=[VMEM] * 3 + [ANY],
        out_specs=[VMEM] * 2,
        input_output_aliases={0: 0},
        compiler_params=params(8),
        name="join",
    )(cot_part, field_own, field_come, first_held)
    arrived = lax.all_to_all(cot_part, ("dp", "half", "quad"), 0, 0, tiled=True)

    mode_rows = rows * owners
    sent, pairs = pl.pallas_call(
        modes_kernel,
        out_shape=[
            pltpu.VMEM((owners, QUAD, 2, rows, C), half),
            pltpu.VMEM((QUAD, mode_rows, 2 * C), half),
        ],
        in_specs=[VMEM] * 5,
        out_specs=[VMEM] * 2,
        compiler_params=params(8),
        name="mode_grads",
    )(arrived.reshape(owners, halves, QUAD, rows, C), field_sum, rounded, gather, scatter)

    returned = lax.all_to_all(
        sent.reshape(owners * QUAD, 2, rows, C), ("dp", "quad"), 0, 0, tiled=True
    )
    back, inputs = pl.pallas_call(
        sort_kernel,
        out_shape=[pltpu.VMEM(per_half, half), pltpu.VMEM((QUAD, mode_rows, C), half)],
        in_specs=[VMEM] * 2,
        out_specs=[VMEM] * 2,
        compiler_params=params(8),
        name="sort_modes",
    )(returned.reshape(owners, QUAD, 2, rows, C), scatter)
    back_come = swap_halves(back)

    count = 4
    steps = QUAD * pencils // count

    def adam(mode, after, *before):
        return pl.pallas_call(
            functools.partial(adam_kernel, mode),
            out_shape=[pltpu.HBM(split, f32)] * 3 + [pltpu.VMEM((8, C), f32)],
            in_specs=[VMEM] * 5 + [ANY] + [HBM] * len(before),
            out_specs=[HBM] * 3 + [VMEM],
            scratch_shapes=[
                pltpu.VMEM((3, steps, count, 2, C, C), f32),
                pltpu.SemaphoreType.DMA((steps, 3)),
            ],
            input_output_aliases={6 + k: k for k in range(len(before))},
            compiler_params=params(16),
            cost_estimate=cost(8 * weights.size),
            name="adam",
        )(inputs, pairs, weights_held, first_held, second_held, after, *before)

    *updated, token = adam(0, back)
    blocks = pl.pallas_call(
        back_x_kernel,
        out_shape=[pltpu.VMEM((cells, owners, height, C), half)] * QUAD,
        in_specs=[SMEM] + [VMEM] * 3 + [ANY],
        out_specs=[VMEM] * QUAD,
        scratch_shapes=[
            pltpu.VMEM((halves,) + per_half, half),
            pltpu.VMEM((QUAD, cells, owners, height, C), half),
        ],
        compiler_params=params(8),
        name="back_x",
    )(place, back, back_come, back_table_x, token)
    *updated, token = adam(1, blocks[1], *updated)
    blocks = exchange(blocks)
    field_grad = pl.pallas_call(
        back_yz_kernel,
        out_shape=jax.ShapeDtypeStruct((cells, NY * NZ, C), half),
        in_specs=[SMEM] + [VMEM] * (QUAD + 1) + [ANY],
        out_specs=VMEM,
        scratch_shapes=[pltpu.VMEM((QUAD, cells, owners, height, C), half)],
        compiler_params=params(8),
        name="back_yz",
    )(place, *blocks, back_table_yz, token)
    return (field_grad.reshape(field.shape), *[values.reshape(weights.shape) for values in updated])


def trig_tables(length, modes_kept, signed):
    cosine, sine_part = np_tables(length, modes_kept, signed)
    return jnp.asarray(cosine, half), jnp.asarray(sine_part, half)


def forward_table(cosine, sine_part):
    real_row = jnp.stack([cosine, -sine_part], axis=-1)
    imag_row = jnp.stack([sine_part, cosine], axis=-1)
    return jnp.stack([real_row, imag_row], axis=1)


def inverse_table(cosine, sine_part):
    real_row = jnp.stack([cosine.T, sine_part.T], axis=-1)
    imag_row = jnp.stack([-sine_part.T, cosine.T], axis=-1)
    return jnp.stack([real_row, imag_row], axis=1)


def adam_update(weights, first_moment, second_moment, weight_grads):
    new_first = decay_first * first_moment + (1.0 - decay_first) * weight_grads
    new_second = decay_second * second_moment + (1.0 - decay_second) * weight_grads * weight_grads
    first_hat = new_first / (1.0 - decay_first**STEP)
    second_hat = new_second / (1.0 - decay_second**STEP)
    new_weights = weights - learn_rate * first_hat / (jnp.sqrt(second_hat) + adam_floor)
    return (new_weights, new_first, new_second)


def general(field, cotangent, weights, first_moment, second_moment):
    slab_count = lax.axis_size("space")
    batch_local = field.shape[0]
    cells_x = field.shape[1]
    total_x = cells_x * slab_count
    cos_z, sin_z = trig_tables(NZ, MZ, False)
    cos_y, sin_y = trig_tables(NY, MY, True)
    cos_x, sin_x = trig_tables(total_x, MX, True)
    table_z = jnp.stack([cos_z, -sin_z], axis=1)
    table_y = forward_table(cos_y, sin_y)
    table_x = forward_table(cos_x, sin_x)
    back_table_x = inverse_table(cos_x, sin_x)
    back_table_y = inverse_table(cos_y, sin_y)
    back_table_z = jnp.stack([cos_z.T, -sin_z.T], axis=0)
    product = functools.partial(jnp.einsum, preferred_element_type=f32)

    def swap(values, axis, split, concat):
        return lax.all_to_all(values, axis, split_axis=split, concat_axis=concat, tiled=True)

    def to_modes(slab_field):
        first_pass = product("bxyzc,zpk->bxypkc", slab_field, table_z).astype(half)
        second = product("bxypkc,ypmq->bxmkqc", first_pass, table_y).astype(half)
        second = second.reshape(batch_local, cells_x, MYZ, 2, C)
        along = product("bxpjc,xjmq->bmpqc", swap(second, "space", 2, 1), table_x).astype(half)
        return swap(swap(along, "space", 1, 2), "dp", 2, 0)

    field_hat = to_modes(field)
    cot_hat = to_modes(cotangent)
    rotated = jnp.stack([cot_hat[:, :, :, 1], -cot_hat[:, :, :, 0]], axis=3)
    form_in = "bmpjc,bmpjo->mpco"
    weight_grads = jnp.stack([product(form_in, field_hat, cot_hat), product(form_in, field_hat, rotated)], axis=2)
    half_weights = weights.astype(half)
    form_back = "mpjio,bmpjo->bmpi"
    mode_grads = jnp.stack(
        [product(form_back, half_weights, cot_hat), product(form_back, half_weights, rotated)], axis=3
    ).astype(half)
    updated = adam_update(weights, first_moment, second_moment, weight_grads)
    pencils = swap(swap(mode_grads, "dp", 0, 2), "space", 2, 1)
    back_x = product("bmpjc,mjxq->bxpqc", pencils, back_table_x).astype(half)
    unpacked = swap(back_x, "space", 1, 2).reshape(batch_local, cells_x, MY, MZ, 2, C)
    back_y = product("bxmkjc,mjyq->bxyqkc", unpacked, back_table_y).astype(half)
    field_grad = product("bxyqkc,qkz->bxyzc", back_y, back_table_z).astype(half)
    return (field_grad, *updated)


def solution(mesh):
    owners, spaces = mesh.shape["dp"], mesh.shape["space"]
    pencils = MYZ // (owners * QUAD)
    if spaces == 2 * QUAD and MX == 2 * spaces and MYZ % (owners * QUAD * 8) == 0 and pencils * owners % 2 == 0:
        mesh = jax.sharding.Mesh(mesh.devices.reshape(owners, 2, QUAD), ("dp", "half", "quad"))
        space, on_device = ("half", "quad"), fast
    else:
        space, on_device = "space", general
    grid = P("dp", space, None, None, None)
    held = P(space, "dp", None, None, None)
    return jax.shard_map(
        on_device,
        mesh=mesh,
        in_specs=(grid, grid, held, held, held),
        out_specs=(grid, held, held, held),
        check_vma=False,
    )
```

time: 87.2 us -> 71.7 us (0.82)
  local copies, waits for them, and re-layouts: 15.8 us -> 0 us
  blocking collectives: 34.9 us -> 24 us
  Pallas kernels: 21.1 us -> 29.4 us
  starting transfers between devices: 8.16 us -> 12.2 us
  waiting for transfers between devices: 5.99 us -> 5 us
    unnamed x24 -> x0, local copies, waits for them, and re-layouts: 15.8 us -> none
    all_to_all x2, blocking collectives: 34.9 us -> 24 us  [the longest x1 14.3 us: fast(): arrived = lax.all_to_all(cot_part, ('dp', 'half', 'quad'), 0, 0, tiled=True)]
    pallas_call x5 -> x11, Pallas kernels: 19.4 us -> 27.7 us  [the longest x2 10.6 us: adam(): pl.pallas_call(functools.partial(adam_kernel, mode), out_shape=[pltpu.HBM...]
    ppermute x6 -> x8, starting transfers between devices: 8.16 us -> 12.2 us  [the longest x6 8.16 us: exchange(): lax.ppermute(blocks[r], 'quad', [(q, q ^ r) for q in range(QUAD)])]
    ppermute x6 -> x8, waiting for transfers between devices: 5.99 us -> 5 us  [the longest x2 2.77 us: swap_halves(): return lax.ppermute(values, 'half', [(0, 1), (1, 0)])]
  transfers between devices with their start and end apart: 6 -> 8, of which waited for: 3 -> 3; matrix products, arithmetic and copies ran while one was open for 0% -> 0% of each run, Pallas kernels for 16% -> 29%
where the time goes in v2:
time: 71.7 us; the launch traced here: 71.5 us
  Pallas kernels  29.4 us (41%)
  blocking collectives  24 us (33%)
  starting transfers between devices  12.2 us (17%)
  waiting for transfers between devices  5 us (7%)
  between operations  0.77 us (1%)
    all_to_all x1, blocking collectives, fast(): arrived = lax.all_to_all(cot_part, ('dp', 'half', 'quad'), 0, 0, tiled=True)  14.3 us
    pallas_call x2, Pallas kernels, adam(): pl.pallas_call(functools.partial(adam_kernel, mode), out_shape=[pltpu.HBM...  10.6 us
    all_to_all x1, blocking collectives, fast(): lax.all_to_all(sent.reshape(owners * QUAD, 2, rows, C), ('dp', 'quad'), 0...  9.74 us
    ppermute x6, starting transfers between devices, exchange(): lax.ppermute(blocks[r], 'quad', [(q, q ^ r) for q in range(QUAD)])  8.16 us
    pallas_call x1, Pallas kernels, fast(): pl.pallas_call(stage_moments_kernel, out_shape=[vmem(first), vmem(second)...  5.93 us
    ppermute x2, starting transfers between devices, swap_halves(): return lax.ppermute(values, 'half', [(0, 1), (1, 0)])  4.04 us
    pallas_call x1, Pallas kernels, fast(): pl.pallas_call(stage_weights_kernel, out_shape=[vmem(big)] + [vmem(t) for...  3.74 us
    pallas_call x1, Pallas kernels, fast(): pl.pallas_call(yz_kernel, out_shape=[pltpu.VMEM((2, cells, owners * heigh...  2.85 us
  transfers between devices with their start and end apart: 8, of which 3 were waited for; matrix products, arithmetic and copies ran while one was open for 0% of the time, Pallas kernels for 29%

profile of v2, /device:TPU:0, one launch (start us, length us, event | category | flops | bytes accessed | tf_op | source)
XLA Modules:
  0.0 71.5 jit_solution(2393674127497429723)
XLA Ops:
  0.6 0.1 pad_add_fusion.place
  0.7 2.8 %yz_modes.1 = (bf16[2,4,64,128]{3,2,1,0:T(8,128)(2,1)S(1)}, bf16[2,4,64,128]{3,2,1,0:T(8,128)(2,1)S(1)}, bf16[2,4,64,128]{3,2,1,0:T(8,128)(2,1)S(1)}, bf16[2,4,64,128]{3,2,1,0:T(8,128)(2,1)S(1)}) custom-call(s32[2]{0:T(128)S(1)} %pad_add_fusion.place, bf16[4,512,128]{2,1,0:T(8,128)(2,1)} %bitcast.11, bf16[4,512,128]{2,1,0:T(8,128)(2,1)} %bitcast.12, ...), custom_call_target="tpu_custom_call" | custom-call | tf_op jit(solution)/shard_map/yz_modes/pallas_call | solution.py:384
  3.6 3.0 %collective-permute-start = (bf16[2,4,64,128]{3,2,1,0:T(8,128)(2,1)S(1)}, bf16[2,4,64,128]{3,2,1,0:T(8,128)(2,1)S(1)}, u32[]{:S(2)}, u32[]{:S(2)}) collective-permute-start(bf16[2,4,64,128]{3,2,1,0:T(8,128)(2,1)S(1)} %get-tuple-element.38), channel_id=1, source_target_pairs={{0,1},{1,0},{2,3},{3,2},{4,5},{5,4},{6,7},{7,6},{8,9},{9,8},{10,11... | collective-permute-start | bytes 393224 | tf_op jit(solution)/shard_map/ppermute | solution.py:357
  6.6 1.6 %collective-permute-start.1 = (bf16[2,4,64,128]{3,2,1,0:T(8,128)(2,1)S(1)}, bf16[2,4,64,128]{3,2,1,0:T(8,128)(2,1)S(1)}, u32[]{:S(2)}, u32[]{:S(2)}) collective-permute-start(bf16[2,4,64,128]{3,2,1,0:T(8,128)(2,1)S(1)} %get-tuple-element.39), channel_id=1, source_target_pairs={{0,2},{1,3},{2,0},{3,1},{4,6},{5,7},{6,4},{7,5},{8,10},{9,11},{10,... | collective-permute-start | bytes 393224 | tf_op jit(solution)/shard_map/ppermute | solution.py:357
  8.2 0.0 collective-permute-start.2
  8.2 3.7 %stage_weights.1 = (f32[2,32,2,128,128]{4,3,2,1,0:T(8,128)S(1)}, bf16[2,256,256]{2,1,0:T(8,128)(2,1)S(1)}, bf16[2,128,256]{2,1,0:T(8,128)(2,1)S(1)}, bf16[2,128,...) custom-call(bf16[2,4,64,128]{3,2,1,0:T(8,128)(2,1)S(1)} %get-tuple-e, ...), custom_call_target="tpu_custom_call" | custom-call | bytes 16777216 | tf_op jit(solution)/shard_map/stage_weights/pallas_call | solution.py:401
  11.9 0.0 collective-permute-done.refs_1_
  11.9 1.0 %collective-permute-done.1.refs_2_ = bf16[2,4,64,128]{3,2,1,0:T(8,128)(2,1)S(1)} collective-permute-done((bf16[2,4,64,128]{3,2,1,0:T(8,128)(2,1)S(1)}, bf16[2,4,64,128]{3,2,1,0:T(8,128)(2,1)S(1)}, u32[]{:S(2)}, u32[]{:S(2)}) %collective-permute-start.1) | collective-permute-done | bytes 131104 | tf_op jit(solution)/shard_map/ppermute | solution.py:357
  13.0 1.2 %collective-permute-done.2.refs_3_ = bf16[2,4,64,128]{3,2,1,0:T(8,128)(2,1)S(1)} collective-permute-done((bf16[2,4,64,128]{3,2,1,0:T(8,128)(2,1)S(1)}, bf16[2,4,64,128]{3,2,1,0:T(8,128)(2,1)S(1)}, u32[]{:S(2)}, u32[]{:S(2)}) %collective-permute-start.2) | collective-permute-done | bytes 131104 | tf_op jit(solution)/shard_map/ppermute | solution.py:357
  14.2 0.8 %x_modes_field.1 = (bf16[16,32,128]{2,1,0:T(8,128)(2,1)S(1)}, bf16[16,32,128]{2,1,0:T(8,128)(2,1)S(1)}) custom-call(s32[2]{0:T(128)S(1)} %pad_add_fusion.place, bf16[2,4,64,128]{3,2,1,0:T(8,128)(2,1)S(1)} %get-tuple-element.37.after.refs_0_, bf16[2,4,64,128]{3,2,1,0:T(8,128)(2,1)S(1)} %collective-permute-done.refs_1_, ...), custom_call_target="tpu_custom_call" | custom-call | tf_op jit(solution)/shard_map/x_modes_field/pallas_call | solution.py:416
  15.0 2.8 %collective-permute-start.3 = (bf16[16,32,128]{2,1,0:T(8,128)(2,1)S(1)}, bf16[16,32,128]{2,1,0:T(8,128)(2,1)S(1)}, u32[]{:S(2)}, u32[]{:S(2)}) collective-permute-start(bf16[16,32,128]{2,1,0:T(8,128)(2,1)S(1)} %get-tuple-element.42.refs_5_.after), channel_id=1, source_target_pairs={{0,4},{4,0},{1,5},{5,1},{2,6},{6,2},{3,7},{7,3},{8,12},{12,8},{9,1... | collective-permute-start | bytes 393224 | tf_op jit(solution)/shard_map/ppermute | solution.py:362
  17.8 5.9 %stage_moments.1 = (f32[2,32,2,128,128]{4,3,2,1,0:T(8,128)S(1)}, f32[2,32,2,128,128]{4,3,2,1,0:T(8,128)S(1)}) custom-call(bf16[16,32,128]{2,1,0:T(8,128)(2,1)S(1)} %get-tuple-element.42.refs_5_.after, f32[2,32,2,128,128]{4,3,2,1,0:T(8,128)} %first.1, f32[2,32,2,128,128]{4,3,2,1,0:T(8,128)} %second.1), custom_call_target="tpu_custom_call" | custom-call | bytes 16777216 | tf_op jit(solution)/shard_map/stage_moments/pallas_call | solution.py:435
  23.7 0.8 %x_modes_cot.1.cot_in = bf16[32,32,128]{2,1,0:T(8,128)(2,1)S(1)} custom-call(s32[2]{0:T(128)S(1)} %pad_add_fusion.place, bf16[2,4,64,128]{3,2,1,0:T(8,128)(2,1)S(1)} %get-tuple-element.37.after.refs_0_, bf16[2,4,64,128]{3,2,1,0:T(8,128)(2,1)S(1)} %collective-permute-done.refs_1_, bf16[2,4,64,128]{3,2,1,0:T(8,128)(2,1)S(1)} %collective-permute-done.1.refs_2_, ...), custom_call_target="tpu_custom_call" | custom-call | tf_op jit(solution)/shard_map/x_modes_cot/pallas_call | solution.py:426
  24.5 0.0 collective-permute-done.3.come
  24.6 14.3 %all_to_all.10 = bf16[32,32,128]{2,1,0:T(8,128)(2,1)S(1)} all-to-all(bf16[32,32,128]{2,1,0:T(8,128)(2,1)S(1)} %get-tuple-element.45), channel_id=1, replica_groups=mesh['dp'=4,'half'=2,'quad'=4] {'dp','half','quad'}, dimensions={0} | all-to-all | bytes 524288 | tf_op jit(solution)/shard_map/all_to_all | solution.py:454
  38.9 2.0 %mode_grads.1 = (bf16[4,4,2,32,128]{4,3,2,1,0:T(8,128)(2,1)S(1)}, bf16[4,128,256]{2,1,0:T(8,128)(2,1)S(1)}) custom-call(bf16[4,2,4,32,128]{4,3,2,1,0:T(8,128)(2,1)S(1)} %bitcast.8, bf16[16,32,128]{2,1,0:T(8,128)(2,1)S(1)} %get-tuple-element.46.field, bf16[2,32,128,256]{3,2,1,0:T(8,128)(2,1)S(1)} %get-tuple-element.47.weights, ...), custom_call_target="tpu_custom_call" | custom-call | tf_op jit(solution)/shard_map/mode_grads/pallas_call | solution.py:457
  40.9 9.7 %all_to_all.11 = bf16[16,2,32,128]{3,2,1,0:T(8,128)(2,1)S(1)} all-to-all(bf16[16,2,32,128]{3,2,1,0:T(8,128)(2,1)S(1)} %bitcast.10), channel_id=1, replica_groups=mesh['dp'=4,'half'=2,'quad'=4] {'dp','quad'}, dimensions={0} | all-to-all | bytes 524288 | tf_op jit(solution)/shard_map/all_to_all | solution.py:469
  50.6 0.2 sort_modes.1
  50.8 1.2 %collective-permute-start.4 = (bf16[16,32,128]{2,1,0:T(8,128)(2,1)S(1)}, bf16[16,32,128]{2,1,0:T(8,128)(2,1)S(1)}, u32[]{:S(2)}, u32[]{:S(2)}) collective-permute-start(bf16[16,32,128]{2,1,0:T(8,128)(2,1)S(1)} %get-tuple-element.51.refs_0_.own), channel_id=1, source_target_pairs={{0,4},{4,0},{1,5},{5,1},{2,6},{6,2},{3,7},{7,3},{8,12},{12,8},{9,1... | collective-permute-start | bytes 393224 | tf_op jit(solution)/shard_map/ppermute | solution.py:362
  52.0 5.3 %adam.2 = (f32[2,32,2,128,128]{4,3,2,1,0:T(8,128)}, f32[2,32,2,128,128]{4,3,2,1,0:T(8,128)}, f32[2,32,2,128,128]{4,3,2,1,0:T(8,128)}, f32[8,128]{1,0:T(8,128)S(1)}) custom-call(bf16[4,128,128]{2,1,0:T(8,128)(2,1)S(1)} %get-tuple-element.53.inputs, bf16[4,128,256]{2,1,0:T(8,128)(2,1)S(1)} %get-tuple-element.54.pairs, ...), custom_call_target="tpu_custom_call" | custom-call | bytes 16777216 | tf_op jit(solution)/shard_map/adam/pallas_call | solution.py:486
  57.3 2.8 %collective-permute-done.4.come = bf16[16,32,128]{2,1,0:T(8,128)(2,1)S(1)} collective-permute-done((bf16[16,32,128]{2,1,0:T(8,128)(2,1)S(1)}, bf16[16,32,128]{2,1,0:T(8,128)(2,1)S(1)}, u32[]{:S(2)}, u32[]{:S(2)}) %collective-permute-start.4) | collective-permute-done | bytes 131104 | tf_op jit(solution)/shard_map/ppermute | solution.py:362
  60.1 0.8 %back_x.1 = (bf16[4,4,16,128]{3,2,1,0:T(8,128)(2,1)S(1)}, bf16[4,4,16,128]{3,2,1,0:T(8,128)(2,1)S(1)}, bf16[4,4,16,128]{3,2,1,0:T(8,128)(2,1)S(1)}, bf16[4,4,16,128]{3,2,1,0:T(8,128)(2,1)S(1)}) custom-call(s32[2]{0:T(128)S(1)} %pad_add_fusion.place, bf16[16,32,128]{2,1,0:T(8,128)(2,1)S(1)} %get-tuple-element.51.refs_0_.own, ...), custom_call_target="tpu_custom_call" | custom-call | tf_op jit(solution)/shard_map/back_x/pallas_call | solution.py:502
  60.9 0.1 collective-permute-start.6
  61.0 2.0 %collective-permute-start.7 = (bf16[4,4,16,128]{3,2,1,0:T(8,128)(2,1)S(1)}, bf16[4,4,16,128]{3,2,1,0:T(8,128)(2,1)S(1)}, u32[]{:S(2)}, u32[]{:S(2)}) collective-permute-start(bf16[4,4,16,128]{3,2,1,0:T(8,128)(2,1)S(1)} %get-tuple-element.61), channel_id=1, source_target_pairs={{0,3},{1,2},{2,1},{3,0},{4,7},{5,6},{6,5},{7,4},{8,11},{9,10},{10,... | collective-permute-start | bytes 196616 | tf_op jit(solution)/shard_map/ppermute | solution.py:357
  63.0 1.5 %collective-permute-start.5 = (bf16[4,4,16,128]{3,2,1,0:T(8,128)(2,1)S(1)}, bf16[4,4,16,128]{3,2,1,0:T(8,128)(2,1)S(1)}, u32[]{:S(2)}, u32[]{:S(2)}) collective-permute-start(bf16[4,4,16,128]{3,2,1,0:T(8,128)(2,1)S(1)} %get-tuple-element.59.refs_0_), channel_id=1, source_target_pairs={{0,1},{1,0},{2,3},{3,2},{4,5},{5,4},{6,7},{7,6},{8,9},{9,8},{10,11... | collective-permute-start | bytes 196616 | tf_op jit(solution)/shard_map/ppermute | solution.py:357
  64.5 5.3 %adam.3 = (f32[2,32,2,128,128]{4,3,2,1,0:T(8,128)}, f32[2,32,2,128,128]{4,3,2,1,0:T(8,128)}, f32[2,32,2,128,128]{4,3,2,1,0:T(8,128)}, f32[8,128]{1,0:T(8,128)S(1)}) custom-call(bf16[4,128,128]{2,1,0:T(8,128)(2,1)S(1)} %get-tuple-element.53.inputs, ...), custom_call_target="tpu_custom_call", output_to_operand_aliasing={{0}: (6, {}), {1}: (7, {}), {2}: (8, {})} | custom-call | bytes 16777216 | tf_op jit(solution)/shard_map/adam/pallas_call | solution.py:486
  69.8 0.0 collective-permute-done.6.refs_2_
  69.8 0.0 collective-permute-done.7.refs_3_
  69.8 0.0 collective-permute-done.5.refs_1_
  69.8 1.7 %back_yz.1 = bf16[4,512,128]{2,1,0:T(8,128)(2,1)} custom-call(s32[2]{0:T(128)S(1)} %pad_add_fusion.place, bf16[4,4,16,128]{3,2,1,0:T(8,128)(2,1)S(1)} %get-tuple-element.58.refs_0_, bf16[4,4,16,128]{3,2,1,0:T(8,128)(2,1)S(1)} %collective-permute-done.5.refs_1_, bf16[4,4,16,128]{3,2,1,0:T(8,128)(2,1)S(1)} %collective-permute-done.6.refs_2_, ...), custom_call_target="tpu_custom_call" | custom-call | tf_op jit(solution)/shard_map/back_yz/pallas_call | solution.py:516
  (1 shorter events, 0.0 us)
Async XLA Ops:
  3.6 8.4 %collective-permute-start = (bf16[2,4,64,128]{3,2,1,0:T(8,128)(2,1)S(1)}, bf16[2,4,64,128]{3,2,1,0:T(8,128)(2,1)S(1)}, u32[]{:S(2)}, u32[]{:S(2)}) collective-permute-start(bf16[2,4,64,128]{3,2,1,0:T(8,128)(2,1)S(1)} %get-tuple-element.38), channel_id=1, source_target_pairs={{0,1},{1,0},{2,3},{3,2},{4,5},{5,4},{6,7},{7,6},{8,9},{9,8},{10,11... | collective-permute-start | bytes 393224 | tf_op jit(solution)/shard_map/ppermute | solution.py:357
  6.6 6.4 %collective-permute-start.1 = (bf16[2,4,64,128]{3,2,1,0:T(8,128)(2,1)S(1)}, bf16[2,4,64,128]{3,2,1,0:T(8,128)(2,1)S(1)}, u32[]{:S(2)}, u32[]{:S(2)}) collective-permute-start(bf16[2,4,64,128]{3,2,1,0:T(8,128)(2,1)S(1)} %get-tuple-element.39), channel_id=1, source_target_pairs={{0,2},{1,3},{2,0},{3,1},{4,6},{5,7},{6,4},{7,5},{8,10},{9,11},{10,... | collective-permute-start | bytes 393224 | tf_op jit(solution)/shard_map/ppermute | solution.py:357
  8.2 6.0 %collective-permute-start.2 = (bf16[2,4,64,128]{3,2,1,0:T(8,128)(2,1)S(1)}, bf16[2,4,64,128]{3,2,1,0:T(8,128)(2,1)S(1)}, u32[]{:S(2)}, u32[]{:S(2)}) collective-permute-start(bf16[2,4,64,128]{3,2,1,0:T(8,128)(2,1)S(1)} %get-tuple-element.40), channel_id=1, source_target_pairs={{0,3},{1,2},{2,1},{3,0},{4,7},{5,6},{6,5},{7,4},{8,11},{9,10},{10,... | collective-permute-start | bytes 393224 | tf_op jit(solution)/shard_map/ppermute | solution.py:357
  15.0 9.6 %collective-permute-start.3 = (bf16[16,32,128]{2,1,0:T(8,128)(2,1)S(1)}, bf16[16,32,128]{2,1,0:T(8,128)(2,1)S(1)}, u32[]{:S(2)}, u32[]{:S(2)}) collective-permute-start(bf16[16,32,128]{2,1,0:T(8,128)(2,1)S(1)} %get-tuple-element.42.refs_5_.after), channel_id=1, source_target_pairs={{0,4},{4,0},{1,5},{5,1},{2,6},{6,2},{3,7},{7,3},{8,12},{12,8},{9,1... | collective-permute-start | bytes 393224 | tf_op jit(solution)/shard_map/ppermute | solution.py:362
  50.8 9.3 %collective-permute-start.4 = (bf16[16,32,128]{2,1,0:T(8,128)(2,1)S(1)}, bf16[16,32,128]{2,1,0:T(8,128)(2,1)S(1)}, u32[]{:S(2)}, u32[]{:S(2)}) collective-permute-start(bf16[16,32,128]{2,1,0:T(8,128)(2,1)S(1)} %get-tuple-element.51.refs_0_.own), channel_id=1, source_target_pairs={{0,4},{4,0},{1,5},{5,1},{2,6},{6,2},{3,7},{7,3},{8,12},{12,8},{9,1... | collective-permute-start | bytes 393224 | tf_op jit(solution)/shard_map/ppermute | solution.py:362
  60.9 8.9 %collective-permute-start.6 = (bf16[4,4,16,128]{3,2,1,0:T(8,128)(2,1)S(1)}, bf16[4,4,16,128]{3,2,1,0:T(8,128)(2,1)S(1)}, u32[]{:S(2)}, u32[]{:S(2)}) collective-permute-start(bf16[4,4,16,128]{3,2,1,0:T(8,128)(2,1)S(1)} %get-tuple-element.60), channel_id=1, source_target_pairs={{0,2},{1,3},{2,0},{3,1},{4,6},{5,7},{6,4},{7,5},{8,10},{9,11},{10,... | collective-permute-start | bytes 196616 | tf_op jit(solution)/shard_map/ppermute | solution.py:357
  61.0 8.8 %collective-permute-start.7 = (bf16[4,4,16,128]{3,2,1,0:T(8,128)(2,1)S(1)}, bf16[4,4,16,128]{3,2,1,0:T(8,128)(2,1)S(1)}, u32[]{:S(2)}, u32[]{:S(2)}) collective-permute-start(bf16[4,4,16,128]{3,2,1,0:T(8,128)(2,1)S(1)} %get-tuple-element.61), channel_id=1, source_target_pairs={{0,3},{1,2},{2,1},{3,0},{4,7},{5,6},{6,5},{7,4},{8,11},{9,10},{10,... | collective-permute-start | bytes 196616 | tf_op jit(solution)/shard_map/ppermute | solution.py:357
  63.0 6.8 %collective-permute-start.5 = (bf16[4,4,16,128]{3,2,1,0:T(8,128)(2,1)S(1)}, bf16[4,4,16,128]{3,2,1,0:T(8,128)(2,1)S(1)}, u32[]{:S(2)}, u32[]{:S(2)}) collective-permute-start(bf16[4,4,16,128]{3,2,1,0:T(8,128)(2,1)S(1)} %get-tuple-element.59.refs_0_), channel_id=1, source_target_pairs={{0,1},{1,0},{2,3},{3,2},{4,5},{5,4},{6,7},{7,6},{8,9},{9,8},{10,11... | collective-permute-start | bytes 196616 | tf_op jit(solution)/shard_map/ppermute | solution.py:357

commit v3 on v2

--- a/solution.py
+++ b/solution.py
@@ -99,40 +99,42 @@
     return lax.dot_general(a, b, (dims, ((), ())), preferred_element_type=f32)
 
 
-def yz_kernel(place, field, cotangent, table, *refs):
-    blocks, (mixed, cells_in, sems) = refs[:QUAD], refs[QUAD:]
+def yz_transform(source, mixed, blocks):
+    rows = mixed.shape[0] // QUAD
+    for x in range(0, source.shape[0], 2):
+        pair = jnp.concatenate([source[x], source[x + 1]], axis=1)
+        result = dot(mixed[...], pair).astype(half)
+        for r in range(QUAD):
+            piece = result[r * rows : (r + 1) * rows]
+            blocks[r][x] = piece[:, :C]
+            blocks[r][x + 1] = piece[:, C:]
+
+
+def yz_field_kernel(field, cotangent, table, later, *refs):
+    blocks, (mixed, cot_held, later_held, cells_in, sems) = refs[:QUAD], refs[QUAD:]
     rows = table.shape[1]
-    cells = field.shape[0]
     loads = [
-        pltpu.make_async_copy(table.at[place[0] ^ r], mixed.at[pl.ds(r * rows, rows)], sems.at[r]) for r in range(QUAD)
+        pltpu.make_async_copy(table.at[lax.axis_index("quad") ^ r], mixed.at[pl.ds(r * rows, rows)], sems.at[r]) for r in range(QUAD)
     ]
-    for which, source in enumerate((field, cotangent)):
-        for x in range(0, cells, 2):
-            loads.append(
-                pltpu.make_async_copy(source.at[x : x + 2], cells_in.at[which, x : x + 2], sems.at[len(loads)])
-            )
+    for source, target in ((field, cells_in), (cotangent, cot_held), (later, later_held)):
+        loads.append(pltpu.make_async_copy(source, target, sems.at[len(loads)]))
     for load in loads:
         load.start()
-    for load in loads[:QUAD]:
+    for load in loads[: QUAD + 1]:
         load.wait()
-    matrix = mixed[...]
-    at = QUAD
-    for which in range(2):
-        for x in range(0, cells, 2):
-            loads[at].wait()
-            at += 1
-            pair = jnp.concatenate([cells_in[which, x], cells_in[which, x + 1]], axis=1)
-            result = dot(matrix, pair).astype(half)
-            for r in range(QUAD):
-                piece = result[r * rows : (r + 1) * rows]
-                blocks[r][which, x] = piece[:, :C]
-                blocks[r][which, x + 1] = piece[:, C:]
-
-
-def x_transform(place, which, pieces, table, held):
+    yz_transform(cells_in, mixed, blocks)
+    for load in loads[QUAD + 1 :]:
+        load.wait()
+
+
+def yz_cot_kernel(cot_held, mixed, *blocks):
+    yz_transform(cot_held, mixed, blocks)
+
+
+def x_transform(pieces, table, held):
     for r in range(QUAD):
-        held[place[0] ^ r] = pieces[r][which]
-    matrix = table[place[1]]
+        held[lax.axis_index("quad") ^ r] = pieces[r][...]
+    matrix = table[lax.axis_index("half")]
     cells, rows = held.shape[1:3]
     height = matrix.shape[1] // QUAD // cells
     results = []
@@ -148,25 +150,18 @@
     return results
 
 
-def x_field_kernel(place, *refs):
-    pieces, (table, own, other, held, split) = refs[:QUAD], refs[QUAD:]
-    for d, result in enumerate(x_transform(place, 0, pieces, table, held)):
+def x_kernel(extra, *refs):
+    pieces, table, (own, other, held, split) = refs[:QUAD], refs[QUAD], refs[QUAD + 1 + extra :]
+    for d, result in enumerate(x_transform(pieces, table, held)):
         split[:, d * QUAD : (d + 1) * QUAD] = result.reshape(split.shape[0], QUAD, -1, C)
-    own[...] = split[place[1]]
-    other[...] = split[1 - place[1]]
-
-
-def x_cot_kernel(place, *refs):
-    pieces, (table, _, out, held) = refs[:QUAD], refs[QUAD:]
-    results = x_transform(place, 1, pieces, table, held)
-    spaces = out.shape[0] // len(results)
-    for d, result in enumerate(results):
-        out[d * spaces : (d + 1) * spaces] = result.reshape(spaces, -1, C)
-
-
-def join_kernel(cot_in, own, come, after, cot_out, summed):
-    del cot_in, after, cot_out
-    summed[...] = (own[...].astype(f32) + come[...].astype(f32)).astype(half)
+    own[...] = split[lax.axis_index("half")]
+    other[...] = split[1 - lax.axis_index("half")]
+
+
+def sum_kernel(field_own, field_come, cot_own, cot_come, *refs):
+    out = refs[-1]
+    for which, (own, come) in enumerate(((field_own, field_come), (cot_own, cot_come))):
+        out[:, which] = (own[...].astype(f32) + come[...].astype(f32)).astype(half)
 
 
 def start_all(loads):
@@ -174,26 +169,31 @@
         load.start()
 
 
-def stage_weights_kernel(after, weights, *refs):
+def stage_kernel(after, weights, *refs):
     count = (len(refs) - 3) // 2
     sources, weights_held, held = refs[:count], refs[count], refs[count + 1 : 2 * count + 1]
     rounded, sems = refs[2 * count + 1 :]
     del after
-    pieces = 8
     modes, pencils = weights.shape[:2]
-    each = modes * pencils // pieces
+    each = pencils // 4
+    spans = [(m, p) for m in range(modes) for p in range(0, pencils, each)]
     loads = []
-    for k in range(pieces):
-        m, p = k * each // pencils, k * each % pencils
-        loads.append(
-            pltpu.make_async_copy(weights.at[m, p : p + each], weights_held.at[m, p : p + each], sems.at[k])
-        )
+
+    def add(source, target):
+        loads.append(pltpu.make_async_copy(source, target, sems.at[len(loads)]))
+
+    for m, p in spans:
+        add(weights.at[m, p : p + each], weights_held.at[m, p : p + each])
     for source, target in zip(sources, held):
-        loads.append(pltpu.make_async_copy(source, target, sems.at[len(loads)]))
-    start_all(loads)
-    for k in range(pieces):
+        if len(source.shape) < 5:
+            add(source, target)
+        else:
+            for m, p in spans:
+                add(source.at[m, p : p + each], target.at[m, p : p + each])
+    for load in loads:
+        load.start()
+    for k, (m, p) in enumerate(spans):
         loads[k].wait()
-        m, p = k * each // pencils, k * each % pencils
 
         def body(i, carry):
             for part in range(2):
@@ -201,34 +201,20 @@
             return carry
 
         lax.fori_loop(0, each, body, 0)
-    for load in loads[pieces:]:
+    for load in loads[len(spans) :]:
         load.wait()
 
 
-def stage_moments_kernel(after, first, second, first_held, second_held, sems):
-    del after
-    loads = []
-    pencils = first.shape[1]
-    each = pencils // 4
-    for source, target in ((first, first_held), (second, second_held)):
-        for m in range(target.shape[0]):
-            for p in range(0, pencils, each):
-                loads.append(
-                    pltpu.make_async_copy(source.at[m, p : p + each], target.at[m, p : p + each], sems.at[len(loads)])
-                )
-    start_all(loads)
-    for load in loads:
-        load.wait()
-
-
-def modes_kernel(arrived, field, weights, gather, scatter, sent, pairs):
-    batch, halves, quad, rows, _ = arrived.shape
+def modes_kernel(arrived, weights, gather, scatter, sent, inputs, pairs):
+    batch, quad, _, rows, _ = arrived.shape
     modes, pencils = weights.shape[0], weights.shape[1] // quad
     height = batch * 2
-    sent[:, :, 1] = field[...].reshape(batch, quad, rows, C)
     for q in range(quad):
-        cot = arrived[:, :, q].reshape(-1, C)
-        pair = jnp.concatenate([dot(gather[0], cot), dot(gather[1], cot)], axis=1).astype(half)
+        field = arrived[:, q, 0].reshape(-1, C)
+        cot = arrived[:, q, 1].reshape(-1, C)
+        both = dot(gather[0], jnp.concatenate([field, cot], axis=1)).astype(half)
+        inputs[q] = both[:, :C]
+        pair = jnp.concatenate([both[:, C:], dot(gather[1], cot).astype(half)], axis=1)
         pairs[q] = pair
         results = []
         for m in range(modes):
@@ -239,42 +225,38 @@
                 result = dot(pair[at : at + 2 * height], columns, ((1,), (1,)))
                 results += [result[:height, :C], result[height:, C:]]
         grads = jnp.concatenate(results, axis=0).astype(half)
-        sent[:, q, 0] = dot(scatter[0], grads).astype(half).reshape(batch, rows, C)
-
-
-def sort_kernel(arrived, gather, back, inputs):
-    batch, quad = arrived.shape[:2]
-    back[...] = arrived[:, :, 0].reshape(back.shape)
-    for q in range(quad):
-        inputs[q] = dot(gather[1], arrived[:, q, 1].reshape(-1, C)).astype(half)
-
-
-def adam_kernel(mode, inputs, pairs, weights, first, second, *refs):
+        sent[:, q] = dot(scatter[...], grads).astype(half).reshape(batch, rows, C)
+
+
+def adam_kernel(begin, inputs, pairs, weights, first, second, *refs):
     new_weights, new_first, new_second, token, held, sems = refs[-6:]
     new = (new_weights, new_first, new_second)
     modes, pencils = weights.shape[:2]
     steps, count = held.shape[1:3]
     height = inputs.shape[1] // (modes * (pencils // QUAD))
-    per_quad = steps // QUAD
+    per_mode = pencils // count
+    per_quad = per_mode // QUAD
     scale_first = learn_rate / (1.0 - decay_first**STEP)
     scale_second = 1.0 / (1.0 - decay_second**STEP)
 
     def copies(i):
+        mode, at = (i + begin) // per_mode, (i + begin) % per_mode
         return [
-            pltpu.make_async_copy(held.at[o, i], new[o].at[mode, pl.ds(i * count, count)], sems.at[i, o])
+            pltpu.make_async_copy(held.at[o, i], new[o].at[mode, pl.ds(at * count, count)], sems.at[i, o])
             for o in range(3)
         ]
 
     def body(i, carry):
+        mode, at = (i + begin) // per_mode, (i + begin) % per_mode
         rows = count * height
-        row = pl.multiple_of((mode * per_quad + i % per_quad) * rows, rows)
-        us = inputs[i // per_quad, pl.ds(row, rows), :]
-        gs = pairs[i // per_quad, pl.ds(row, rows), :]
+        row = pl.multiple_of((mode * per_quad + at % per_quad) * rows, rows)
+        us = inputs[at // per_quad, pl.ds(row, rows), :]
+        gs = pairs[at // per_quad, pl.ds(row, rows), :]
         for k in range(count):
             u = us[k * height : (k + 1) * height]
             g = gs[k * height : (k + 1) * height]
             grads = dot(u, g, ((0,), (0,)))
-            p = i * count + k
+            p = at * count + k
             for part in range(2):
                 grad = grads[:, part * C : (part + 1) * C]
                 m = decay_first * first[mode, p, part] + (1.0 - decay_first) * grad
@@ -300,11 +282,11 @@
     token[...] = jnp.zeros_like(token)
 
 
-def back_x_kernel(place, own, come, table, after, *refs):
+def back_x_kernel(own, come, table, after, *refs):
     blocks, (arrived, held) = refs[:QUAD], refs[QUAD:]
-    arrived[place[1]] = own[...]
-    arrived[1 - place[1]] = come[...]
-    matrix = table[place[1]]
+    arrived[lax.axis_index("half")] = own[...]
+    arrived[1 - lax.axis_index("half")] = come[...]
+    matrix = table[lax.axis_index("half")]
     cells, owners, height, _ = blocks[0].shape
     halves = arrived.shape[0]
     span = cells * height
@@ -319,13 +301,13 @@
             held[q, :, d] = piece[:, :, :C]
             held[q, :, d + 1] = piece[:, :, C:]
     for r in range(QUAD):
-        blocks[r][...] = held[place[0] ^ r]
-
-
-def back_yz_kernel(place, *refs):
+        blocks[r][...] = held[lax.axis_index("quad") ^ r]
+
+
+def back_yz_kernel(*refs):
     pieces, (table, after, out, held) = refs[:QUAD], refs[QUAD:]
     for r in range(QUAD):
-        held[place[0] ^ r] = pieces[r][...]
+        held[lax.axis_index("quad") ^ r] = pieces[r][...]
     matrix = table[...]
     for x in range(0, out.shape[0], 2):
         columns = jnp.concatenate([held[:, k].reshape(-1, C) for k in (x, x + 1)], axis=1)
@@ -335,7 +317,6 @@
 
 
 VMEM = pl.BlockSpec(memory_space=pltpu.VMEM)
-SMEM = pl.BlockSpec(memory_space=pltpu.SMEM)
 HBM = pl.BlockSpec(memory_space=pltpu.HBM)
 ANY = pl.BlockSpec(memory_space=pl.ANY)
 MIB = 1 << 20
@@ -371,120 +352,107 @@
     pencils = MYZ // owners // QUAD
     modes = MX // spaces
     height = pencils * 2
-    place = jnp.stack([lax.axis_index("quad"), lax.axis_index("half")]).astype(jnp.int32)
     table_yz = yz_table(owners)
     table_x, back_table_x = x_tables(total_x, halves, pencils)
     back_table_yz = np.ascontiguousarray(table_yz.reshape(MYZ * 2, NY * NZ).T)
-    gather = gather_tables(owners, halves, modes, pencils)
+    gather = gather_tables(owners, 1, modes, pencils)
     scatter = scatter_table(owners, modes, pencils)
-    scatter = np.stack([scatter, scatter.T])
     vmem = lambda values: pltpu.VMEM(values.shape, values.dtype)
 
     flat = (cells, NY * NZ, C)
-    blocks = pl.pallas_call(
-        yz_kernel,
-        out_shape=[pltpu.VMEM((2, cells, owners * height, C), half)] * QUAD,
-        in_specs=[SMEM] + [HBM] * 3,
+    block = pltpu.VMEM((cells, owners * height, C), half)
+    *field_blocks, mixed, cot_held, table_x = pl.pallas_call(
+        yz_field_kernel,
+        out_shape=[block] * QUAD + [pltpu.VMEM((MYZ * 2, NY * NZ), half), pltpu.VMEM(flat, half), vmem(table_x)],
+        in_specs=[HBM] * 4,
+        out_specs=[VMEM] * (QUAD + 3),
+        scratch_shapes=[pltpu.VMEM(flat, half), pltpu.SemaphoreType.DMA((QUAD + 3,))],
+        compiler_params=params(8),
+        name="yz_modes_field",
+    )(
+        in_hbm(field.reshape(flat)),
+        in_hbm(cotangent.reshape(flat)),
+        in_hbm(jnp.asarray(table_yz)),
+        in_hbm(jnp.asarray(table_x)),
+    )
+    cot_blocks = pl.pallas_call(
+        yz_cot_kernel,
+        out_shape=[block] * QUAD,
+        in_specs=[VMEM] * 2,
         out_specs=[VMEM] * QUAD,
-        scratch_shapes=[
-            pltpu.VMEM((MYZ * 2, NY * NZ), half),
-            pltpu.VMEM((2,) + flat, half),
-            pltpu.SemaphoreType.DMA((QUAD + cells,)),
-        ],
-        compiler_params=params(8),
-        name="yz_modes",
-    )(place, in_hbm(field.reshape(flat)), in_hbm(cotangent.reshape(flat)), in_hbm(jnp.asarray(table_yz)))
+        compiler_params=params(8),
+        name="yz_modes_cot",
+    )(cot_held, mixed)
 
     split = (modes, QUAD * pencils, 2, C, C)
     big, first, second = weights.reshape(split), first_moment.reshape(split), second_moment.reshape(split)
-    staged = [jnp.asarray(t) for t in (table_x, gather, scatter, back_table_x, back_table_yz)]
-    weights_held, table_x, gather, scatter, back_table_x, back_table_yz, rounded = pl.pallas_call(
-        stage_weights_kernel,
+    field_blocks = exchange(field_blocks)
+    cot_blocks = exchange(cot_blocks)
+
+    rows = modes * height
+    per_half = (owners * QUAD, rows, C)
+    gathered = pltpu.VMEM((QUAD, cells, owners * height, C), half)
+
+    def x_modes(pieces, *after):
+        return pl.pallas_call(
+            functools.partial(x_kernel, len(after)),
+            out_shape=[pltpu.VMEM(per_half, half)] * 2,
+            in_specs=[VMEM] * (QUAD + 1) + [ANY] * len(after),
+            out_specs=[VMEM] * 2,
+            scratch_shapes=[gathered, pltpu.VMEM((halves,) + per_half, half)],
+            compiler_params=params(8),
+            name="x_modes",
+        )(*pieces, table_x, *after)
+
+    field_own, field_other = x_modes(field_blocks)
+    field_come = swap_halves(field_other)
+    cot_own, cot_other = x_modes(cot_blocks, field_other)
+    cot_come = swap_halves(cot_other)
+    staged = [jnp.asarray(t) for t in (gather, scatter, back_table_x, back_table_yz)] + [first, second]
+    weights_held, gather, scatter, back_table_x, back_table_yz, first_held, second_held, rounded = pl.pallas_call(
+        stage_kernel,
         out_shape=[vmem(big)] + [vmem(t) for t in staged] + [pltpu.VMEM((modes, QUAD * pencils, C, 2 * C), half)],
         in_specs=[ANY] + [HBM] * (1 + len(staged)),
         out_specs=[VMEM] * (2 + len(staged)),
-        scratch_shapes=[pltpu.SemaphoreType.DMA((8 + len(staged),))],
-        compiler_params=params(8),
-        cost_estimate=cost(weights.size * 8),
-        name="stage_weights",
-    )(blocks[0], in_hbm(big), *[in_hbm(t) for t in staged])
-    blocks = exchange(blocks)
-
-    rows = modes * height
-    per_half = (owners * QUAD, rows, C)
-    gathered = pltpu.VMEM((QUAD, cells, owners * height, C), half)
-    field_own, field_other = pl.pallas_call(
-        x_field_kernel,
-        out_shape=[pltpu.VMEM(per_half, half)] * 2,
-        in_specs=[SMEM] + [VMEM] * (QUAD + 1),
-        out_specs=[VMEM] * 2,
-        scratch_shapes=[gathered, pltpu.VMEM((halves,) + per_half, half)],
-        compiler_params=params(8),
-        name="x_modes_field",
-    )(place, *blocks, table_x)
-    field_come = swap_halves(field_other)
-    cot_part = pl.pallas_call(
-        x_cot_kernel,
-        out_shape=pltpu.VMEM((owners * spaces, rows, C), half),
-        in_specs=[SMEM] + [VMEM] * (QUAD + 1) + [ANY],
+        scratch_shapes=[pltpu.SemaphoreType.DMA((12 * modes + len(staged) - 2,))],
+        compiler_params=params(8),
+        cost_estimate=cost(0),
+        name="stage",
+    )(cot_other, in_hbm(big), *[in_hbm(t) for t in staged])
+    summed = pl.pallas_call(
+        sum_kernel,
+        out_shape=pltpu.VMEM((owners * QUAD, 2, rows, C), half),
+        in_specs=[VMEM] * 4 + [ANY],
         out_specs=VMEM,
-        scratch_shapes=[gathered],
-        compiler_params=params(8),
-        name="x_modes_cot",
-    )(place, *blocks, table_x, field_other)
-    first_held, second_held = pl.pallas_call(
-        stage_moments_kernel,
-        out_shape=[vmem(first), vmem(second)],
-        in_specs=[ANY] + [HBM] * 2,
-        out_specs=[VMEM] * 2,
-        scratch_shapes=[pltpu.SemaphoreType.DMA((8 * modes,))],
-        compiler_params=params(8),
-        cost_estimate=cost(weights.size * 8),
-        name="stage_moments",
-    )(field_other, in_hbm(first), in_hbm(second))
-    cot_part, field_sum = pl.pallas_call(
-        join_kernel,
-        out_shape=[pltpu.VMEM((owners * spaces, rows, C), half), pltpu.VMEM(per_half, half)],
-        in_specs=[VMEM] * 3 + [ANY],
-        out_specs=[VMEM] * 2,
-        input_output_aliases={0: 0},
-        compiler_params=params(8),
-        name="join",
-    )(cot_part, field_own, field_come, first_held)
-    arrived = lax.all_to_all(cot_part, ("dp", "half", "quad"), 0, 0, tiled=True)
+        compiler_params=params(8),
+        name="sum_halves",
+    )(field_own, field_come, cot_own, cot_come, first_held)
+    arrived = lax.all_to_all(summed, ("dp", "quad"), 0, 0, tiled=True)
 
     mode_rows = rows * owners
-    sent, pairs = pl.pallas_call(
+    sent, inputs, pairs = pl.pallas_call(
         modes_kernel,
         out_shape=[
-            pltpu.VMEM((owners, QUAD, 2, rows, C), half),
+            pltpu.VMEM((owners, QUAD, rows, C), half),
+            pltpu.VMEM((QUAD, mode_rows, C), half),
             pltpu.VMEM((QUAD, mode_rows, 2 * C), half),
         ],
-        in_specs=[VMEM] * 5,
-        out_specs=[VMEM] * 2,
+        in_specs=[VMEM] * 4,
+        out_specs=[VMEM] * 3,
         compiler_params=params(8),
         name="mode_grads",
-    )(arrived.reshape(owners, halves, QUAD, rows, C), field_sum, rounded, gather, scatter)
-
-    returned = lax.all_to_all(
-        sent.reshape(owners * QUAD, 2, rows, C), ("dp", "quad"), 0, 0, tiled=True
-    )
-    back, inputs = pl.pallas_call(
-        sort_kernel,
-        out_shape=[pltpu.VMEM(per_half, half), pltpu.VMEM((QUAD, mode_rows, C), half)],
-        in_specs=[VMEM] * 2,
-        out_specs=[VMEM] * 2,
-        compiler_params=params(8),
-        name="sort_modes",
-    )(returned.reshape(owners, QUAD, 2, rows, C), scatter)
+    )(arrived.reshape(owners, QUAD, 2, rows, C), rounded, gather, scatter)
+    back = lax.all_to_all(sent.reshape(per_half), ("dp", "quad"), 0, 0, tiled=True)
     back_come = swap_halves(back)
 
     count = 4
-    steps = QUAD * pencils // count
-
-    def adam(mode, after, *before):
+    total = modes * QUAD * pencils // count
+    first_steps = total * 12 // 16
+
+    def adam(begin, end, after, *before):
+        steps = end - begin
         return pl.pallas_call(
-            functools.partial(adam_kernel, mode),
+            functools.partial(adam_kernel, begin),
             out_shape=[pltpu.HBM(split, f32)] * 3 + [pltpu.VMEM((8, C), f32)],
             in_specs=[VMEM] * 5 + [ANY] + [HBM] * len(before),
             out_specs=[HBM] * 3 + [VMEM],
@@ -493,16 +461,16 @@
                 pltpu.SemaphoreType.DMA((steps, 3)),
             ],
             input_output_aliases={6 + k: k for k in range(len(before))},
-            compiler_params=params(16),
-            cost_estimate=cost(8 * weights.size),
+            compiler_params=params(22),
+            cost_estimate=cost(16 * weights.size * steps // total),
             name="adam",
         )(inputs, pairs, weights_held, first_held, second_held, after, *before)
 
-    *updated, token = adam(0, back)
+    *updated, token = adam(0, first_steps, back)
     blocks = pl.pallas_call(
         back_x_kernel,
         out_shape=[pltpu.VMEM((cells, owners, height, C), half)] * QUAD,
-        in_specs=[SMEM] + [VMEM] * 3 + [ANY],
+        in_specs=[VMEM] * 3 + [ANY],
         out_specs=[VMEM] * QUAD,
         scratch_shapes=[
             pltpu.VMEM((halves,) + per_half, half),
@@ -510,18 +478,18 @@
         ],
         compiler_params=params(8),
         name="back_x",
-    )(place, back, back_come, back_table_x, token)
-    *updated, token = adam(1, blocks[1], *updated)
+    )(back, back_come, back_table_x, token)
+    *updated, token = adam(first_steps, total, blocks[1], *updated)
     blocks = exchange(blocks)
     field_grad = pl.pallas_call(
         back_yz_kernel,
         out_shape=jax.ShapeDtypeStruct((cells, NY * NZ, C), half),
-        in_specs=[SMEM] + [VMEM] * (QUAD + 1) + [ANY],
+        in_specs=[VMEM] * (QUAD + 1) + [ANY],
         out_specs=VMEM,
         scratch_shapes=[pltpu.VMEM((QUAD, cells, owners, height, C), half)],
         compiler_params=params(8),
         name="back_yz",
-    )(place, *blocks, back_table_yz, token)
+    )(*blocks, back_table_yz, token)
     return (field_grad.reshape(field.shape), *[values.reshape(weights.shape) for values in updated])
 
 

time: 71.7 us -> 66.6 us (0.929)
  starting transfers between devices: 12.2 us -> 17.5 us
  blocking collectives: 24 us -> 18.8 us
  Pallas kernels: 29.4 us -> 25.2 us
  waiting for transfers between devices: 5 us -> 4.14 us
    all_to_all x2, blocking collectives: 24 us -> 18.8 us  [the longest x1 10.1 us: fast(): arrived = lax.all_to_all(summed, ('dp', 'quad'), 0, 0, tiled=True)]
    ppermute x6 -> x9, starting transfers between devices: 8.16 us -> 11.7 us  [exchange(): lax.ppermute(blocks[r], 'quad', [(q, q ^ r) for q in range(QUAD)])]
    pallas_call x10 -> x9, Pallas kernels: 26.9 us -> 23.8 us  [the longest x2 10.7 us: adam(): pl.pallas_call(functools.partial(adam_kernel, begin), out_shape=[pltpu.HB...]
    ppermute x2 -> x3, starting transfers between devices: 4.04 us -> 5.8 us  [swap_halves(): return lax.ppermute(values, 'half', [(0, 1), (1, 0)])]
    ppermute x2 -> x3, waiting for transfers between devices: 2.77 us -> 1.24 us  [swap_halves(): return lax.ppermute(values, 'half', [(0, 1), (1, 0)])]
    ppermute x6 -> x9, waiting for transfers between devices: 2.23 us -> 2.91 us  [exchange(): lax.ppermute(blocks[r], 'quad', [(q, q ^ r) for q in range(QUAD)])]
  transfers between devices with their start and end apart: 8 -> 12, of which waited for: 3 -> 3; matrix products, arithmetic and copies ran while one was open for 0% -> 0% of each run, Pallas kernels for 29% -> 30%
where the time goes in v3:
time: 66.6 us; the launch traced here: 66.4 us
  Pallas kernels  25.2 us (38%)
  blocking collectives  18.8 us (28%)
  starting transfers between devices  17.5 us (26%)
  waiting for transfers between devices  4.14 us (6%)
  between operations  0.77 us (1%)
    ppermute x9, starting transfers between devices, exchange(): lax.ppermute(blocks[r], 'quad', [(q, q ^ r) for q in range(QUAD)])  11.7 us
    pallas_call x2, Pallas kernels, adam(): pl.pallas_call(functools.partial(adam_kernel, begin), out_shape=[pltpu.HB...  10.7 us
    all_to_all x1, blocking collectives, fast(): arrived = lax.all_to_all(summed, ('dp', 'quad'), 0, 0, tiled=True)  10.1 us
    all_to_all x1, blocking collectives, fast(): lax.all_to_all(sent.reshape(per_half), ('dp', 'quad'), 0, 0, tiled=True)  8.65 us
    pallas_call x1, Pallas kernels, fast(): pl.pallas_call(stage_kernel, out_shape=[vmem(big)] + [vmem(t) for t in st...  8.6 us
    ppermute x3, starting transfers between devices, swap_halves(): return lax.ppermute(values, 'half', [(0, 1), (1, 0)])  5.8 us
    ppermute x9, waiting for transfers between devices, exchange(): lax.ppermute(blocks[r], 'quad', [(q, q ^ r) for q in range(QUAD)])  2.91 us
    pallas_call x1, Pallas kernels, fast(): pl.pallas_call(modes_kernel, out_shape=[pltpu.VMEM((owners, QUAD, rows, C...  1.98 us
  transfers between devices with their start and end apart: 12, of which 3 were waited for; matrix products, arithmetic and copies ran while one was open for 0% of the time, Pallas kernels for 30%

profile of v3, /device:TPU:0, one launch (start us, length us, event | category | flops | bytes accessed | tf_op | source)
XLA Modules:
  0.0 66.4 jit_solution(220287244072663575)
XLA Ops:
  0.6 1.6 %yz_modes_field.1 = (bf16[4,64,128]{2,1,0:T(8,128)(2,1)S(1)}, bf16[4,64,128]{2,1,0:T(8,128)(2,1)S(1)}, bf16[4,64,128]{2,1,0:T(8,128)(2,1)S(1)}, bf16[4,64,128]{2...) custom-call(bf16[4,512,128]{2,1,0:T(8,128)(2,1)} %bitcast.7, ...), custom_call_target="tpu_custom_call" | custom-call | tf_op jit(solution)/shard_map/yz_modes_field/pallas_call | solution.py:364
  2.2 3.0 %collective-permute-start = (bf16[4,64,128]{2,1,0:T(8,128)(2,1)S(1)}, bf16[4,64,128]{2,1,0:T(8,128)(2,1)S(1)}, u32[]{:S(2)}, u32[]{:S(2)}) collective-permute-start(bf16[4,64,128]{2,1,0:T(8,128)(2,1)S(1)} %get-tuple-element.43), channel_id=1, source_target_pairs={{0,1},{1,0},{2,3},{3,2},{4,5},{5,4},{6,7},{7,6},{8,9},{9,8},{10,11... | collective-permute-start | bytes 196616 | tf_op jit(solution)/shard_map/ppermute | solution.py:338
  5.2 1.6 %collective-permute-start.1 = (bf16[4,64,128]{2,1,0:T(8,128)(2,1)S(1)}, bf16[4,64,128]{2,1,0:T(8,128)(2,1)S(1)}, u32[]{:S(2)}, u32[]{:S(2)}) collective-permute-start(bf16[4,64,128]{2,1,0:T(8,128)(2,1)S(1)} %get-tuple-element.44), channel_id=1, source_target_pairs={{0,2},{1,3},{2,0},{3,1},{4,6},{5,7},{6,4},{7,5},{8,10},{9,11},{10,... | collective-permute-start | bytes 196616 | tf_op jit(solution)/shard_map/ppermute | solution.py:338
  6.8 0.0 collective-permute-start.2
  6.8 0.3 yz_modes_cot.1
  7.1 2.0 %collective-permute-start.4 = (bf16[4,64,128]{2,1,0:T(8,128)(2,1)S(1)}, bf16[4,64,128]{2,1,0:T(8,128)(2,1)S(1)}, u32[]{:S(2)}, u32[]{:S(2)}) collective-permute-start(bf16[4,64,128]{2,1,0:T(8,128)(2,1)S(1)} %get-tuple-element.52), channel_id=1, source_target_pairs={{0,1},{1,0},{2,3},{3,2},{4,5},{5,4},{6,7},{7,6},{8,9},{9,8},{10,11... | collective-permute-start | bytes 196616 | tf_op jit(solution)/shard_map/ppermute | solution.py:338
  9.1 1.6 %collective-permute-start.5 = (bf16[4,64,128]{2,1,0:T(8,128)(2,1)S(1)}, bf16[4,64,128]{2,1,0:T(8,128)(2,1)S(1)}, u32[]{:S(2)}, u32[]{:S(2)}) collective-permute-start(bf16[4,64,128]{2,1,0:T(8,128)(2,1)S(1)} %get-tuple-element.53), channel_id=1, source_target_pairs={{0,2},{1,3},{2,0},{3,1},{4,6},{5,7},{6,4},{7,5},{8,10},{9,11},{10,... | collective-permute-start | bytes 196616 | tf_op jit(solution)/shard_map/ppermute | solution.py:338
  10.7 0.0 collective-permute-done.refs_1_
  10.7 0.0 collective-permute-start.6
  10.7 0.0 collective-permute-done.1.refs_2_
  10.7 1.4 %collective-permute-done.2.refs_3_ = bf16[4,64,128]{2,1,0:T(8,128)(2,1)S(1)} collective-permute-done((bf16[4,64,128]{2,1,0:T(8,128)(2,1)S(1)}, bf16[4,64,128]{2,1,0:T(8,128)(2,1)S(1)}, u32[]{:S(2)}, u32[]{:S(2)}) %collective-permute-start.2) | collective-permute-done | bytes 65568 | tf_op jit(solution)/shard_map/ppermute | solution.py:338
  12.1 0.3 x_modes.2
  12.4 2.7 %collective-permute-start.3 = (bf16[16,32,128]{2,1,0:T(8,128)(2,1)S(1)}, bf16[16,32,128]{2,1,0:T(8,128)(2,1)S(1)}, u32[]{:S(2)}, u32[]{:S(2)}) collective-permute-start(bf16[16,32,128]{2,1,0:T(8,128)(2,1)S(1)} %get-tuple-element.48.refs_5_), channel_id=1, source_target_pairs={{0,4},{4,0},{1,5},{5,1},{2,6},{6,2},{3,7},{7,3},{8,12},{12,8},{9,1... | collective-permute-start | bytes 393224 | tf_op jit(solution)/shard_map/ppermute | solution.py:343
  15.0 0.0 collective-permute-done.4.refs_1_
  15.0 0.0 collective-permute-done.5.refs_2_
  15.0 1.5 %collective-permute-done.6.refs_3_ = bf16[4,64,128]{2,1,0:T(8,128)(2,1)S(1)} collective-permute-done((bf16[4,64,128]{2,1,0:T(8,128)(2,1)S(1)}, bf16[4,64,128]{2,1,0:T(8,128)(2,1)S(1)}, u32[]{:S(2)}, u32[]{:S(2)}) %collective-permute-start.6) | collective-permute-done | bytes 65568 | tf_op jit(solution)/shard_map/ppermute | solution.py:338
  16.5 0.3 x_modes.3
  16.8 2.6 %collective-permute-start.7 = (bf16[16,32,128]{2,1,0:T(8,128)(2,1)S(1)}, bf16[16,32,128]{2,1,0:T(8,128)(2,1)S(1)}, u32[]{:S(2)}, u32[]{:S(2)}) collective-permute-start(bf16[16,32,128]{2,1,0:T(8,128)(2,1)S(1)} %get-tuple-element.56.after), channel_id=1, source_target_pairs={{0,4},{4,0},{1,5},{5,1},{2,6},{6,2},{3,7},{7,3},{8,12},{12,8},{9,1... | collective-permute-start | bytes 393224 | tf_op jit(solution)/shard_map/ppermute | solution.py:343
  19.5 8.6 %stage.1 = (f32[2,32,2,128,128]{4,3,2,1,0:T(8,128)S(1)}, bf16[2,128,128]{2,1,0:T(8,128)(2,1)S(1)}, bf16[128,128]{1,0:T(8,128)(2,1)S(1)}, bf16[2,256,256]{2,1,0:T...) custom-call(bf16[16,32,128]{2,1,0:T(8,128)(2,1)S(1)} %get-tuple-elem, ...), custom_call_target="tpu_custom_call" | custom-call | tf_op jit(solution)/shard_map/stage/pallas_call | solution.py:412
  28.1 0.0 collective-permute-done.3.field_come
  28.1 0.0 collective-permute-done.7.cot_come
  28.1 0.1 sum_halves.1
  28.2 10.1 %all_to_all.10 = bf16[16,2,32,128]{3,2,1,0:T(8,128)(2,1)S(1)} all-to-all(bf16[16,2,32,128]{3,2,1,0:T(8,128)(2,1)S(1)} %sum_halves.1), channel_id=1, replica_groups=mesh['dp'=4,'half'=2,'quad'=4] {'dp','quad'}, dimensions={0} | all-to-all | bytes 524288 | tf_op jit(solution)/shard_map/all_to_all | solution.py:430
  38.3 2.0 %mode_grads.1 = (bf16[4,4,32,128]{3,2,1,0:T(8,128)(2,1)S(1)}, bf16[4,128,128]{2,1,0:T(8,128)(2,1)S(1)}, bf16[4,128,256]{2,1,0:T(8,128)(2,1)S(1)}) custom-call(bf16[4,4,2,32,128]{4,3,2,1,0:T(8,128)(2,1)S(1)} %bitcast.5, bf16[2,32,128,256]{3,2,1,0:T(8,128)(2,1)S(1)} %get-tuple-element.58.weights, bf16[2,128,128]{2,1,0:T(8,128)(2,1)S(1)} %get-tuple-element.59.gather, ...), custom_call_target="tpu_custom_call" | custom-call | tf_op jit(solution)/shard_map/mode_grads/pallas_call | solution.py:433
  40.3 8.6 %all_to_all.11.refs_0_.own = bf16[16,32,128]{2,1,0:T(8,128)(2,1)S(1)} all-to-all(bf16[16,32,128]{2,1,0:T(8,128)(2,1)S(1)} %bitcast.6), channel_id=1, replica_groups=mesh['dp'=4,'half'=2,'quad'=4] {'dp','quad'}, dimensions={0} | all-to-all | bytes 262144 | tf_op jit(solution)/shard_map/all_to_all | solution.py:445
  48.9 0.5 collective-permute-start.8
  49.4 7.5 %adam.2 = (f32[2,32,2,128,128]{4,3,2,1,0:T(8,128)}, f32[2,32,2,128,128]{4,3,2,1,0:T(8,128)}, f32[2,32,2,128,128]{4,3,2,1,0:T(8,128)}, f32[8,128]{1,0:T(8,128)S(1)}) custom-call(bf16[4,128,128]{2,1,0:T(8,128)(2,1)S(1)} %get-tuple-element.63.inputs, bf16[4,128,256]{2,1,0:T(8,128)(2,1)S(1)} %get-tuple-element.64.pairs, ...), custom_call_target="tpu_custom_call" | custom-call | bytes 25165824 | tf_op jit(solution)/shard_map/adam/pallas_call | solution.py:454
  56.9 1.2 %collective-permute-done.8.come = bf16[16,32,128]{2,1,0:T(8,128)(2,1)S(1)} collective-permute-done((bf16[16,32,128]{2,1,0:T(8,128)(2,1)S(1)}, bf16[16,32,128]{2,1,0:T(8,128)(2,1)S(1)}, u32[]{:S(2)}, u32[]{:S(2)}) %collective-permute-start.8) | collective-permute-done | bytes 131104 | tf_op jit(solution)/shard_map/ppermute | solution.py:343
  58.1 0.3 back_x.1
  58.4 0.1 collective-permute-start.10
  58.5 2.0 %collective-permute-start.11 = (bf16[4,4,16,128]{3,2,1,0:T(8,128)(2,1)S(1)}, bf16[4,4,16,128]{3,2,1,0:T(8,128)(2,1)S(1)}, u32[]{:S(2)}, u32[]{:S(2)}) collective-permute-start(bf16[4,4,16,128]{3,2,1,0:T(8,128)(2,1)S(1)} %get-tuple-element.71), channel_id=1, source_target_pairs={{0,3},{1,2},{2,1},{3,0},{4,7},{5,6},{6,5},{7,4},{8,11},{9,10},{10,... | collective-permute-start | bytes 196616 | tf_op jit(solution)/shard_map/ppermute | solution.py:338
  60.5 1.5 %collective-permute-start.9 = (bf16[4,4,16,128]{3,2,1,0:T(8,128)(2,1)S(1)}, bf16[4,4,16,128]{3,2,1,0:T(8,128)(2,1)S(1)}, u32[]{:S(2)}, u32[]{:S(2)}) collective-permute-start(bf16[4,4,16,128]{3,2,1,0:T(8,128)(2,1)S(1)} %get-tuple-element.69.refs_0_), channel_id=1, source_target_pairs={{0,1},{1,0},{2,3},{3,2},{4,5},{5,4},{6,7},{7,6},{8,9},{9,8},{10,11... | collective-permute-start | bytes 196616 | tf_op jit(solution)/shard_map/ppermute | solution.py:338
  62.0 3.2 %adam.3 = (f32[2,32,2,128,128]{4,3,2,1,0:T(8,128)}, f32[2,32,2,128,128]{4,3,2,1,0:T(8,128)}, f32[2,32,2,128,128]{4,3,2,1,0:T(8,128)}, f32[8,128]{1,0:T(8,128)S(1)}) custom-call(bf16[4,128,128]{2,1,0:T(8,128)(2,1)S(1)} %get-tuple-element.63.inputs, ...), custom_call_target="tpu_custom_call", output_to_operand_aliasing={{0}: (6, {}), {1}: (7, {}), {2}: (8, {})} | custom-call | bytes 8388608 | tf_op jit(solution)/shard_map/adam/pallas_call | solution.py:454
  65.2 0.0 collective-permute-done.10.refs_2_
  65.2 0.0 collective-permute-done.11.refs_3_
  65.2 0.0 collective-permute-done.9.refs_1_
  65.2 1.1 %back_yz.1 = bf16[4,512,128]{2,1,0:T(8,128)(2,1)} custom-call(bf16[4,4,16,128]{3,2,1,0:T(8,128)(2,1)S(1)} %get-tuple-element.68.refs_0_, bf16[4,4,16,128]{3,2,1,0:T(8,128)(2,1)S(1)} %collective-permute-done.9.refs_1_, bf16[4,4,16,128]{3,2,1,0:T(8,128)(2,1)S(1)} %collective-permute-done.10.refs_2_, ...), custom_call_target="tpu_custom_call" | custom-call | tf_op jit(solution)/shard_map/back_yz/pallas_call | solution.py:484
Async XLA Ops:
  2.2 8.5 %collective-permute-start = (bf16[4,64,128]{2,1,0:T(8,128)(2,1)S(1)}, bf16[4,64,128]{2,1,0:T(8,128)(2,1)S(1)}, u32[]{:S(2)}, u32[]{:S(2)}) collective-permute-start(bf16[4,64,128]{2,1,0:T(8,128)(2,1)S(1)} %get-tuple-element.43), channel_id=1, source_target_pairs={{0,1},{1,0},{2,3},{3,2},{4,5},{5,4},{6,7},{7,6},{8,9},{9,8},{10,11... | collective-permute-start | bytes 196616 | tf_op jit(solution)/shard_map/ppermute | solution.py:338
  5.2 5.5 %collective-permute-start.1 = (bf16[4,64,128]{2,1,0:T(8,128)(2,1)S(1)}, bf16[4,64,128]{2,1,0:T(8,128)(2,1)S(1)}, u32[]{:S(2)}, u32[]{:S(2)}) collective-permute-start(bf16[4,64,128]{2,1,0:T(8,128)(2,1)S(1)} %get-tuple-element.44), channel_id=1, source_target_pairs={{0,2},{1,3},{2,0},{3,1},{4,6},{5,7},{6,4},{7,5},{8,10},{9,11},{10,... | collective-permute-start | bytes 196616 | tf_op jit(solution)/shard_map/ppermute | solution.py:338
  6.8 5.3 %collective-permute-start.2 = (bf16[4,64,128]{2,1,0:T(8,128)(2,1)S(1)}, bf16[4,64,128]{2,1,0:T(8,128)(2,1)S(1)}, u32[]{:S(2)}, u32[]{:S(2)}) collective-permute-start(bf16[4,64,128]{2,1,0:T(8,128)(2,1)S(1)} %get-tuple-element.45), channel_id=1, source_target_pairs={{0,3},{1,2},{2,1},{3,0},{4,7},{5,6},{6,5},{7,4},{8,11},{9,10},{10,... | collective-permute-start | bytes 196616 | tf_op jit(solution)/shard_map/ppermute | solution.py:338
  7.1 7.9 %collective-permute-start.4 = (bf16[4,64,128]{2,1,0:T(8,128)(2,1)S(1)}, bf16[4,64,128]{2,1,0:T(8,128)(2,1)S(1)}, u32[]{:S(2)}, u32[]{:S(2)}) collective-permute-start(bf16[4,64,128]{2,1,0:T(8,128)(2,1)S(1)} %get-tuple-element.52), channel_id=1, source_target_pairs={{0,1},{1,0},{2,3},{3,2},{4,5},{5,4},{6,7},{7,6},{8,9},{9,8},{10,11... | collective-permute-start | bytes 196616 | tf_op jit(solution)/shard_map/ppermute | solution.py:338
  9.1 5.9 %collective-permute-start.5 = (bf16[4,64,128]{2,1,0:T(8,128)(2,1)S(1)}, bf16[4,64,128]{2,1,0:T(8,128)(2,1)S(1)}, u32[]{:S(2)}, u32[]{:S(2)}) collective-permute-start(bf16[4,64,128]{2,1,0:T(8,128)(2,1)S(1)} %get-tuple-element.53), channel_id=1, source_target_pairs={{0,2},{1,3},{2,0},{3,1},{4,6},{5,7},{6,4},{7,5},{8,10},{9,11},{10,... | collective-permute-start | bytes 196616 | tf_op jit(solution)/shard_map/ppermute | solution.py:338
  10.7 5.9 %collective-permute-start.6 = (bf16[4,64,128]{2,1,0:T(8,128)(2,1)S(1)}, bf16[4,64,128]{2,1,0:T(8,128)(2,1)S(1)}, u32[]{:S(2)}, u32[]{:S(2)}) collective-permute-start(bf16[4,64,128]{2,1,0:T(8,128)(2,1)S(1)} %get-tuple-element.54), channel_id=1, source_target_pairs={{0,3},{1,2},{2,1},{3,0},{4,7},{5,6},{6,5},{7,4},{8,11},{9,10},{10,... | collective-permute-start | bytes 196616 | tf_op jit(solution)/shard_map/ppermute | solution.py:338
  12.4 15.7 %collective-permute-start.3 = (bf16[16,32,128]{2,1,0:T(8,128)(2,1)S(1)}, bf16[16,32,128]{2,1,0:T(8,128)(2,1)S(1)}, u32[]{:S(2)}, u32[]{:S(2)}) collective-permute-start(bf16[16,32,128]{2,1,0:T(8,128)(2,1)S(1)} %get-tuple-element.48.refs_5_), channel_id=1, source_target_pairs={{0,4},{4,0},{1,5},{5,1},{2,6},{6,2},{3,7},{7,3},{8,12},{12,8},{9,1... | collective-permute-start | bytes 393224 | tf_op jit(solution)/shard_map/ppermute | solution.py:343
  16.8 11.2 %collective-permute-start.7 = (bf16[16,32,128]{2,1,0:T(8,128)(2,1)S(1)}, bf16[16,32,128]{2,1,0:T(8,128)(2,1)S(1)}, u32[]{:S(2)}, u32[]{:S(2)}) collective-permute-start(bf16[16,32,128]{2,1,0:T(8,128)(2,1)S(1)} %get-tuple-element.56.after), channel_id=1, source_target_pairs={{0,4},{4,0},{1,5},{5,1},{2,6},{6,2},{3,7},{7,3},{8,12},{12,8},{9,1... | collective-permute-start | bytes 393224 | tf_op jit(solution)/shard_map/ppermute | solution.py:343
  48.9 9.2 %collective-permute-start.8 = (bf16[16,32,128]{2,1,0:T(8,128)(2,1)S(1)}, bf16[16,32,128]{2,1,0:T(8,128)(2,1)S(1)}, u32[]{:S(2)}, u32[]{:S(2)}) collective-permute-start(bf16[16,32,128]{2,1,0:T(8,128)(2,1)S(1)} %all_to_all.11.refs_0_.own), channel_id=1, source_target_pairs={{0,4},{4,0},{1,5},{5,1},{2,6},{6,2},{3,7},{7,3},{8,12},{12,8},{9,1... | collective-permute-start | bytes 393224 | tf_op jit(solution)/shard_map/ppermute | solution.py:343
  58.4 6.8 %collective-permute-start.10 = (bf16[4,4,16,128]{3,2,1,0:T(8,128)(2,1)S(1)}, bf16[4,4,16,128]{3,2,1,0:T(8,128)(2,1)S(1)}, u32[]{:S(2)}, u32[]{:S(2)}) collective-permute-start(bf16[4,4,16,128]{3,2,1,0:T(8,128)(2,1)S(1)} %get-tuple-element.70), channel_id=1, source_target_pairs={{0,2},{1,3},{2,0},{3,1},{4,6},{5,7},{6,4},{7,5},{8,10},{9,11},{10,... | collective-permute-start | bytes 196616 | tf_op jit(solution)/shard_map/ppermute | solution.py:338
  58.5 6.7 %collective-permute-start.11 = (bf16[4,4,16,128]{3,2,1,0:T(8,128)(2,1)S(1)}, bf16[4,4,16,128]{3,2,1,0:T(8,128)(2,1)S(1)}, u32[]{:S(2)}, u32[]{:S(2)}) collective-permute-start(bf16[4,4,16,128]{3,2,1,0:T(8,128)(2,1)S(1)} %get-tuple-element.71), channel_id=1, source_target_pairs={{0,3},{1,2},{2,1},{3,0},{4,7},{5,6},{6,5},{7,4},{8,11},{9,10},{10,... | collective-permute-start | bytes 196616 | tf_op jit(solution)/shard_map/ppermute | solution.py:338
  60.5 4.7 %collective-permute-start.9 = (bf16[4,4,16,128]{3,2,1,0:T(8,128)(2,1)S(1)}, bf16[4,4,16,128]{3,2,1,0:T(8,128)(2,1)S(1)}, u32[]{:S(2)}, u32[]{:S(2)}) collective-permute-start(bf16[4,4,16,128]{3,2,1,0:T(8,128)(2,1)S(1)} %get-tuple-element.69.refs_0_), channel_id=1, source_target_pairs={{0,1},{1,0},{2,3},{3,2},{4,5},{5,4},{6,7},{7,6},{8,9},{9,8},{10,11... | collective-permute-start | bytes 196616 | tf_op jit(solution)/shard_map/ppermute | solution.py:338

commit v4 on v3

--- a/solution.py
+++ b/solution.py
@@ -408,8 +408,8 @@
     field_come = swap_halves(field_other)
     cot_own, cot_other = x_modes(cot_blocks, field_other)
     cot_come = swap_halves(cot_other)
-    staged = [jnp.asarray(t) for t in (gather, scatter, back_table_x, back_table_yz)] + [first, second]
-    weights_held, gather, scatter, back_table_x, back_table_yz, first_held, second_held, rounded = pl.pallas_call(
+    staged = [jnp.asarray(t) for t in (gather, scatter, back_table_x, back_table_yz)]
+    weights_held, gather, scatter, back_table_x, back_table_yz, rounded = pl.pallas_call(
         stage_kernel,
         out_shape=[vmem(big)] + [vmem(t) for t in staged] + [pltpu.VMEM((modes, QUAD * pencils, C, 2 * C), half)],
         in_specs=[ANY] + [HBM] * (1 + len(staged)),
@@ -426,7 +426,7 @@
         out_specs=VMEM,
         compiler_params=params(8),
         name="sum_halves",
-    )(field_own, field_come, cot_own, cot_come, first_held)
+    )(field_own, field_come, cot_own, cot_come, rounded)
     arrived = lax.all_to_all(summed, ("dp", "quad"), 0, 0, tiled=True)
 
     mode_rows = rows * owners
@@ -464,7 +464,7 @@
             compiler_params=params(22),
             cost_estimate=cost(16 * weights.size * steps // total),
             name="adam",
-        )(inputs, pairs, weights_held, first_held, second_held, after, *before)
+        )(inputs, pairs, weights_held, first, second, after, *before)
 
     *updated, token = adam(0, first_steps, back)
     blocks = pl.pallas_call(

time: 66.6 us -> 65.7 us (0.986)
  Pallas kernels: 25.2 us -> 21.1 us
  starting transfers between devices: 17.5 us -> 20 us
    pallas_call x1, Pallas kernels: 8.6 us -> 4.5 us  [fast(): pl.pallas_call(stage_kernel, out_shape=[vmem(big)] + [vmem(t) for t in st...]
    ppermute x3, starting transfers between devices: 5.8 us -> 8.33 us  [swap_halves(): return lax.ppermute(values, 'half', [(0, 1), (1, 0)])]
  transfers between devices with their start and end apart: 12 -> 12, of which waited for: 3 -> 3; matrix products, arithmetic and copies ran while one was open for 0% -> 0% of each run, Pallas kernels for 30% -> 25%
where the time goes in v4:
time: 65.7 us; the launch traced here: 65.5 us
  Pallas kernels  21.1 us (32%)
  starting transfers between devices  20 us (30%)
  blocking collectives  19.3 us (29%)
  waiting for transfers between devices  4.24 us (6%)
  between operations  0.77 us (1%)
    ppermute x9, starting transfers between devices, exchange(): lax.ppermute(blocks[r], 'quad', [(q, q ^ r) for q in range(QUAD)])  11.7 us
    pallas_call x2, Pallas kernels, adam(): pl.pallas_call(functools.partial(adam_kernel, begin), out_shape=[pltpu.HB...  10.7 us
    all_to_all x1, blocking collectives, fast(): arrived = lax.all_to_all(summed, ('dp', 'quad'), 0, 0, tiled=True)  10.6 us
    all_to_all x1, blocking collectives, fast(): lax.all_to_all(sent.reshape(per_half), ('dp', 'quad'), 0, 0, tiled=True)  8.65 us
    ppermute x3, starting transfers between devices, swap_halves(): return lax.ppermute(values, 'half', [(0, 1), (1, 0)])  8.33 us
    pallas_call x1, Pallas kernels, fast(): pl.pallas_call(stage_kernel, out_shape=[vmem(big)] + [vmem(t) for t in st...  4.5 us
    ppermute x9, waiting for transfers between devices, exchange(): lax.ppermute(blocks[r], 'quad', [(q, q ^ r) for q in range(QUAD)])  2.91 us
    pallas_call x1, Pallas kernels, fast(): pl.pallas_call(modes_kernel, out_shape=[pltpu.VMEM((owners, QUAD, rows, C...  1.98 us
  transfers between devices with their start and end apart: 12, of which 3 were waited for; matrix products, arithmetic and copies ran while one was open for 0% of the time, Pallas kernels for 25%

profile of v4, /device:TPU:0, one launch (start us, length us, event | category | flops | bytes accessed | tf_op | source)
XLA Modules:
  0.0 65.5 jit_solution(5669839948732598355)
XLA Ops:
  0.6 1.6 %yz_modes_field.1 = (bf16[4,64,128]{2,1,0:T(8,128)(2,1)S(1)}, bf16[4,64,128]{2,1,0:T(8,128)(2,1)S(1)}, bf16[4,64,128]{2,1,0:T(8,128)(2,1)S(1)}, bf16[4,64,128]{2...) custom-call(bf16[4,512,128]{2,1,0:T(8,128)(2,1)} %bitcast.9, ...), custom_call_target="tpu_custom_call" | custom-call | tf_op jit(solution)/shard_map/yz_modes_field/pallas_call | solution.py:364
  2.2 3.0 %collective-permute-start = (bf16[4,64,128]{2,1,0:T(8,128)(2,1)S(1)}, bf16[4,64,128]{2,1,0:T(8,128)(2,1)S(1)}, u32[]{:S(2)}, u32[]{:S(2)}) collective-permute-start(bf16[4,64,128]{2,1,0:T(8,128)(2,1)S(1)} %get-tuple-element.41), channel_id=1, source_target_pairs={{0,1},{1,0},{2,3},{3,2},{4,5},{5,4},{6,7},{7,6},{8,9},{9,8},{10,11... | collective-permute-start | bytes 196616 | tf_op jit(solution)/shard_map/ppermute | solution.py:338
  5.2 1.6 %collective-permute-start.1 = (bf16[4,64,128]{2,1,0:T(8,128)(2,1)S(1)}, bf16[4,64,128]{2,1,0:T(8,128)(2,1)S(1)}, u32[]{:S(2)}, u32[]{:S(2)}) collective-permute-start(bf16[4,64,128]{2,1,0:T(8,128)(2,1)S(1)} %get-tuple-element.42), channel_id=1, source_target_pairs={{0,2},{1,3},{2,0},{3,1},{4,6},{5,7},{6,4},{7,5},{8,10},{9,11},{10,... | collective-permute-start | bytes 196616 | tf_op jit(solution)/shard_map/ppermute | solution.py:338
  6.8 0.0 collective-permute-start.2
  6.8 0.3 yz_modes_cot.1
  7.1 2.0 %collective-permute-start.4 = (bf16[4,64,128]{2,1,0:T(8,128)(2,1)S(1)}, bf16[4,64,128]{2,1,0:T(8,128)(2,1)S(1)}, u32[]{:S(2)}, u32[]{:S(2)}) collective-permute-start(bf16[4,64,128]{2,1,0:T(8,128)(2,1)S(1)} %get-tuple-element.50), channel_id=1, source_target_pairs={{0,1},{1,0},{2,3},{3,2},{4,5},{5,4},{6,7},{7,6},{8,9},{9,8},{10,11... | collective-permute-start | bytes 196616 | tf_op jit(solution)/shard_map/ppermute | solution.py:338
  9.1 1.6 %collective-permute-start.5 = (bf16[4,64,128]{2,1,0:T(8,128)(2,1)S(1)}, bf16[4,64,128]{2,1,0:T(8,128)(2,1)S(1)}, u32[]{:S(2)}, u32[]{:S(2)}) collective-permute-start(bf16[4,64,128]{2,1,0:T(8,128)(2,1)S(1)} %get-tuple-element.51), channel_id=1, source_target_pairs={{0,2},{1,3},{2,0},{3,1},{4,6},{5,7},{6,4},{7,5},{8,10},{9,11},{10,... | collective-permute-start | bytes 196616 | tf_op jit(solution)/shard_map/ppermute | solution.py:338
  10.7 0.0 collective-permute-done.refs_1_
  10.7 0.0 collective-permute-start.6
  10.7 0.0 collective-permute-done.1.refs_2_
  10.7 1.4 %collective-permute-done.2.refs_3_ = bf16[4,64,128]{2,1,0:T(8,128)(2,1)S(1)} collective-permute-done((bf16[4,64,128]{2,1,0:T(8,128)(2,1)S(1)}, bf16[4,64,128]{2,1,0:T(8,128)(2,1)S(1)}, u32[]{:S(2)}, u32[]{:S(2)}) %collective-permute-start.2) | collective-permute-done | bytes 65568 | tf_op jit(solution)/shard_map/ppermute | solution.py:338
  12.1 0.3 x_modes.2
  12.4 2.7 %collective-permute-start.3 = (bf16[16,32,128]{2,1,0:T(8,128)(2,1)S(1)}, bf16[16,32,128]{2,1,0:T(8,128)(2,1)S(1)}, u32[]{:S(2)}, u32[]{:S(2)}) collective-permute-start(bf16[16,32,128]{2,1,0:T(8,128)(2,1)S(1)} %get-tuple-element.46.refs_5_), channel_id=1, source_target_pairs={{0,4},{4,0},{1,5},{5,1},{2,6},{6,2},{3,7},{7,3},{8,12},{12,8},{9,1... | collective-permute-start | bytes 393224 | tf_op jit(solution)/shard_map/ppermute | solution.py:343
  15.0 0.0 collective-permute-done.4.refs_1_
  15.0 0.0 collective-permute-done.5.refs_2_
  15.0 1.5 %collective-permute-done.6.refs_3_ = bf16[4,64,128]{2,1,0:T(8,128)(2,1)S(1)} collective-permute-done((bf16[4,64,128]{2,1,0:T(8,128)(2,1)S(1)}, bf16[4,64,128]{2,1,0:T(8,128)(2,1)S(1)}, u32[]{:S(2)}, u32[]{:S(2)}) %collective-permute-start.6) | collective-permute-done | bytes 65568 | tf_op jit(solution)/shard_map/ppermute | solution.py:338
  16.5 0.3 x_modes.3
  16.8 0.0 slice-start
  16.8 0.0 copy-start
  16.9 2.6 %collective-permute-start.7 = (bf16[16,32,128]{2,1,0:T(8,128)(2,1)S(1)}, bf16[16,32,128]{2,1,0:T(8,128)(2,1)S(1)}, u32[]{:S(2)}, u32[]{:S(2)}) collective-permute-start(bf16[16,32,128]{2,1,0:T(8,128)(2,1)S(1)} %get-tuple-element.54.after), channel_id=1, source_target_pairs={{0,4},{4,0},{1,5},{5,1},{2,6},{6,2},{3,7},{7,3},{8,12},{12,8},{9,1... | collective-permute-start | bytes 393224 | tf_op jit(solution)/shard_map/ppermute | solution.py:343
  19.5 4.5 %stage.1 = (f32[2,32,2,128,128]{4,3,2,1,0:T(8,128)S(1)}, bf16[2,128,128]{2,1,0:T(8,128)(2,1)S(1)}, bf16[128,128]{1,0:T(8,128)(2,1)S(1)}, bf16[2,256,256]{2,1,0:T...) custom-call(bf16[16,32,128]{2,1,0:T(8,128)(2,1)S(1)} %get-tuple-element.54.after, ...), custom_call_target="tpu_custom_call" | custom-call | tf_op jit(solution)/shard_map/stage/pallas_call | solution.py:412
  24.0 0.0 collective-permute-done.3.field_come
  24.0 1.3 %collective-permute-done.7.cot_come = bf16[16,32,128]{2,1,0:T(8,128)(2,1)S(1)} collective-permute-done((bf16[16,32,128]{2,1,0:T(8,128)(2,1)S(1)}, bf16[16,32,128]{2,1,0:T(8,128)(2,1)S(1)}, u32[]{:S(2)}, u32[]{:S(2)}) %collective-permute-start.7) | collective-permute-done | bytes 131104 | tf_op jit(solution)/shard_map/ppermute | solution.py:343
  25.3 0.0 slice-start.1
  25.3 0.1 sum_halves.1
  25.4 10.6 %all_to_all.10 = bf16[16,2,32,128]{3,2,1,0:T(8,128)(2,1)S(1)} all-to-all(bf16[16,2,32,128]{3,2,1,0:T(8,128)(2,1)S(1)} %sum_halves.1), channel_id=1, replica_groups=mesh['dp'=4,'half'=2,'quad'=4] {'dp','quad'}, dimensions={0} | all-to-all | bytes 524288 | tf_op jit(solution)/shard_map/all_to_all | solution.py:430
  36.0 2.0 %mode_grads.1 = (bf16[4,4,32,128]{3,2,1,0:T(8,128)(2,1)S(1)}, bf16[4,128,128]{2,1,0:T(8,128)(2,1)S(1)}, bf16[4,128,256]{2,1,0:T(8,128)(2,1)S(1)}) custom-call(bf16[4,4,2,32,128]{4,3,2,1,0:T(8,128)(2,1)S(1)} %bitcast.7, bf16[2,32,128,256]{3,2,1,0:T(8,128)(2,1)S(1)} %get-tuple-element.55.refs_0_.weights, bf16[2,128,128]{2,1,0:T(8,128)(2,1)S(1)} %get-tuple-element.56.gather, ...), custom_call_target="tpu_custom_call" | custom-call | tf_op jit(solution)/shard_map/mode_grads/pallas_call | solution.py:433
  38.0 8.6 %all_to_all.11.refs_0_.own = bf16[16,32,128]{2,1,0:T(8,128)(2,1)S(1)} all-to-all(bf16[16,32,128]{2,1,0:T(8,128)(2,1)S(1)} %bitcast.8), channel_id=1, replica_groups=mesh['dp'=4,'half'=2,'quad'=4] {'dp','quad'}, dimensions={0} | all-to-all | bytes 262144 | tf_op jit(solution)/shard_map/all_to_all | solution.py:445
  46.7 3.0 %collective-permute-start.8 = (bf16[16,32,128]{2,1,0:T(8,128)(2,1)S(1)}, bf16[16,32,128]{2,1,0:T(8,128)(2,1)S(1)}, u32[]{:S(2)}, u32[]{:S(2)}) collective-permute-start(bf16[16,32,128]{2,1,0:T(8,128)(2,1)S(1)} %all_to_all.11.refs_0_.own), channel_id=1, source_target_pairs={{0,4},{4,0},{1,5},{5,1},{2,6},{6,2},{3,7},{7,3},{8,12},{12,8},{9,1... | collective-permute-start | bytes 393224 | tf_op jit(solution)/shard_map/ppermute | solution.py:343
  49.7 0.0 slice-done
  49.7 0.0 copy-done
  49.7 0.0 slice-done.1
  49.7 7.5 %adam.2 = (f32[2,32,2,128,128]{4,3,2,1,0:T(8,128)}, f32[2,32,2,128,128]{4,3,2,1,0:T(8,128)}, f32[2,32,2,128,128]{4,3,2,1,0:T(8,128)}, f32[8,128]{1,0:T(8,128)S(1)}) custom-call(bf16[4,128,128]{2,1,0:T(8,128)(2,1)S(1)} %get-tuple-element.60.inputs, bf16[4,128,256]{2,1,0:T(8,128)(2,1)S(1)} %get-tuple-element.61.pairs, ...), custom_call_target="tpu_custom_call" | custom-call | bytes 25165824 | tf_op jit(solution)/shard_map/adam/pallas_call | solution.py:454
  57.2 0.0 collective-permute-done.8.come
  57.2 0.3 back_x.1
  57.5 0.7 %collective-permute-start.10 = (bf16[4,4,16,128]{3,2,1,0:T(8,128)(2,1)S(1)}, bf16[4,4,16,128]{3,2,1,0:T(8,128)(2,1)S(1)}, u32[]{:S(2)}, u32[]{:S(2)}) collective-permute-start(bf16[4,4,16,128]{3,2,1,0:T(8,128)(2,1)S(1)} %get-tuple-element.66), channel_id=1, source_target_pairs={{0,2},{1,3},{2,0},{3,1},{4,6},{5,7},{6,4},{7,5},{8,10},{9,11},{10,... | collective-permute-start | bytes 196616 | tf_op jit(solution)/shard_map/ppermute | solution.py:338
  58.2 1.4 %collective-permute-start.11 = (bf16[4,4,16,128]{3,2,1,0:T(8,128)(2,1)S(1)}, bf16[4,4,16,128]{3,2,1,0:T(8,128)(2,1)S(1)}, u32[]{:S(2)}, u32[]{:S(2)}) collective-permute-start(bf16[4,4,16,128]{3,2,1,0:T(8,128)(2,1)S(1)} %get-tuple-element.67), channel_id=1, source_target_pairs={{0,3},{1,2},{2,1},{3,0},{4,7},{5,6},{6,5},{7,4},{8,11},{9,10},{10,... | collective-permute-start | bytes 196616 | tf_op jit(solution)/shard_map/ppermute | solution.py:338
  59.6 1.5 %collective-permute-start.9 = (bf16[4,4,16,128]{3,2,1,0:T(8,128)(2,1)S(1)}, bf16[4,4,16,128]{3,2,1,0:T(8,128)(2,1)S(1)}, u32[]{:S(2)}, u32[]{:S(2)}) collective-permute-start(bf16[4,4,16,128]{3,2,1,0:T(8,128)(2,1)S(1)} %get-tuple-element.65.refs_0_), channel_id=1, source_target_pairs={{0,1},{1,0},{2,3},{3,2},{4,5},{5,4},{6,7},{7,6},{8,9},{9,8},{10,11... | collective-permute-start | bytes 196616 | tf_op jit(solution)/shard_map/ppermute | solution.py:338
  61.0 3.2 %adam.3 = (f32[2,32,2,128,128]{4,3,2,1,0:T(8,128)}, f32[2,32,2,128,128]{4,3,2,1,0:T(8,128)}, f32[2,32,2,128,128]{4,3,2,1,0:T(8,128)}, f32[8,128]{1,0:T(8,128)S(1)}) custom-call(bf16[4,128,128]{2,1,0:T(8,128)(2,1)S(1)} %get-tuple-element.60.inputs, ...), custom_call_target="tpu_custom_call", output_to_operand_aliasing={{0}: (6, {}), {1}: (7, {}), {2}: (8, {})} | custom-call | bytes 8388608 | tf_op jit(solution)/shard_map/adam/pallas_call | solution.py:454
  64.3 0.0 collective-permute-done.10.refs_2_
  64.3 0.0 collective-permute-done.11.refs_3_
  64.3 0.0 collective-permute-done.9.refs_1_
  64.3 1.1 %back_yz.1 = bf16[4,512,128]{2,1,0:T(8,128)(2,1)} custom-call(bf16[4,4,16,128]{3,2,1,0:T(8,128)(2,1)S(1)} %get-tuple-element.64.refs_0_, bf16[4,4,16,128]{3,2,1,0:T(8,128)(2,1)S(1)} %collective-permute-done.9.refs_1_, bf16[4,4,16,128]{3,2,1,0:T(8,128)(2,1)S(1)} %collective-permute-done.10.refs_2_, ...), custom_call_target="tpu_custom_call" | custom-call | tf_op jit(solution)/shard_map/back_yz/pallas_call | solution.py:484
  (1 shorter events, 0.0 us)
Async XLA Ops:
  2.2 8.5 %collective-permute-start = (bf16[4,64,128]{2,1,0:T(8,128)(2,1)S(1)}, bf16[4,64,128]{2,1,0:T(8,128)(2,1)S(1)}, u32[]{:S(2)}, u32[]{:S(2)}) collective-permute-start(bf16[4,64,128]{2,1,0:T(8,128)(2,1)S(1)} %get-tuple-element.41), channel_id=1, source_target_pairs={{0,1},{1,0},{2,3},{3,2},{4,5},{5,4},{6,7},{7,6},{8,9},{9,8},{10,11... | collective-permute-start | bytes 196616 | tf_op jit(solution)/shard_map/ppermute | solution.py:338
  5.2 5.5 %collective-permute-start.1 = (bf16[4,64,128]{2,1,0:T(8,128)(2,1)S(1)}, bf16[4,64,128]{2,1,0:T(8,128)(2,1)S(1)}, u32[]{:S(2)}, u32[]{:S(2)}) collective-permute-start(bf16[4,64,128]{2,1,0:T(8,128)(2,1)S(1)} %get-tuple-element.42), channel_id=1, source_target_pairs={{0,2},{1,3},{2,0},{3,1},{4,6},{5,7},{6,4},{7,5},{8,10},{9,11},{10,... | collective-permute-start | bytes 196616 | tf_op jit(solution)/shard_map/ppermute | solution.py:338
  6.8 5.3 %collective-permute-start.2 = (bf16[4,64,128]{2,1,0:T(8,128)(2,1)S(1)}, bf16[4,64,128]{2,1,0:T(8,128)(2,1)S(1)}, u32[]{:S(2)}, u32[]{:S(2)}) collective-permute-start(bf16[4,64,128]{2,1,0:T(8,128)(2,1)S(1)} %get-tuple-element.43), channel_id=1, source_target_pairs={{0,3},{1,2},{2,1},{3,0},{4,7},{5,6},{6,5},{7,4},{8,11},{9,10},{10,... | collective-permute-start | bytes 196616 | tf_op jit(solution)/shard_map/ppermute | solution.py:338
  7.1 7.9 %collective-permute-start.4 = (bf16[4,64,128]{2,1,0:T(8,128)(2,1)S(1)}, bf16[4,64,128]{2,1,0:T(8,128)(2,1)S(1)}, u32[]{:S(2)}, u32[]{:S(2)}) collective-permute-start(bf16[4,64,128]{2,1,0:T(8,128)(2,1)S(1)} %get-tuple-element.50), channel_id=1, source_target_pairs={{0,1},{1,0},{2,3},{3,2},{4,5},{5,4},{6,7},{7,6},{8,9},{9,8},{10,11... | collective-permute-start | bytes 196616 | tf_op jit(solution)/shard_map/ppermute | solution.py:338
  9.1 5.9 %collective-permute-start.5 = (bf16[4,64,128]{2,1,0:T(8,128)(2,1)S(1)}, bf16[4,64,128]{2,1,0:T(8,128)(2,1)S(1)}, u32[]{:S(2)}, u32[]{:S(2)}) collective-permute-start(bf16[4,64,128]{2,1,0:T(8,128)(2,1)S(1)} %get-tuple-element.51), channel_id=1, source_target_pairs={{0,2},{1,3},{2,0},{3,1},{4,6},{5,7},{6,4},{7,5},{8,10},{9,11},{10,... | collective-permute-start | bytes 196616 | tf_op jit(solution)/shard_map/ppermute | solution.py:338
  10.7 5.9 %collective-permute-start.6 = (bf16[4,64,128]{2,1,0:T(8,128)(2,1)S(1)}, bf16[4,64,128]{2,1,0:T(8,128)(2,1)S(1)}, u32[]{:S(2)}, u32[]{:S(2)}) collective-permute-start(bf16[4,64,128]{2,1,0:T(8,128)(2,1)S(1)} %get-tuple-element.52), channel_id=1, source_target_pairs={{0,3},{1,2},{2,1},{3,0},{4,7},{5,6},{6,5},{7,4},{8,11},{9,10},{10,... | collective-permute-start | bytes 196616 | tf_op jit(solution)/shard_map/ppermute | solution.py:338
  12.4 11.6 %collective-permute-start.3 = (bf16[16,32,128]{2,1,0:T(8,128)(2,1)S(1)}, bf16[16,32,128]{2,1,0:T(8,128)(2,1)S(1)}, u32[]{:S(2)}, u32[]{:S(2)}) collective-permute-start(bf16[16,32,128]{2,1,0:T(8,128)(2,1)S(1)} %get-tuple-element.46.refs_5_), channel_id=1, source_target_pairs={{0,4},{4,0},{1,5},{5,1},{2,6},{6,2},{3,7},{7,3},{8,12},{12,8},{9,1... | collective-permute-start | bytes 393224 | tf_op jit(solution)/shard_map/ppermute | solution.py:343
  16.8 32.9 %slice-start = ((s8[8388608]{0:T(1024)(128)(4,1)}), s8[4194304]{0:T(1024)(128)(4,1)S(1)}, s32[]{:S(2)}) async-start(s8[8388608]{0:T(1024)(128)(4,1)} %bitcast.5), calls=%async_computation.2 | async-start | bytes 8388608
  16.8 32.8 %copy-start = (f32[2,32,2,128,128]{4,3,2,1,0:T(8,128)S(1)}, f32[2,32,2,128,128]{4,3,2,1,0:T(8,128)}, u32[]{:S(2)}) copy-start(f32[2,32,2,128,128]{4,3,2,1,0:T(8,128)} %second.3) | copy-start | bytes 25165828
  16.9 8.5 %collective-permute-start.7 = (bf16[16,32,128]{2,1,0:T(8,128)(2,1)S(1)}, bf16[16,32,128]{2,1,0:T(8,128)(2,1)S(1)}, u32[]{:S(2)}, u32[]{:S(2)}) collective-permute-start(bf16[16,32,128]{2,1,0:T(8,128)(2,1)S(1)} %get-tuple-element.54.after), channel_id=1, source_target_pairs={{0,4},{4,0},{1,5},{5,1},{2,6},{6,2},{3,7},{7,3},{8,12},{12,8},{9,1... | collective-permute-start | bytes 393224 | tf_op jit(solution)/shard_map/ppermute | solution.py:343
  25.3 24.4 %slice-start.1 = ((s8[8388608]{0:T(1024)(128)(4,1)}), s8[4194304]{0:T(1024)(128)(4,1)S(1)}, s32[]{:S(2)}) async-start(s8[8388608]{0:T(1024)(128)(4,1)} %bitcast.5), calls=%async_computation.3 | async-start | bytes 8388608
  46.7 10.5 %collective-permute-start.8 = (bf16[16,32,128]{2,1,0:T(8,128)(2,1)S(1)}, bf16[16,32,128]{2,1,0:T(8,128)(2,1)S(1)}, u32[]{:S(2)}, u32[]{:S(2)}) collective-permute-start(bf16[16,32,128]{2,1,0:T(8,128)(2,1)S(1)} %all_to_all.11.refs_0_.own), channel_id=1, source_target_pairs={{0,4},{4,0},{1,5},{5,1},{2,6},{6,2},{3,7},{7,3},{8,12},{12,8},{9,1... | collective-permute-start | bytes 393224 | tf_op jit(solution)/shard_map/ppermute | solution.py:343
  57.5 6.8 %collective-permute-start.10 = (bf16[4,4,16,128]{3,2,1,0:T(8,128)(2,1)S(1)}, bf16[4,4,16,128]{3,2,1,0:T(8,128)(2,1)S(1)}, u32[]{:S(2)}, u32[]{:S(2)}) collective-permute-start(bf16[4,4,16,128]{3,2,1,0:T(8,128)(2,1)S(1)} %get-tuple-element.66), channel_id=1, source_target_pairs={{0,2},{1,3},{2,0},{3,1},{4,6},{5,7},{6,4},{7,5},{8,10},{9,11},{10,... | collective-permute-start | bytes 196616 | tf_op jit(solution)/shard_map/ppermute | solution.py:338
  58.2 6.1 %collective-permute-start.11 = (bf16[4,4,16,128]{3,2,1,0:T(8,128)(2,1)S(1)}, bf16[4,4,16,128]{3,2,1,0:T(8,128)(2,1)S(1)}, u32[]{:S(2)}, u32[]{:S(2)}) collective-permute-start(bf16[4,4,16,128]{3,2,1,0:T(8,128)(2,1)S(1)} %get-tuple-element.67), channel_id=1, source_target_pairs={{0,3},{1,2},{2,1},{3,0},{4,7},{5,6},{6,5},{7,4},{8,11},{9,10},{10,... | collective-permute-start | bytes 196616 | tf_op jit(solution)/shard_map/ppermute | solution.py:338
  59.6 4.7 %collective-permute-start.9 = (bf16[4,4,16,128]{3,2,1,0:T(8,128)(2,1)S(1)}, bf16[4,4,16,128]{3,2,1,0:T(8,128)(2,1)S(1)}, u32[]{:S(2)}, u32[]{:S(2)}) collective-permute-start(bf16[4,4,16,128]{3,2,1,0:T(8,128)(2,1)S(1)} %get-tuple-element.65.refs_0_), channel_id=1, source_target_pairs={{0,1},{1,0},{2,3},{3,2},{4,5},{5,4},{6,7},{7,6},{8,9},{9,8},{10,11... | collective-permute-start | bytes 196616 | tf_op jit(solution)/shard_map/ppermute | solution.py:338

commit v5 on v4

--- a/solution.py
+++ b/solution.py
@@ -99,74 +99,47 @@
     return lax.dot_general(a, b, (dims, ((), ())), preferred_element_type=f32)
 
 
-def yz_transform(source, mixed, blocks):
-    rows = mixed.shape[0] // QUAD
-    for x in range(0, source.shape[0], 2):
-        pair = jnp.concatenate([source[x], source[x + 1]], axis=1)
-        result = dot(mixed[...], pair).astype(half)
-        for r in range(QUAD):
-            piece = result[r * rows : (r + 1) * rows]
-            blocks[r][x] = piece[:, :C]
-            blocks[r][x + 1] = piece[:, C:]
-
-
-def yz_field_kernel(field, cotangent, table, later, *refs):
-    blocks, (mixed, cot_held, later_held, cells_in, sems) = refs[:QUAD], refs[QUAD:]
+def yz_kernel(field, cotangent, table, *refs):
+    blocks, (mixed, cells_in, sems) = refs[:QUAD], refs[QUAD:]
     rows = table.shape[1]
+    cells = field.shape[0]
     loads = [
         pltpu.make_async_copy(table.at[lax.axis_index("quad") ^ r], mixed.at[pl.ds(r * rows, rows)], sems.at[r]) for r in range(QUAD)
     ]
-    for source, target in ((field, cells_in), (cotangent, cot_held), (later, later_held)):
-        loads.append(pltpu.make_async_copy(source, target, sems.at[len(loads)]))
+    for which, source in enumerate((field, cotangent)):
+        loads.append(pltpu.make_async_copy(source, cells_in.at[which], sems.at[len(loads)]))
     for load in loads:
         load.start()
-    for load in loads[: QUAD + 1]:
+    for load in loads:
         load.wait()
-    yz_transform(cells_in, mixed, blocks)
-    for load in loads[QUAD + 1 :]:
-        load.wait()
-
-
-def yz_cot_kernel(cot_held, mixed, *blocks):
-    yz_transform(cot_held, mixed, blocks)
-
-
-def x_transform(pieces, table, held):
+    for which in range(2):
+        for x in range(0, cells, 2):
+            pair = jnp.concatenate([cells_in[which, x], cells_in[which, x + 1]], axis=1)
+            result = dot(mixed[...], pair).astype(half)
+            for r in range(QUAD):
+                piece = result[r * rows : (r + 1) * rows]
+                blocks[r][which, x] = piece[:, :C]
+                blocks[r][which, x + 1] = piece[:, C:]
+
+
+def x_kernel(*refs):
+    pieces, (table, out, held) = refs[:QUAD], refs[QUAD:]
     for r in range(QUAD):
         held[lax.axis_index("quad") ^ r] = pieces[r][...]
     matrix = table[lax.axis_index("half")]
-    cells, rows = held.shape[1:3]
+    fields, cells, rows = held.shape[1:4]
     height = matrix.shape[1] // QUAD // cells
-    results = []
-    for d in range(0, rows // height, 2):
+    spaces = out.shape[0] // (rows // height)
+    for d in range(rows // height):
         columns = [
             jnp.concatenate(
-                [held[q, x, k * height : (k + 1) * height, :] for q in range(QUAD) for x in range(cells)], axis=0
+                [held[q, f, x, d * height : (d + 1) * height, :] for q in range(QUAD) for x in range(cells)], axis=0
             )
-            for k in (d, d + 1)
+            for f in range(fields)
         ]
         result = dot(matrix, jnp.concatenate(columns, axis=1)).astype(half)
-        results += [result[:, :C], result[:, C:]]
-    return results
-
-
-def x_kernel(extra, *refs):
-    pieces, table, (own, other, held, split) = refs[:QUAD], refs[QUAD], refs[QUAD + 1 + extra :]
-    for d, result in enumerate(x_transform(pieces, table, held)):
-        split[:, d * QUAD : (d + 1) * QUAD] = result.reshape(split.shape[0], QUAD, -1, C)
-    own[...] = split[lax.axis_index("half")]
-    other[...] = split[1 - lax.axis_index("half")]
-
-
-def sum_kernel(field_own, field_come, cot_own, cot_come, *refs):
-    out = refs[-1]
-    for which, (own, come) in enumerate(((field_own, field_come), (cot_own, cot_come))):
-        out[:, which] = (own[...].astype(f32) + come[...].astype(f32)).astype(half)
-
-
-def start_all(loads):
-    for load in loads:
-        load.start()
+        for f in range(fields):
+            out[d * spaces : (d + 1) * spaces, f] = result[:, f * C : (f + 1) * C].reshape(spaces, -1, C)
 
 
 def stage_kernel(after, weights, *refs):
@@ -206,12 +179,12 @@
 
 
 def modes_kernel(arrived, weights, gather, scatter, sent, inputs, pairs):
-    batch, quad, _, rows, _ = arrived.shape
+    batch, halves, quad, _, rows, _ = arrived.shape
     modes, pencils = weights.shape[0], weights.shape[1] // quad
     height = batch * 2
     for q in range(quad):
-        field = arrived[:, q, 0].reshape(-1, C)
-        cot = arrived[:, q, 1].reshape(-1, C)
+        field = arrived[:, :, q, 0].reshape(-1, C)
+        cot = arrived[:, :, q, 1].reshape(-1, C)
         both = dot(gather[0], jnp.concatenate([field, cot], axis=1)).astype(half)
         inputs[q] = both[:, :C]
         pair = jnp.concatenate([both[:, C:], dot(gather[1], cot).astype(half)], axis=1)
@@ -355,79 +328,52 @@
     table_yz = yz_table(owners)
     table_x, back_table_x = x_tables(total_x, halves, pencils)
     back_table_yz = np.ascontiguousarray(table_yz.reshape(MYZ * 2, NY * NZ).T)
-    gather = gather_tables(owners, 1, modes, pencils)
+    gather = gather_tables(owners, halves, modes, pencils)
     scatter = scatter_table(owners, modes, pencils)
     vmem = lambda values: pltpu.VMEM(values.shape, values.dtype)
 
     flat = (cells, NY * NZ, C)
-    block = pltpu.VMEM((cells, owners * height, C), half)
-    *field_blocks, mixed, cot_held, table_x = pl.pallas_call(
-        yz_field_kernel,
-        out_shape=[block] * QUAD + [pltpu.VMEM((MYZ * 2, NY * NZ), half), pltpu.VMEM(flat, half), vmem(table_x)],
-        in_specs=[HBM] * 4,
-        out_specs=[VMEM] * (QUAD + 3),
-        scratch_shapes=[pltpu.VMEM(flat, half), pltpu.SemaphoreType.DMA((QUAD + 3,))],
+    blocks = pl.pallas_call(
+        yz_kernel,
+        out_shape=[pltpu.VMEM((2, cells, owners * height, C), half)] * QUAD,
+        in_specs=[HBM] * 3,
+        out_specs=[VMEM] * QUAD,
+        scratch_shapes=[
+            pltpu.VMEM((MYZ * 2, NY * NZ), half),
+            pltpu.VMEM((2,) + flat, half),
+            pltpu.SemaphoreType.DMA((QUAD + 2,)),
+        ],
         compiler_params=params(8),
-        name="yz_modes_field",
-    )(
-        in_hbm(field.reshape(flat)),
-        in_hbm(cotangent.reshape(flat)),
-        in_hbm(jnp.asarray(table_yz)),
-        in_hbm(jnp.asarray(table_x)),
-    )
-    cot_blocks = pl.pallas_call(
-        yz_cot_kernel,
-        out_shape=[block] * QUAD,
-        in_specs=[VMEM] * 2,
-        out_specs=[VMEM] * QUAD,
-        compiler_params=params(8),
-        name="yz_modes_cot",
-    )(cot_held, mixed)
+        name="yz_modes",
+    )(in_hbm(field.reshape(flat)), in_hbm(cotangent.reshape(flat)), in_hbm(jnp.asarray(table_yz)))
 
     split = (modes, QUAD * pencils, 2, C, C)
     big, first, second = weights.reshape(split), first_moment.reshape(split), second_moment.reshape(split)
-    field_blocks = exchange(field_blocks)
-    cot_blocks = exchange(cot_blocks)
-
-    rows = modes * height
-    per_half = (owners * QUAD, rows, C)
-    gathered = pltpu.VMEM((QUAD, cells, owners * height, C), half)
-
-    def x_modes(pieces, *after):
-        return pl.pallas_call(
-            functools.partial(x_kernel, len(after)),
-            out_shape=[pltpu.VMEM(per_half, half)] * 2,
-            in_specs=[VMEM] * (QUAD + 1) + [ANY] * len(after),
-            out_specs=[VMEM] * 2,
-            scratch_shapes=[gathered, pltpu.VMEM((halves,) + per_half, half)],
-            compiler_params=params(8),
-            name="x_modes",
-        )(*pieces, table_x, *after)
-
-    field_own, field_other = x_modes(field_blocks)
-    field_come = swap_halves(field_other)
-    cot_own, cot_other = x_modes(cot_blocks, field_other)
-    cot_come = swap_halves(cot_other)
-    staged = [jnp.asarray(t) for t in (gather, scatter, back_table_x, back_table_yz)]
-    weights_held, gather, scatter, back_table_x, back_table_yz, rounded = pl.pallas_call(
+    staged = [jnp.asarray(t) for t in (table_x, gather, scatter, back_table_x, back_table_yz)]
+    weights_held, table_x, gather, scatter, back_table_x, back_table_yz, rounded = pl.pallas_call(
         stage_kernel,
         out_shape=[vmem(big)] + [vmem(t) for t in staged] + [pltpu.VMEM((modes, QUAD * pencils, C, 2 * C), half)],
         in_specs=[ANY] + [HBM] * (1 + len(staged)),
         out_specs=[VMEM] * (2 + len(staged)),
-        scratch_shapes=[pltpu.SemaphoreType.DMA((12 * modes + len(staged) - 2,))],
+        scratch_shapes=[pltpu.SemaphoreType.DMA((4 * modes + len(staged),))],
         compiler_params=params(8),
         cost_estimate=cost(0),
         name="stage",
-    )(cot_other, in_hbm(big), *[in_hbm(t) for t in staged])
-    summed = pl.pallas_call(
-        sum_kernel,
-        out_shape=pltpu.VMEM((owners * QUAD, 2, rows, C), half),
-        in_specs=[VMEM] * 4 + [ANY],
+    )(blocks[0], in_hbm(big), *[in_hbm(t) for t in staged])
+    blocks = exchange(blocks)
+
+    rows = modes * height
+    per_half = (owners * QUAD, rows, C)
+    partial = pl.pallas_call(
+        x_kernel,
+        out_shape=pltpu.VMEM((owners * spaces, 2, rows, C), half),
+        in_specs=[VMEM] * (QUAD + 1),
         out_specs=VMEM,
+        scratch_shapes=[pltpu.VMEM((QUAD, 2, cells, owners * height, C), half)],
         compiler_params=params(8),
-        name="sum_halves",
-    )(field_own, field_come, cot_own, cot_come, rounded)
-    arrived = lax.all_to_all(summed, ("dp", "quad"), 0, 0, tiled=True)
+        name="x_modes",
+    )(*blocks, table_x)
+    arrived = lax.all_to_all(partial, ("dp", "half", "quad"), 0, 0, tiled=True)
 
     mode_rows = rows * owners
     sent, inputs, pairs = pl.pallas_call(
@@ -441,7 +387,7 @@
         out_specs=[VMEM] * 3,
         compiler_params=params(8),
         name="mode_grads",
-    )(arrived.reshape(owners, QUAD, 2, rows, C), rounded, gather, scatter)
+    )(arrived.reshape(owners, halves, QUAD, 2, rows, C), rounded, gather, scatter)
     back = lax.all_to_all(sent.reshape(per_half), ("dp", "quad"), 0, 0, tiled=True)
     back_come = swap_halves(back)
 

time: 65.7 us -> 63.9 us (0.973)
  blocking collectives: 19.3 us -> 30.8 us
  starting transfers between devices: 20 us -> 9.24 us
  waiting for transfers between devices: 4.24 us -> 2.72 us
  Pallas kernels: 21.1 us -> 20.2 us
    all_to_all x1, blocking collectives: 10.6 us -> 22.2 us  [fast(): arrived = lax.all_to_all(partial, ('dp', 'half', 'quad'), 0, 0, tiled=True)]
    ppermute x3 -> x1, starting transfers between devices: 8.33 us -> 1.07 us  [swap_halves(): return lax.ppermute(values, 'half', [(0, 1), (1, 0)])]
    ppermute x9 -> x6, starting transfers between devices: 11.7 us -> 8.16 us  [exchange(): lax.ppermute(blocks[r], 'quad', [(q, q ^ r) for q in range(QUAD)])]
    ppermute x9 -> x6, waiting for transfers between devices: 2.91 us -> 2.07 us  [exchange(): lax.ppermute(blocks[r], 'quad', [(q, q ^ r) for q in range(QUAD)])]
    ppermute x3 -> x1, waiting for transfers between devices: 1.33 us -> 0.64 us  [swap_halves(): return lax.ppermute(values, 'half', [(0, 1), (1, 0)])]
    pallas_call x5 -> x2, Pallas kernels: 2.51 us -> 2.19 us  [the longest x1 1.85 us: fast(): pl.pallas_call(yz_kernel, out_shape=[pltpu.VMEM((2, cells, owners * heigh...]
  transfers between devices with their start and end apart: 12 -> 7, of which waited for: 3 -> 3; matrix products, arithmetic and copies ran while one was open for 0% -> 0% of each run, Pallas kernels for 25% -> 23%
where the time goes in v5:
time: 63.9 us; the launch traced here: 63.7 us
  blocking collectives  30.8 us (48%)
  Pallas kernels  20.2 us (32%)
  starting transfers between devices  9.24 us (14%)
  waiting for transfers between devices  2.72 us (4%)
  between operations  0.73 us (1%)
    all_to_all x1, blocking collectives, fast(): arrived = lax.all_to_all(partial, ('dp', 'half', 'quad'), 0, 0, tiled=True)  22.2 us
    pallas_call x2, Pallas kernels, adam(): pl.pallas_call(functools.partial(adam_kernel, begin), out_shape=[pltpu.HB...  10.7 us
    all_to_all x1, blocking collectives, fast(): lax.all_to_all(sent.reshape(per_half), ('dp', 'quad'), 0, 0, tiled=True)  8.65 us
    ppermute x6, starting transfers between devices, exchange(): lax.ppermute(blocks[r], 'quad', [(q, q ^ r) for q in range(QUAD)])  8.16 us
    pallas_call x1, Pallas kernels, fast(): pl.pallas_call(stage_kernel, out_shape=[vmem(big)] + [vmem(t) for t in st...  3.89 us
    ppermute x6, waiting for transfers between devices, exchange(): lax.ppermute(blocks[r], 'quad', [(q, q ^ r) for q in range(QUAD)])  2.07 us
    pallas_call x1, Pallas kernels, fast(): pl.pallas_call(modes_kernel, out_shape=[pltpu.VMEM((owners, QUAD, rows, C...  2 us
    pallas_call x1, Pallas kernels, fast(): pl.pallas_call(yz_kernel, out_shape=[pltpu.VMEM((2, cells, owners * heigh...  1.85 us
  transfers between devices with their start and end apart: 7, of which 3 were waited for; matrix products, arithmetic and copies ran while one was open for 0% of the time, Pallas kernels for 23%

profile of v5, /device:TPU:0, one launch (start us, length us, event | category | flops | bytes accessed | tf_op | source)
XLA Modules:
  0.0 63.7 jit_solution(16964966981659579630)
XLA Ops:
  0.6 1.8 %yz_modes.1 = (bf16[2,4,64,128]{3,2,1,0:T(8,128)(2,1)S(1)}, bf16[2,4,64,128]{3,2,1,0:T(8,128)(2,1)S(1)}, bf16[2,4,64,128]{3,2,1,0:T(8,128)(2,1)S(1)}, bf16[2,4,64,128]{3,2,1,0:T(8,128)(2,1)S(1)}) custom-call(bf16[4,512,128]{2,1,0:T(8,128)(2,1)} %bitcast.9, bf16[4,512,128]{2,1,0:T(8,128)(2,1)} %bitcast.10, bf16[4,64,512]{2,1,0:T(8,128)(2,1)} %constant.12.clone.table), custom_call_target="tpu_custom_call" | custom-call | tf_op jit(solution)/shard_map/yz_modes/pallas_call | solution.py:336
  2.5 3.0 %collective-permute-start = (bf16[2,4,64,128]{3,2,1,0:T(8,128)(2,1)S(1)}, bf16[2,4,64,128]{3,2,1,0:T(8,128)(2,1)S(1)}, u32[]{:S(2)}, u32[]{:S(2)}) collective-permute-start(bf16[2,4,64,128]{3,2,1,0:T(8,128)(2,1)S(1)} %get-tuple-element.31), channel_id=1, source_target_pairs={{0,1},{1,0},{2,3},{3,2},{4,5},{5,4},{6,7},{7,6},{8,9},{9,8},{10,11... | collective-permute-start | bytes 393224 | tf_op jit(solution)/shard_map/ppermute | solution.py:311
  5.5 1.6 %collective-permute-start.1 = (bf16[2,4,64,128]{3,2,1,0:T(8,128)(2,1)S(1)}, bf16[2,4,64,128]{3,2,1,0:T(8,128)(2,1)S(1)}, u32[]{:S(2)}, u32[]{:S(2)}) collective-permute-start(bf16[2,4,64,128]{3,2,1,0:T(8,128)(2,1)S(1)} %get-tuple-element.32), channel_id=1, source_target_pairs={{0,2},{1,3},{2,0},{3,1},{4,6},{5,7},{6,4},{7,5},{8,10},{9,11},{10,... | collective-permute-start | bytes 393224 | tf_op jit(solution)/shard_map/ppermute | solution.py:311
  7.1 0.0 collective-permute-start.2
  7.1 0.0 slice-start
  7.1 0.0 slice-start.1
  7.1 0.0 copy-start
  7.1 3.9 %stage.1 = (f32[2,32,2,128,128]{4,3,2,1,0:T(8,128)S(1)}, bf16[2,256,256]{2,1,0:T(8,128)(2,1)S(1)}, bf16[2,128,256]{2,1,0:T(8,128)(2,1)S(1)}, bf16[128,128]{1,0:T...) custom-call(bf16[2,4,64,128]{3,2,1,0:T(8,128)(2,1)S(1)} %get-tuple-e, ...), custom_call_target="tpu_custom_call" | custom-call | tf_op jit(solution)/shard_map/stage/pallas_call | solution.py:353
  11.0 0.0 collective-permute-done.refs_1_
  11.0 0.9 %collective-permute-done.1.refs_2_ = bf16[2,4,64,128]{3,2,1,0:T(8,128)(2,1)S(1)} collective-permute-done((bf16[2,4,64,128]{3,2,1,0:T(8,128)(2,1)S(1)}, bf16[2,4,64,128]{3,2,1,0:T(8,128)(2,1)S(1)}, u32[]{:S(2)}, u32[]{:S(2)}) %collective-permute-start.1) | collective-permute-done | bytes 131104 | tf_op jit(solution)/shard_map/ppermute | solution.py:311
  11.9 1.2 %collective-permute-done.2.refs_3_ = bf16[2,4,64,128]{3,2,1,0:T(8,128)(2,1)S(1)} collective-permute-done((bf16[2,4,64,128]{3,2,1,0:T(8,128)(2,1)S(1)}, bf16[2,4,64,128]{3,2,1,0:T(8,128)(2,1)S(1)}, u32[]{:S(2)}, u32[]{:S(2)}) %collective-permute-start.2) | collective-permute-done | bytes 131104 | tf_op jit(solution)/shard_map/ppermute | solution.py:311
  13.1 0.3 x_modes.1
  13.4 22.2 %all_to_all.10 = bf16[32,2,32,128]{3,2,1,0:T(8,128)(2,1)S(1)} all-to-all(bf16[32,2,32,128]{3,2,1,0:T(8,128)(2,1)S(1)} %x_modes.1), channel_id=1, replica_groups=mesh['dp'=4,'half'=2,'quad'=4] {'dp','half','quad'}, dimensions={0} | all-to-all | bytes 1048576 | tf_op jit(solution)/shard_map/all_to_all | solution.py:376
  35.6 2.0 %mode_grads.1 = (bf16[4,4,32,128]{3,2,1,0:T(8,128)(2,1)S(1)}, bf16[4,128,128]{2,1,0:T(8,128)(2,1)S(1)}, bf16[4,128,256]{2,1,0:T(8,128)(2,1)S(1)}) custom-call(bf16[4,2,4,2,32,128]{5,4,3,2,1,0:T(8,128)(2,1)S(1)} %bitcast.7, bf16[2,32,128,256]{3,2,1,0:T(8,128)(2,1)S(1)} %get-tuple-element.35.weights, bf16[2,128,256]{2,1,0:T(8,128)(2,1)S(1)} %get-tuple-element.36.gather, ...), custom_call_target="tpu_custom_call" | custom-call | tf_op jit(solution)/shard_map/mode_grads/pallas_call | solution.py:379
  37.6 8.6 %all_to_all.11.refs_0_.own = bf16[16,32,128]{2,1,0:T(8,128)(2,1)S(1)} all-to-all(bf16[16,32,128]{2,1,0:T(8,128)(2,1)S(1)} %bitcast.8), channel_id=1, replica_groups=mesh['dp'=4,'half'=2,'quad'=4] {'dp','quad'}, dimensions={0} | all-to-all | bytes 262144 | tf_op jit(solution)/shard_map/all_to_all | solution.py:391
  46.2 1.1 %collective-permute-start.3 = (bf16[16,32,128]{2,1,0:T(8,128)(2,1)S(1)}, bf16[16,32,128]{2,1,0:T(8,128)(2,1)S(1)}, u32[]{:S(2)}, u32[]{:S(2)}) collective-permute-start(bf16[16,32,128]{2,1,0:T(8,128)(2,1)S(1)} %all_to_all.11.refs_0_.own), channel_id=1, source_target_pairs={{0,4},{4,0},{1,5},{5,1},{2,6},{6,2},{3,7},{7,3},{8,12},{12,8},{9,1... | collective-permute-start | bytes 393224 | tf_op jit(solution)/shard_map/ppermute | solution.py:316
  47.3 0.0 slice-done
  47.3 0.0 slice-done.1
  47.3 0.0 copy-done
  47.3 7.5 %adam.2 = (f32[2,32,2,128,128]{4,3,2,1,0:T(8,128)}, f32[2,32,2,128,128]{4,3,2,1,0:T(8,128)}, f32[2,32,2,128,128]{4,3,2,1,0:T(8,128)}, f32[8,128]{1,0:T(8,128)S(1)}) custom-call(bf16[4,128,128]{2,1,0:T(8,128)(2,1)S(1)} %get-tuple-element.40.inputs, bf16[4,128,256]{2,1,0:T(8,128)(2,1)S(1)} %get-tuple-element.41.pairs, ...), custom_call_target="tpu_custom_call" | custom-call | bytes 25165824 | tf_op jit(solution)/shard_map/adam/pallas_call | solution.py:400
  54.8 0.6 %collective-permute-done.3.come = bf16[16,32,128]{2,1,0:T(8,128)(2,1)S(1)} collective-permute-done((bf16[16,32,128]{2,1,0:T(8,128)(2,1)S(1)}, bf16[16,32,128]{2,1,0:T(8,128)(2,1)S(1)}, u32[]{:S(2)}, u32[]{:S(2)}) %collective-permute-start.3) | collective-permute-done | bytes 131104 | tf_op jit(solution)/shard_map/ppermute | solution.py:316
  55.5 0.3 back_x.1
  55.7 0.1 collective-permute-start.5
  55.8 2.0 %collective-permute-start.6 = (bf16[4,4,16,128]{3,2,1,0:T(8,128)(2,1)S(1)}, bf16[4,4,16,128]{3,2,1,0:T(8,128)(2,1)S(1)}, u32[]{:S(2)}, u32[]{:S(2)}) collective-permute-start(bf16[4,4,16,128]{3,2,1,0:T(8,128)(2,1)S(1)} %get-tuple-element.47), channel_id=1, source_target_pairs={{0,3},{1,2},{2,1},{3,0},{4,7},{5,6},{6,5},{7,4},{8,11},{9,10},{10,... | collective-permute-start | bytes 196616 | tf_op jit(solution)/shard_map/ppermute | solution.py:311
  57.8 1.5 %collective-permute-start.4 = (bf16[4,4,16,128]{3,2,1,0:T(8,128)(2,1)S(1)}, bf16[4,4,16,128]{3,2,1,0:T(8,128)(2,1)S(1)}, u32[]{:S(2)}, u32[]{:S(2)}) collective-permute-start(bf16[4,4,16,128]{3,2,1,0:T(8,128)(2,1)S(1)} %get-tuple-element.45.refs_0_), channel_id=1, source_target_pairs={{0,1},{1,0},{2,3},{3,2},{4,5},{5,4},{6,7},{7,6},{8,9},{9,8},{10,11... | collective-permute-start | bytes 196616 | tf_op jit(solution)/shard_map/ppermute | solution.py:311
  59.3 3.2 %adam.3 = (f32[2,32,2,128,128]{4,3,2,1,0:T(8,128)}, f32[2,32,2,128,128]{4,3,2,1,0:T(8,128)}, f32[2,32,2,128,128]{4,3,2,1,0:T(8,128)}, f32[8,128]{1,0:T(8,128)S(1)}) custom-call(bf16[4,128,128]{2,1,0:T(8,128)(2,1)S(1)} %get-tuple-element.40.inputs, ...), custom_call_target="tpu_custom_call", output_to_operand_aliasing={{0}: (6, {}), {1}: (7, {}), {2}: (8, {})} | custom-call | bytes 8388608 | tf_op jit(solution)/shard_map/adam/pallas_call | solution.py:400
  62.5 0.0 collective-permute-done.5.refs_2_
  62.6 0.0 collective-permute-done.6.refs_3_
  62.6 0.0 collective-permute-done.4.refs_1_
  62.6 1.1 %back_yz.1 = bf16[4,512,128]{2,1,0:T(8,128)(2,1)} custom-call(bf16[4,4,16,128]{3,2,1,0:T(8,128)(2,1)S(1)} %get-tuple-element.44.refs_0_, bf16[4,4,16,128]{3,2,1,0:T(8,128)(2,1)S(1)} %collective-permute-done.4.refs_1_, bf16[4,4,16,128]{3,2,1,0:T(8,128)(2,1)S(1)} %collective-permute-done.5.refs_2_, bf16[4,4,16,128]{3,2,1,0:T(8,128)(2,1)S(1)} %collective-permute-done.6.refs_3_, ...), custom_call_target="tpu_custom_call" | custom-call | tf_op jit(solution)/shard_map/back_yz/pallas_call | solution.py:430
  (1 shorter events, 0.0 us)
Async XLA Ops:
  2.5 8.5 %collective-permute-start = (bf16[2,4,64,128]{3,2,1,0:T(8,128)(2,1)S(1)}, bf16[2,4,64,128]{3,2,1,0:T(8,128)(2,1)S(1)}, u32[]{:S(2)}, u32[]{:S(2)}) collective-permute-start(bf16[2,4,64,128]{3,2,1,0:T(8,128)(2,1)S(1)} %get-tuple-element.31), channel_id=1, source_target_pairs={{0,1},{1,0},{2,3},{3,2},{4,5},{5,4},{6,7},{7,6},{8,9},{9,8},{10,11... | collective-permute-start | bytes 393224 | tf_op jit(solution)/shard_map/ppermute | solution.py:311
  5.5 6.4 %collective-permute-start.1 = (bf16[2,4,64,128]{3,2,1,0:T(8,128)(2,1)S(1)}, bf16[2,4,64,128]{3,2,1,0:T(8,128)(2,1)S(1)}, u32[]{:S(2)}, u32[]{:S(2)}) collective-permute-start(bf16[2,4,64,128]{3,2,1,0:T(8,128)(2,1)S(1)} %get-tuple-element.32), channel_id=1, source_target_pairs={{0,2},{1,3},{2,0},{3,1},{4,6},{5,7},{6,4},{7,5},{8,10},{9,11},{10,... | collective-permute-start | bytes 393224 | tf_op jit(solution)/shard_map/ppermute | solution.py:311
  7.1 6.0 %collective-permute-start.2 = (bf16[2,4,64,128]{3,2,1,0:T(8,128)(2,1)S(1)}, bf16[2,4,64,128]{3,2,1,0:T(8,128)(2,1)S(1)}, u32[]{:S(2)}, u32[]{:S(2)}) collective-permute-start(bf16[2,4,64,128]{3,2,1,0:T(8,128)(2,1)S(1)} %get-tuple-element.33), channel_id=1, source_target_pairs={{0,3},{1,2},{2,1},{3,0},{4,7},{5,6},{6,5},{7,4},{8,11},{9,10},{10,... | collective-permute-start | bytes 393224 | tf_op jit(solution)/shard_map/ppermute | solution.py:311
  7.1 40.2 %slice-start = ((s8[8388608]{0:T(1024)(128)(4,1)}), s8[4194304]{0:T(1024)(128)(4,1)S(1)}, s32[]{:S(2)}) async-start(s8[8388608]{0:T(1024)(128)(4,1)} %bitcast.5), calls=%async_computation.2 | async-start | bytes 8388608
  7.1 40.2 %slice-start.1 = ((s8[8388608]{0:T(1024)(128)(4,1)}), s8[4194304]{0:T(1024)(128)(4,1)S(1)}, s32[]{:S(2)}) async-start(s8[8388608]{0:T(1024)(128)(4,1)} %bitcast.5), calls=%async_computation.3 | async-start | bytes 8388608
  7.1 40.2 %copy-start = (f32[2,32,2,128,128]{4,3,2,1,0:T(8,128)S(1)}, f32[2,32,2,128,128]{4,3,2,1,0:T(8,128)}, u32[]{:S(2)}) copy-start(f32[2,32,2,128,128]{4,3,2,1,0:T(8,128)} %second.3) | copy-start | bytes 25165828
  46.2 9.2 %collective-permute-start.3 = (bf16[16,32,128]{2,1,0:T(8,128)(2,1)S(1)}, bf16[16,32,128]{2,1,0:T(8,128)(2,1)S(1)}, u32[]{:S(2)}, u32[]{:S(2)}) collective-permute-start(bf16[16,32,128]{2,1,0:T(8,128)(2,1)S(1)} %all_to_all.11.refs_0_.own), channel_id=1, source_target_pairs={{0,4},{4,0},{1,5},{5,1},{2,6},{6,2},{3,7},{7,3},{8,12},{12,8},{9,1... | collective-permute-start | bytes 393224 | tf_op jit(solution)/shard_map/ppermute | solution.py:316
  55.7 6.8 %collective-permute-start.5 = (bf16[4,4,16,128]{3,2,1,0:T(8,128)(2,1)S(1)}, bf16[4,4,16,128]{3,2,1,0:T(8,128)(2,1)S(1)}, u32[]{:S(2)}, u32[]{:S(2)}) collective-permute-start(bf16[4,4,16,128]{3,2,1,0:T(8,128)(2,1)S(1)} %get-tuple-element.46), channel_id=1, source_target_pairs={{0,2},{1,3},{2,0},{3,1},{4,6},{5,7},{6,4},{7,5},{8,10},{9,11},{10,... | collective-permute-start | bytes 196616 | tf_op jit(solution)/shard_map/ppermute | solution.py:311
  55.8 6.7 %collective-permute-start.6 = (bf16[4,4,16,128]{3,2,1,0:T(8,128)(2,1)S(1)}, bf16[4,4,16,128]{3,2,1,0:T(8,128)(2,1)S(1)}, u32[]{:S(2)}, u32[]{:S(2)}) collective-permute-start(bf16[4,4,16,128]{3,2,1,0:T(8,128)(2,1)S(1)} %get-tuple-element.47), channel_id=1, source_target_pairs={{0,3},{1,2},{2,1},{3,0},{4,7},{5,6},{6,5},{7,4},{8,11},{9,10},{10,... | collective-permute-start | bytes 196616 | tf_op jit(solution)/shard_map/ppermute | solution.py:311
  57.8 4.7 %collective-permute-start.4 = (bf16[4,4,16,128]{3,2,1,0:T(8,128)(2,1)S(1)}, bf16[4,4,16,128]{3,2,1,0:T(8,128)(2,1)S(1)}, u32[]{:S(2)}, u32[]{:S(2)}) collective-permute-start(bf16[4,4,16,128]{3,2,1,0:T(8,128)(2,1)S(1)} %get-tuple-element.45.refs_0_), channel_id=1, source_target_pairs={{0,1},{1,0},{2,3},{3,2},{4,5},{5,4},{6,7},{7,6},{8,9},{9,8},{10,11... | collective-permute-start | bytes 196616 | tf_op jit(solution)/shard_map/ppermute | solution.py:311

commit v6 on v5

--- a/solution.py
+++ b/solution.py
@@ -86,7 +86,7 @@
                 turned[m, p, b, 0, b, :, m, p, 1] = 1.0
                 turned[m, p, b, 1, b, :, m, p, 0] = -1.0
     rows = modes * pencils * batch * 2
-    both = np.stack([plain.reshape(rows, -1), turned.reshape(rows, -1)])
+    both = np.concatenate([plain.reshape(rows, -1), turned.reshape(rows, -1)])
     return both.astype(ml_dtypes.bfloat16)
 
 
@@ -182,13 +182,19 @@
     batch, halves, quad, _, rows, _ = arrived.shape
     modes, pencils = weights.shape[0], weights.shape[1] // quad
     height = batch * 2
+    columns_out = []
+    all_pairs = []
     for q in range(quad):
         field = arrived[:, :, q, 0].reshape(-1, C)
         cot = arrived[:, :, q, 1].reshape(-1, C)
-        both = dot(gather[0], jnp.concatenate([field, cot], axis=1)).astype(half)
-        inputs[q] = both[:, :C]
-        pair = jnp.concatenate([both[:, C:], dot(gather[1], cot).astype(half)], axis=1)
+        both = dot(gather[...], jnp.concatenate([field, cot], axis=1)).astype(half)
+        count = both.shape[0] // 2
+        inputs[q] = both[:count, :C]
+        pair = jnp.concatenate([both[:count, C:], both[count:, C:]], axis=1)
         pairs[q] = pair
+        all_pairs.append(pair)
+    for q in range(quad):
+        pair = all_pairs[q]
         results = []
         for m in range(modes):
             for p in range(0, pencils, 2):
@@ -197,8 +203,10 @@
                 columns = weights[m, first : first + 2].reshape(2 * C, 2 * C)
                 result = dot(pair[at : at + 2 * height], columns, ((1,), (1,)))
                 results += [result[:height, :C], result[height:, C:]]
-        grads = jnp.concatenate(results, axis=0).astype(half)
-        sent[:, q] = dot(scatter[...], grads).astype(half).reshape(batch, rows, C)
+        columns_out.append(jnp.concatenate(results, axis=0).astype(half))
+    spread = dot(scatter[...], jnp.concatenate(columns_out, axis=1)).astype(half)
+    for q in range(quad):
+        sent[:, q] = spread[:, q * C : (q + 1) * C].reshape(batch, rows, C)
 
 
 def adam_kernel(begin, inputs, pairs, weights, first, second, *refs):

time: 63.9 us -> 63.4 us (level)
  no operation moved by 1% of the time
where the time goes in v6:
time: 63.4 us; the launch traced here: 63.2 us
  blocking collectives  30.8 us (49%)
  Pallas kernels  19.7 us (31%)
  starting transfers between devices  9.24 us (15%)
  waiting for transfers between devices  2.72 us (4%)
  between operations  0.73 us (1%)
    all_to_all x1, blocking collectives, fast(): arrived = lax.all_to_all(partial, ('dp', 'half', 'quad'), 0, 0, tiled=True)  22.2 us
    pallas_call x2, Pallas kernels, adam(): pl.pallas_call(functools.partial(adam_kernel, begin), out_shape=[pltpu.HB...  10.7 us
    all_to_all x1, blocking collectives, fast(): lax.all_to_all(sent.reshape(per_half), ('dp', 'quad'), 0, 0, tiled=True)  8.65 us
    ppermute x6, starting transfers between devices, exchange(): lax.ppermute(blocks[r], 'quad', [(q, q ^ r) for q in range(QUAD)])  8.16 us
    pallas_call x1, Pallas kernels, fast(): pl.pallas_call(stage_kernel, out_shape=[vmem(big)] + [vmem(t) for t in st...  3.89 us
    ppermute x6, waiting for transfers between devices, exchange(): lax.ppermute(blocks[r], 'quad', [(q, q ^ r) for q in range(QUAD)])  2.07 us
    pallas_call x1, Pallas kernels, fast(): pl.pallas_call(yz_kernel, out_shape=[pltpu.VMEM((2, cells, owners * heigh...  1.85 us
    pallas_call x1, Pallas kernels, fast(): pl.pallas_call(modes_kernel, out_shape=[pltpu.VMEM((owners, QUAD, rows, C...  1.49 us
  transfers between devices with their start and end apart: 7, of which 3 were waited for; matrix products, arithmetic and copies ran while one was open for 0% of the time, Pallas kernels for 23%

profile of v6, /device:TPU:0, one launch (start us, length us, event | category | flops | bytes accessed | tf_op | source)
XLA Modules:
  0.0 63.2 jit_solution(3185185955969497465)
XLA Ops:
  0.6 1.8 %yz_modes.1 = (bf16[2,4,64,128]{3,2,1,0:T(8,128)(2,1)S(1)}, bf16[2,4,64,128]{3,2,1,0:T(8,128)(2,1)S(1)}, bf16[2,4,64,128]{3,2,1,0:T(8,128)(2,1)S(1)}, bf16[2,4,64,128]{3,2,1,0:T(8,128)(2,1)S(1)}) custom-call(bf16[4,512,128]{2,1,0:T(8,128)(2,1)} %bitcast.9, bf16[4,512,128]{2,1,0:T(8,128)(2,1)} %bitcast.10, bf16[4,64,512]{2,1,0:T(8,128)(2,1)} %constant.12.clone.table), custom_call_target="tpu_custom_call" | custom-call | tf_op jit(solution)/shard_map/yz_modes/pallas_call | solution.py:344
  2.5 3.0 %collective-permute-start = (bf16[2,4,64,128]{3,2,1,0:T(8,128)(2,1)S(1)}, bf16[2,4,64,128]{3,2,1,0:T(8,128)(2,1)S(1)}, u32[]{:S(2)}, u32[]{:S(2)}) collective-permute-start(bf16[2,4,64,128]{3,2,1,0:T(8,128)(2,1)S(1)} %get-tuple-element.31), channel_id=1, source_target_pairs={{0,1},{1,0},{2,3},{3,2},{4,5},{5,4},{6,7},{7,6},{8,9},{9,8},{10,11... | collective-permute-start | bytes 393224 | tf_op jit(solution)/shard_map/ppermute | solution.py:319
  5.5 1.6 %collective-permute-start.1 = (bf16[2,4,64,128]{3,2,1,0:T(8,128)(2,1)S(1)}, bf16[2,4,64,128]{3,2,1,0:T(8,128)(2,1)S(1)}, u32[]{:S(2)}, u32[]{:S(2)}) collective-permute-start(bf16[2,4,64,128]{3,2,1,0:T(8,128)(2,1)S(1)} %get-tuple-element.32), channel_id=1, source_target_pairs={{0,2},{1,3},{2,0},{3,1},{4,6},{5,7},{6,4},{7,5},{8,10},{9,11},{10,... | collective-permute-start | bytes 393224 | tf_op jit(solution)/shard_map/ppermute | solution.py:319
  7.1 0.0 collective-permute-start.2
  7.1 0.0 slice-start
  7.1 0.0 slice-start.1
  7.1 0.0 copy-start
  7.1 3.9 %stage.1 = (f32[2,32,2,128,128]{4,3,2,1,0:T(8,128)S(1)}, bf16[2,256,256]{2,1,0:T(8,128)(2,1)S(1)}, bf16[256,256]{1,0:T(8,128)(2,1)S(1)}, bf16[128,128]{1,0:T(8,1...) custom-call(bf16[2,4,64,128]{3,2,1,0:T(8,128)(2,1)S(1)} %get-tuple-e, ...), custom_call_target="tpu_custom_call" | custom-call | tf_op jit(solution)/shard_map/stage/pallas_call | solution.py:361
  11.0 0.0 collective-permute-done.refs_1_
  11.0 0.9 %collective-permute-done.1.refs_2_ = bf16[2,4,64,128]{3,2,1,0:T(8,128)(2,1)S(1)} collective-permute-done((bf16[2,4,64,128]{3,2,1,0:T(8,128)(2,1)S(1)}, bf16[2,4,64,128]{3,2,1,0:T(8,128)(2,1)S(1)}, u32[]{:S(2)}, u32[]{:S(2)}) %collective-permute-start.1) | collective-permute-done | bytes 131104 | tf_op jit(solution)/shard_map/ppermute | solution.py:319
  11.9 1.2 %collective-permute-done.2.refs_3_ = bf16[2,4,64,128]{3,2,1,0:T(8,128)(2,1)S(1)} collective-permute-done((bf16[2,4,64,128]{3,2,1,0:T(8,128)(2,1)S(1)}, bf16[2,4,64,128]{3,2,1,0:T(8,128)(2,1)S(1)}, u32[]{:S(2)}, u32[]{:S(2)}) %collective-permute-start.2) | collective-permute-done | bytes 131104 | tf_op jit(solution)/shard_map/ppermute | solution.py:319
  13.1 0.3 x_modes.1
  13.4 22.2 %all_to_all.10 = bf16[32,2,32,128]{3,2,1,0:T(8,128)(2,1)S(1)} all-to-all(bf16[32,2,32,128]{3,2,1,0:T(8,128)(2,1)S(1)} %x_modes.1), channel_id=1, replica_groups=mesh['dp'=4,'half'=2,'quad'=4] {'dp','half','quad'}, dimensions={0} | all-to-all | bytes 1048576 | tf_op jit(solution)/shard_map/all_to_all | solution.py:384
  35.6 1.5 %mode_grads.1 = (bf16[4,4,32,128]{3,2,1,0:T(8,128)(2,1)S(1)}, bf16[4,128,128]{2,1,0:T(8,128)(2,1)S(1)}, bf16[4,128,256]{2,1,0:T(8,128)(2,1)S(1)}) custom-call(bf16[4,2,4,2,32,128]{5,4,3,2,1,0:T(8,128)(2,1)S(1)} %bitcast.7, bf16[2,32,128,256]{3,2,1,0:T(8,128)(2,1)S(1)} %get-tuple-element.35.weights, bf16[256,256]{1,0:T(8,128)(2,1)S(1)} %get-tuple-element.36.gather, ...), custom_call_target="tpu_custom_call" | custom-call | tf_op jit(solution)/shard_map/mode_grads/pallas_call | solution.py:387
  37.1 8.6 %all_to_all.11.refs_0_.own = bf16[16,32,128]{2,1,0:T(8,128)(2,1)S(1)} all-to-all(bf16[16,32,128]{2,1,0:T(8,128)(2,1)S(1)} %bitcast.8), channel_id=1, replica_groups=mesh['dp'=4,'half'=2,'quad'=4] {'dp','quad'}, dimensions={0} | all-to-all | bytes 262144 | tf_op jit(solution)/shard_map/all_to_all | solution.py:399
  45.7 1.1 %collective-permute-start.3 = (bf16[16,32,128]{2,1,0:T(8,128)(2,1)S(1)}, bf16[16,32,128]{2,1,0:T(8,128)(2,1)S(1)}, u32[]{:S(2)}, u32[]{:S(2)}) collective-permute-start(bf16[16,32,128]{2,1,0:T(8,128)(2,1)S(1)} %all_to_all.11.refs_0_.own), channel_id=1, source_target_pairs={{0,4},{4,0},{1,5},{5,1},{2,6},{6,2},{3,7},{7,3},{8,12},{12,8},{9,1... | collective-permute-start | bytes 393224 | tf_op jit(solution)/shard_map/ppermute | solution.py:324
  46.8 0.0 slice-done
  46.8 0.0 slice-done.1
  46.8 0.0 copy-done
  46.8 7.5 %adam.2 = (f32[2,32,2,128,128]{4,3,2,1,0:T(8,128)}, f32[2,32,2,128,128]{4,3,2,1,0:T(8,128)}, f32[2,32,2,128,128]{4,3,2,1,0:T(8,128)}, f32[8,128]{1,0:T(8,128)S(1)}) custom-call(bf16[4,128,128]{2,1,0:T(8,128)(2,1)S(1)} %get-tuple-element.40.inputs, bf16[4,128,256]{2,1,0:T(8,128)(2,1)S(1)} %get-tuple-element.41.pairs, ...), custom_call_target="tpu_custom_call" | custom-call | bytes 25165824 | tf_op jit(solution)/shard_map/adam/pallas_call | solution.py:408
  54.3 0.6 %collective-permute-done.3.come = bf16[16,32,128]{2,1,0:T(8,128)(2,1)S(1)} collective-permute-done((bf16[16,32,128]{2,1,0:T(8,128)(2,1)S(1)}, bf16[16,32,128]{2,1,0:T(8,128)(2,1)S(1)}, u32[]{:S(2)}, u32[]{:S(2)}) %collective-permute-start.3) | collective-permute-done | bytes 131104 | tf_op jit(solution)/shard_map/ppermute | solution.py:324
  55.0 0.3 back_x.1
  55.2 0.1 collective-permute-start.5
  55.3 2.0 %collective-permute-start.6 = (bf16[4,4,16,128]{3,2,1,0:T(8,128)(2,1)S(1)}, bf16[4,4,16,128]{3,2,1,0:T(8,128)(2,1)S(1)}, u32[]{:S(2)}, u32[]{:S(2)}) collective-permute-start(bf16[4,4,16,128]{3,2,1,0:T(8,128)(2,1)S(1)} %get-tuple-element.47), channel_id=1, source_target_pairs={{0,3},{1,2},{2,1},{3,0},{4,7},{5,6},{6,5},{7,4},{8,11},{9,10},{10,... | collective-permute-start | bytes 196616 | tf_op jit(solution)/shard_map/ppermute | solution.py:319
  57.3 1.5 %collective-permute-start.4 = (bf16[4,4,16,128]{3,2,1,0:T(8,128)(2,1)S(1)}, bf16[4,4,16,128]{3,2,1,0:T(8,128)(2,1)S(1)}, u32[]{:S(2)}, u32[]{:S(2)}) collective-permute-start(bf16[4,4,16,128]{3,2,1,0:T(8,128)(2,1)S(1)} %get-tuple-element.45.refs_0_), channel_id=1, source_target_pairs={{0,1},{1,0},{2,3},{3,2},{4,5},{5,4},{6,7},{7,6},{8,9},{9,8},{10,11... | collective-permute-start | bytes 196616 | tf_op jit(solution)/shard_map/ppermute | solution.py:319
  58.8 3.2 %adam.3 = (f32[2,32,2,128,128]{4,3,2,1,0:T(8,128)}, f32[2,32,2,128,128]{4,3,2,1,0:T(8,128)}, f32[2,32,2,128,128]{4,3,2,1,0:T(8,128)}, f32[8,128]{1,0:T(8,128)S(1)}) custom-call(bf16[4,128,128]{2,1,0:T(8,128)(2,1)S(1)} %get-tuple-element.40.inputs, ...), custom_call_target="tpu_custom_call", output_to_operand_aliasing={{0}: (6, {}), {1}: (7, {}), {2}: (8, {})} | custom-call | bytes 8388608 | tf_op jit(solution)/shard_map/adam/pallas_call | solution.py:408
  62.0 0.0 collective-permute-done.5.refs_2_
  62.1 0.0 collective-permute-done.6.refs_3_
  62.1 0.0 collective-permute-done.4.refs_1_
  62.1 1.1 %back_yz.1 = bf16[4,512,128]{2,1,0:T(8,128)(2,1)} custom-call(bf16[4,4,16,128]{3,2,1,0:T(8,128)(2,1)S(1)} %get-tuple-element.44.refs_0_, bf16[4,4,16,128]{3,2,1,0:T(8,128)(2,1)S(1)} %collective-permute-done.4.refs_1_, bf16[4,4,16,128]{3,2,1,0:T(8,128)(2,1)S(1)} %collective-permute-done.5.refs_2_, bf16[4,4,16,128]{3,2,1,0:T(8,128)(2,1)S(1)} %collective-permute-done.6.refs_3_, ...), custom_call_target="tpu_custom_call" | custom-call | tf_op jit(solution)/shard_map/back_yz/pallas_call | solution.py:438
  (1 shorter events, 0.0 us)
Async XLA Ops:
  2.5 8.5 %collective-permute-start = (bf16[2,4,64,128]{3,2,1,0:T(8,128)(2,1)S(1)}, bf16[2,4,64,128]{3,2,1,0:T(8,128)(2,1)S(1)}, u32[]{:S(2)}, u32[]{:S(2)}) collective-permute-start(bf16[2,4,64,128]{3,2,1,0:T(8,128)(2,1)S(1)} %get-tuple-element.31), channel_id=1, source_target_pairs={{0,1},{1,0},{2,3},{3,2},{4,5},{5,4},{6,7},{7,6},{8,9},{9,8},{10,11... | collective-permute-start | bytes 393224 | tf_op jit(solution)/shard_map/ppermute | solution.py:319
  5.5 6.4 %collective-permute-start.1 = (bf16[2,4,64,128]{3,2,1,0:T(8,128)(2,1)S(1)}, bf16[2,4,64,128]{3,2,1,0:T(8,128)(2,1)S(1)}, u32[]{:S(2)}, u32[]{:S(2)}) collective-permute-start(bf16[2,4,64,128]{3,2,1,0:T(8,128)(2,1)S(1)} %get-tuple-element.32), channel_id=1, source_target_pairs={{0,2},{1,3},{2,0},{3,1},{4,6},{5,7},{6,4},{7,5},{8,10},{9,11},{10,... | collective-permute-start | bytes 393224 | tf_op jit(solution)/shard_map/ppermute | solution.py:319
  7.1 6.0 %collective-permute-start.2 = (bf16[2,4,64,128]{3,2,1,0:T(8,128)(2,1)S(1)}, bf16[2,4,64,128]{3,2,1,0:T(8,128)(2,1)S(1)}, u32[]{:S(2)}, u32[]{:S(2)}) collective-permute-start(bf16[2,4,64,128]{3,2,1,0:T(8,128)(2,1)S(1)} %get-tuple-element.33), channel_id=1, source_target_pairs={{0,3},{1,2},{2,1},{3,0},{4,7},{5,6},{6,5},{7,4},{8,11},{9,10},{10,... | collective-permute-start | bytes 393224 | tf_op jit(solution)/shard_map/ppermute | solution.py:319
  7.1 39.7 %slice-start = ((s8[8388608]{0:T(1024)(128)(4,1)}), s8[4194304]{0:T(1024)(128)(4,1)S(1)}, s32[]{:S(2)}) async-start(s8[8388608]{0:T(1024)(128)(4,1)} %bitcast.5), calls=%async_computation.2 | async-start | bytes 8388608
  7.1 39.7 %slice-start.1 = ((s8[8388608]{0:T(1024)(128)(4,1)}), s8[4194304]{0:T(1024)(128)(4,1)S(1)}, s32[]{:S(2)}) async-start(s8[8388608]{0:T(1024)(128)(4,1)} %bitcast.5), calls=%async_computation.3 | async-start | bytes 8388608
  7.1 39.7 %copy-start = (f32[2,32,2,128,128]{4,3,2,1,0:T(8,128)S(1)}, f32[2,32,2,128,128]{4,3,2,1,0:T(8,128)}, u32[]{:S(2)}) copy-start(f32[2,32,2,128,128]{4,3,2,1,0:T(8,128)} %second.3) | copy-start | bytes 25165828
  45.7 9.2 %collective-permute-start.3 = (bf16[16,32,128]{2,1,0:T(8,128)(2,1)S(1)}, bf16[16,32,128]{2,1,0:T(8,128)(2,1)S(1)}, u32[]{:S(2)}, u32[]{:S(2)}) collective-permute-start(bf16[16,32,128]{2,1,0:T(8,128)(2,1)S(1)} %all_to_all.11.refs_0_.own), channel_id=1, source_target_pairs={{0,4},{4,0},{1,5},{5,1},{2,6},{6,2},{3,7},{7,3},{8,12},{12,8},{9,1... | collective-permute-start | bytes 393224 | tf_op jit(solution)/shard_map/ppermute | solution.py:324
  55.2 6.8 %collective-permute-start.5 = (bf16[4,4,16,128]{3,2,1,0:T(8,128)(2,1)S(1)}, bf16[4,4,16,128]{3,2,1,0:T(8,128)(2,1)S(1)}, u32[]{:S(2)}, u32[]{:S(2)}) collective-permute-start(bf16[4,4,16,128]{3,2,1,0:T(8,128)(2,1)S(1)} %get-tuple-element.46), channel_id=1, source_target_pairs={{0,2},{1,3},{2,0},{3,1},{4,6},{5,7},{6,4},{7,5},{8,10},{9,11},{10,... | collective-permute-start | bytes 196616 | tf_op jit(solution)/shard_map/ppermute | solution.py:319
  55.3 6.7 %collective-permute-start.6 = (bf16[4,4,16,128]{3,2,1,0:T(8,128)(2,1)S(1)}, bf16[4,4,16,128]{3,2,1,0:T(8,128)(2,1)S(1)}, u32[]{:S(2)}, u32[]{:S(2)}) collective-permute-start(bf16[4,4,16,128]{3,2,1,0:T(8,128)(2,1)S(1)} %get-tuple-element.47), channel_id=1, source_target_pairs={{0,3},{1,2},{2,1},{3,0},{4,7},{5,6},{6,5},{7,4},{8,11},{9,10},{10,... | collective-permute-start | bytes 196616 | tf_op jit(solution)/shard_map/ppermute | solution.py:319
  57.3 4.7 %collective-permute-start.4 = (bf16[4,4,16,128]{3,2,1,0:T(8,128)(2,1)S(1)}, bf16[4,4,16,128]{3,2,1,0:T(8,128)(2,1)S(1)}, u32[]{:S(2)}, u32[]{:S(2)}) collective-permute-start(bf16[4,4,16,128]{3,2,1,0:T(8,128)(2,1)S(1)} %get-tuple-element.45.refs_0_), channel_id=1, source_target_pairs={{0,1},{1,0},{2,3},{3,2},{4,5},{5,4},{6,7},{7,6},{8,9},{9,8},{10,11... | collective-permute-start | bytes 196616 | tf_op jit(solution)/shard_map/ppermute | solution.py:319

commit v7 on v6

--- a/solution.py
+++ b/solution.py
@@ -19,6 +19,7 @@
 STEP = 100
 MYZ = 128
 QUAD = 4
+PARTNERS = (0, 3, 1, 2)
 
 
 decay_first = 0.9
@@ -100,22 +101,23 @@
 
 
 def yz_kernel(field, cotangent, table, *refs):
-    blocks, (mixed, cells_in, sems) = refs[:QUAD], refs[QUAD:]
+    blocks, (table_in, cells_in, sems) = refs[:QUAD], refs[QUAD:]
     rows = table.shape[1]
     cells = field.shape[0]
     loads = [
-        pltpu.make_async_copy(table.at[lax.axis_index("quad") ^ r], mixed.at[pl.ds(r * rows, rows)], sems.at[r]) for r in range(QUAD)
+        pltpu.make_async_copy(table, table_in, sems.at[0]),
+        pltpu.make_async_copy(field, cells_in.at[0], sems.at[1]),
+        pltpu.make_async_copy(cotangent, cells_in.at[1], sems.at[2]),
     ]
-    for which, source in enumerate((field, cotangent)):
-        loads.append(pltpu.make_async_copy(source, cells_in.at[which], sems.at[len(loads)]))
     for load in loads:
         load.start()
     for load in loads:
         load.wait()
+    matrix = jnp.concatenate([table_in[lax.axis_index("quad") ^ r] for r in range(QUAD)], axis=0)
     for which in range(2):
         for x in range(0, cells, 2):
             pair = jnp.concatenate([cells_in[which, x], cells_in[which, x + 1]], axis=1)
-            result = dot(mixed[...], pair).astype(half)
+            result = dot(matrix, pair).astype(half)
             for r in range(QUAD):
                 piece = result[r * rows : (r + 1) * rows]
                 blocks[r][which, x] = piece[:, :C]
@@ -124,8 +126,8 @@
 
 def x_kernel(*refs):
     pieces, (table, out, held) = refs[:QUAD], refs[QUAD:]
-    for r in range(QUAD):
-        held[lax.axis_index("quad") ^ r] = pieces[r][...]
+    for r, piece in zip(PARTNERS, pieces):
+        held[lax.axis_index("quad") ^ r] = piece[...]
     matrix = table[lax.axis_index("half")]
     fields, cells, rows = held.shape[1:4]
     height = matrix.shape[1] // QUAD // cells
@@ -287,8 +289,8 @@
 
 def back_yz_kernel(*refs):
     pieces, (table, after, out, held) = refs[:QUAD], refs[QUAD:]
-    for r in range(QUAD):
-        held[lax.axis_index("quad") ^ r] = pieces[r][...]
+    for r, piece in zip(PARTNERS, pieces):
+        held[lax.axis_index("quad") ^ r] = piece[...]
     matrix = table[...]
     for x in range(0, out.shape[0], 2):
         columns = jnp.concatenate([held[:, k].reshape(-1, C) for k in (x, x + 1)], axis=1)
@@ -316,7 +318,7 @@
 
 
 def exchange(blocks):
-    moved = [lax.ppermute(blocks[r], "quad", [(q, q ^ r) for q in range(QUAD)]) for r in range(1, QUAD)]
+    moved = [lax.ppermute(blocks[r], "quad", [(q, q ^ r) for q in range(QUAD)]) for r in PARTNERS[1:]]
     return [blocks[0]] + moved
 
 
@@ -347,9 +349,9 @@
         in_specs=[HBM] * 3,
         out_specs=[VMEM] * QUAD,
         scratch_shapes=[
-            pltpu.VMEM((MYZ * 2, NY * NZ), half),
+            pltpu.VMEM(table_yz.shape, half),
             pltpu.VMEM((2,) + flat, half),
-            pltpu.SemaphoreType.DMA((QUAD + 2,)),
+            pltpu.SemaphoreType.DMA((3,)),
         ],
         compiler_params=params(8),
         name="yz_modes",

time: 63.4 us -> 62.2 us (0.981)
  blocking collectives: 30.8 us -> 29.8 us
    all_to_all x1, blocking collectives: 22.2 us -> 21.2 us  [fast(): arrived = lax.all_to_all(partial, ('dp', 'half', 'quad'), 0, 0, tiled=True)]
  transfers between devices with their start and end apart: 7 -> 7, of which waited for: 3 -> 3; matrix products, arithmetic and copies ran while one was open for 0% -> 0% of each run, Pallas kernels for 23% -> 24%
where the time goes in v7:
time: 62.2 us; the launch traced here: 62 us
  blocking collectives  29.8 us (48%)
  Pallas kernels  19.6 us (32%)
  starting transfers between devices  9.32 us (15%)
  waiting for transfers between devices  2.57 us (4%)
  between operations  0.73 us (1%)
    all_to_all x1, blocking collectives, fast(): arrived = lax.all_to_all(partial, ('dp', 'half', 'quad'), 0, 0, tiled=True)  21.2 us
    pallas_call x2, Pallas kernels, adam(): pl.pallas_call(functools.partial(adam_kernel, begin), out_shape=[pltpu.HB...  10.7 us
    all_to_all x1, blocking collectives, fast(): lax.all_to_all(sent.reshape(per_half), ('dp', 'quad'), 0, 0, tiled=True)  8.65 us
    ppermute x6, starting transfers between devices, exchange(): lax.ppermute(blocks[r], 'quad', [(q, q ^ r) for q in range(QUAD)])  8.24 us
    pallas_call x1, Pallas kernels, fast(): pl.pallas_call(stage_kernel, out_shape=[vmem(big)] + [vmem(t) for t in st...  3.88 us
    ppermute x6, waiting for transfers between devices, exchange(): lax.ppermute(blocks[r], 'quad', [(q, q ^ r) for q in range(QUAD)])  1.93 us
    pallas_call x1, Pallas kernels, fast(): pl.pallas_call(yz_kernel, out_shape=[pltpu.VMEM((2, cells, owners * heigh...  1.75 us
    pallas_call x1, Pallas kernels, fast(): pl.pallas_call(modes_kernel, out_shape=[pltpu.VMEM((owners, QUAD, rows, C...  1.49 us
  transfers between devices with their start and end apart: 7, of which 3 were waited for; matrix products, arithmetic and copies ran while one was open for 0% of the time, Pallas kernels for 24%

profile of v7, /device:TPU:0, one launch (start us, length us, event | category | flops | bytes accessed | tf_op | source)
XLA Modules:
  0.0 62.0 jit_solution(1627167710929820202)
XLA Ops:
  0.6 1.8 %yz_modes.1 = (bf16[2,4,64,128]{3,2,1,0:T(8,128)(2,1)S(1)}, bf16[2,4,64,128]{3,2,1,0:T(8,128)(2,1)S(1)}, bf16[2,4,64,128]{3,2,1,0:T(8,128)(2,1)S(1)}, bf16[2,4,64,128]{3,2,1,0:T(8,128)(2,1)S(1)}) custom-call(bf16[4,512,128]{2,1,0:T(8,128)(2,1)} %bitcast.9, bf16[4,512,128]{2,1,0:T(8,128)(2,1)} %bitcast.10, bf16[4,64,512]{2,1,0:T(8,128)(2,1)} %constant.12.clone.table), custom_call_target="tpu_custom_call" | custom-call | tf_op jit(solution)/shard_map/yz_modes/pallas_call | solution.py:346
  2.4 4.0 %collective-permute-start = (bf16[2,4,64,128]{3,2,1,0:T(8,128)(2,1)S(1)}, bf16[2,4,64,128]{3,2,1,0:T(8,128)(2,1)S(1)}, u32[]{:S(2)}, u32[]{:S(2)}) collective-permute-start(bf16[2,4,64,128]{3,2,1,0:T(8,128)(2,1)S(1)} %get-tuple-element.31), channel_id=1, source_target_pairs={{0,3},{1,2},{2,1},{3,0},{4,7},{5,6},{6,5},{7,4},{8,11},{9,10},{10,... | collective-permute-start | bytes 393224 | tf_op jit(solution)/shard_map/ppermute | solution.py:321
  6.4 0.5 collective-permute-start.1
  6.9 0.1 collective-permute-start.2
  7.1 0.0 slice-start
  7.1 0.0 slice-start.1
  7.1 0.0 copy-start
  7.1 3.9 %stage.1 = (f32[2,32,2,128,128]{4,3,2,1,0:T(8,128)S(1)}, bf16[2,256,256]{2,1,0:T(8,128)(2,1)S(1)}, bf16[256,256]{1,0:T(8,128)(2,1)S(1)}, bf16[128,128]{1,0:T(8,1...) custom-call(bf16[2,4,64,128]{3,2,1,0:T(8,128)(2,1)S(1)} %get-tuple-e, ...), custom_call_target="tpu_custom_call" | custom-call | tf_op jit(solution)/shard_map/stage/pallas_call | solution.py:363
  11.0 0.0 collective-permute-done.refs_1_
  11.0 1.8 %collective-permute-done.1.refs_2_ = bf16[2,4,64,128]{3,2,1,0:T(8,128)(2,1)S(1)} collective-permute-done((bf16[2,4,64,128]{3,2,1,0:T(8,128)(2,1)S(1)}, bf16[2,4,64,128]{3,2,1,0:T(8,128)(2,1)S(1)}, u32[]{:S(2)}, u32[]{:S(2)}) %collective-permute-start.1) | collective-permute-done | bytes 131104 | tf_op jit(solution)/shard_map/ppermute | solution.py:321
  12.7 0.2 collective-permute-done.2.refs_3_
  12.9 0.3 x_modes.1
  13.3 21.2 %all_to_all.10 = bf16[32,2,32,128]{3,2,1,0:T(8,128)(2,1)S(1)} all-to-all(bf16[32,2,32,128]{3,2,1,0:T(8,128)(2,1)S(1)} %x_modes.1), channel_id=1, replica_groups=mesh['dp'=4,'half'=2,'quad'=4] {'dp','half','quad'}, dimensions={0} | all-to-all | bytes 1048576 | tf_op jit(solution)/shard_map/all_to_all | solution.py:386
  34.4 1.5 %mode_grads.1 = (bf16[4,4,32,128]{3,2,1,0:T(8,128)(2,1)S(1)}, bf16[4,128,128]{2,1,0:T(8,128)(2,1)S(1)}, bf16[4,128,256]{2,1,0:T(8,128)(2,1)S(1)}) custom-call(bf16[4,2,4,2,32,128]{5,4,3,2,1,0:T(8,128)(2,1)S(1)} %bitcast.7, bf16[2,32,128,256]{3,2,1,0:T(8,128)(2,1)S(1)} %get-tuple-element.35.weights, bf16[256,256]{1,0:T(8,128)(2,1)S(1)} %get-tuple-element.36.gather, ...), custom_call_target="tpu_custom_call" | custom-call | tf_op jit(solution)/shard_map/mode_grads/pallas_call | solution.py:389
  35.9 8.6 %all_to_all.11.refs_0_.own = bf16[16,32,128]{2,1,0:T(8,128)(2,1)S(1)} all-to-all(bf16[16,32,128]{2,1,0:T(8,128)(2,1)S(1)} %bitcast.8), channel_id=1, replica_groups=mesh['dp'=4,'half'=2,'quad'=4] {'dp','quad'}, dimensions={0} | all-to-all | bytes 262144 | tf_op jit(solution)/shard_map/all_to_all | solution.py:401
  44.6 1.1 %collective-permute-start.3 = (bf16[16,32,128]{2,1,0:T(8,128)(2,1)S(1)}, bf16[16,32,128]{2,1,0:T(8,128)(2,1)S(1)}, u32[]{:S(2)}, u32[]{:S(2)}) collective-permute-start(bf16[16,32,128]{2,1,0:T(8,128)(2,1)S(1)} %all_to_all.11.refs_0_.own), channel_id=1, source_target_pairs={{0,4},{4,0},{1,5},{5,1},{2,6},{6,2},{3,7},{7,3},{8,12},{12,8},{9,1... | collective-permute-start | bytes 393224 | tf_op jit(solution)/shard_map/ppermute | solution.py:326
  45.6 0.0 slice-done
  45.6 0.0 slice-done.1
  45.6 0.0 copy-done
  45.7 7.5 %adam.2 = (f32[2,32,2,128,128]{4,3,2,1,0:T(8,128)}, f32[2,32,2,128,128]{4,3,2,1,0:T(8,128)}, f32[2,32,2,128,128]{4,3,2,1,0:T(8,128)}, f32[8,128]{1,0:T(8,128)S(1)}) custom-call(bf16[4,128,128]{2,1,0:T(8,128)(2,1)S(1)} %get-tuple-element.40.inputs, bf16[4,128,256]{2,1,0:T(8,128)(2,1)S(1)} %get-tuple-element.41.pairs, ...), custom_call_target="tpu_custom_call" | custom-call | bytes 25165824 | tf_op jit(solution)/shard_map/adam/pallas_call | solution.py:410
  53.2 0.6 %collective-permute-done.3.come = bf16[16,32,128]{2,1,0:T(8,128)(2,1)S(1)} collective-permute-done((bf16[16,32,128]{2,1,0:T(8,128)(2,1)S(1)}, bf16[16,32,128]{2,1,0:T(8,128)(2,1)S(1)}, u32[]{:S(2)}, u32[]{:S(2)}) %collective-permute-start.3) | collective-permute-done | bytes 131104 | tf_op jit(solution)/shard_map/ppermute | solution.py:326
  53.8 0.3 back_x.1
  54.1 0.1 collective-permute-start.4
  54.2 2.0 %collective-permute-start.6 = (bf16[4,4,16,128]{3,2,1,0:T(8,128)(2,1)S(1)}, bf16[4,4,16,128]{3,2,1,0:T(8,128)(2,1)S(1)}, u32[]{:S(2)}, u32[]{:S(2)}) collective-permute-start(bf16[4,4,16,128]{3,2,1,0:T(8,128)(2,1)S(1)} %get-tuple-element.47), channel_id=1, source_target_pairs={{0,2},{1,3},{2,0},{3,1},{4,6},{5,7},{6,4},{7,5},{8,10},{9,11},{10,... | collective-permute-start | bytes 196616 | tf_op jit(solution)/shard_map/ppermute | solution.py:321
  56.2 1.5 %collective-permute-start.5 = (bf16[4,4,16,128]{3,2,1,0:T(8,128)(2,1)S(1)}, bf16[4,4,16,128]{3,2,1,0:T(8,128)(2,1)S(1)}, u32[]{:S(2)}, u32[]{:S(2)}) collective-permute-start(bf16[4,4,16,128]{3,2,1,0:T(8,128)(2,1)S(1)} %get-tuple-element.46.refs_0_), channel_id=1, source_target_pairs={{0,1},{1,0},{2,3},{3,2},{4,5},{5,4},{6,7},{7,6},{8,9},{9,8},{10,11... | collective-permute-start | bytes 196616 | tf_op jit(solution)/shard_map/ppermute | solution.py:321
  57.6 3.2 %adam.3 = (f32[2,32,2,128,128]{4,3,2,1,0:T(8,128)}, f32[2,32,2,128,128]{4,3,2,1,0:T(8,128)}, f32[2,32,2,128,128]{4,3,2,1,0:T(8,128)}, f32[8,128]{1,0:T(8,128)S(1)}) custom-call(bf16[4,128,128]{2,1,0:T(8,128)(2,1)S(1)} %get-tuple-element.40.inputs, ...), custom_call_target="tpu_custom_call", output_to_operand_aliasing={{0}: (6, {}), {1}: (7, {}), {2}: (8, {})} | custom-call | bytes 8388608 | tf_op jit(solution)/shard_map/adam/pallas_call | solution.py:410
  60.9 0.0 collective-permute-done.4.refs_1_
  60.9 0.0 collective-permute-done.6.refs_3_
  60.9 0.0 collective-permute-done.5.refs_2_
  60.9 1.1 %back_yz.1 = bf16[4,512,128]{2,1,0:T(8,128)(2,1)} custom-call(bf16[4,4,16,128]{3,2,1,0:T(8,128)(2,1)S(1)} %get-tuple-element.44.refs_0_, bf16[4,4,16,128]{3,2,1,0:T(8,128)(2,1)S(1)} %collective-permute-done.4.refs_1_, bf16[4,4,16,128]{3,2,1,0:T(8,128)(2,1)S(1)} %collective-permute-done.5.refs_2_, bf16[4,4,16,128]{3,2,1,0:T(8,128)(2,1)S(1)} %collective-permute-done.6.refs_3_, ...), custom_call_target="tpu_custom_call" | custom-call | tf_op jit(solution)/shard_map/back_yz/pallas_call | solution.py:440
  (1 shorter events, 0.0 us)
Async XLA Ops:
  2.4 8.6 %collective-permute-start = (bf16[2,4,64,128]{3,2,1,0:T(8,128)(2,1)S(1)}, bf16[2,4,64,128]{3,2,1,0:T(8,128)(2,1)S(1)}, u32[]{:S(2)}, u32[]{:S(2)}) collective-permute-start(bf16[2,4,64,128]{3,2,1,0:T(8,128)(2,1)S(1)} %get-tuple-element.31), channel_id=1, source_target_pairs={{0,3},{1,2},{2,1},{3,0},{4,7},{5,6},{6,5},{7,4},{8,11},{9,10},{10,... | collective-permute-start | bytes 393224 | tf_op jit(solution)/shard_map/ppermute | solution.py:321
  6.4 6.3 %collective-permute-start.1 = (bf16[2,4,64,128]{3,2,1,0:T(8,128)(2,1)S(1)}, bf16[2,4,64,128]{3,2,1,0:T(8,128)(2,1)S(1)}, u32[]{:S(2)}, u32[]{:S(2)}) collective-permute-start(bf16[2,4,64,128]{3,2,1,0:T(8,128)(2,1)S(1)} %get-tuple-element.32), channel_id=1, source_target_pairs={{0,1},{1,0},{2,3},{3,2},{4,5},{5,4},{6,7},{7,6},{8,9},{9,8},{10,11... | collective-permute-start | bytes 393224 | tf_op jit(solution)/shard_map/ppermute | solution.py:321
  6.9 6.0 %collective-permute-start.2 = (bf16[2,4,64,128]{3,2,1,0:T(8,128)(2,1)S(1)}, bf16[2,4,64,128]{3,2,1,0:T(8,128)(2,1)S(1)}, u32[]{:S(2)}, u32[]{:S(2)}) collective-permute-start(bf16[2,4,64,128]{3,2,1,0:T(8,128)(2,1)S(1)} %get-tuple-element.33), channel_id=1, source_target_pairs={{0,2},{1,3},{2,0},{3,1},{4,6},{5,7},{6,4},{7,5},{8,10},{9,11},{10,... | collective-permute-start | bytes 393224 | tf_op jit(solution)/shard_map/ppermute | solution.py:321
  7.1 38.6 %slice-start = ((s8[8388608]{0:T(1024)(128)(4,1)}), s8[4194304]{0:T(1024)(128)(4,1)S(1)}, s32[]{:S(2)}) async-start(s8[8388608]{0:T(1024)(128)(4,1)} %bitcast.5), calls=%async_computation.2 | async-start | bytes 8388608
  7.1 38.6 %slice-start.1 = ((s8[8388608]{0:T(1024)(128)(4,1)}), s8[4194304]{0:T(1024)(128)(4,1)S(1)}, s32[]{:S(2)}) async-start(s8[8388608]{0:T(1024)(128)(4,1)} %bitcast.5), calls=%async_computation.3 | async-start | bytes 8388608
  7.1 38.6 %copy-start = (f32[2,32,2,128,128]{4,3,2,1,0:T(8,128)S(1)}, f32[2,32,2,128,128]{4,3,2,1,0:T(8,128)}, u32[]{:S(2)}) copy-start(f32[2,32,2,128,128]{4,3,2,1,0:T(8,128)} %second.3) | copy-start | bytes 25165828
  44.6 9.2 %collective-permute-start.3 = (bf16[16,32,128]{2,1,0:T(8,128)(2,1)S(1)}, bf16[16,32,128]{2,1,0:T(8,128)(2,1)S(1)}, u32[]{:S(2)}, u32[]{:S(2)}) collective-permute-start(bf16[16,32,128]{2,1,0:T(8,128)(2,1)S(1)} %all_to_all.11.refs_0_.own), channel_id=1, source_target_pairs={{0,4},{4,0},{1,5},{5,1},{2,6},{6,2},{3,7},{7,3},{8,12},{12,8},{9,1... | collective-permute-start | bytes 393224 | tf_op jit(solution)/shard_map/ppermute | solution.py:326
  54.1 6.8 %collective-permute-start.4 = (bf16[4,4,16,128]{3,2,1,0:T(8,128)(2,1)S(1)}, bf16[4,4,16,128]{3,2,1,0:T(8,128)(2,1)S(1)}, u32[]{:S(2)}, u32[]{:S(2)}) collective-permute-start(bf16[4,4,16,128]{3,2,1,0:T(8,128)(2,1)S(1)} %get-tuple-element.45), channel_id=1, source_target_pairs={{0,3},{1,2},{2,1},{3,0},{4,7},{5,6},{6,5},{7,4},{8,11},{9,10},{10,... | collective-permute-start | bytes 196616 | tf_op jit(solution)/shard_map/ppermute | solution.py:321
  54.2 6.7 %collective-permute-start.6 = (bf16[4,4,16,128]{3,2,1,0:T(8,128)(2,1)S(1)}, bf16[4,4,16,128]{3,2,1,0:T(8,128)(2,1)S(1)}, u32[]{:S(2)}, u32[]{:S(2)}) collective-permute-start(bf16[4,4,16,128]{3,2,1,0:T(8,128)(2,1)S(1)} %get-tuple-element.47), channel_id=1, source_target_pairs={{0,2},{1,3},{2,0},{3,1},{4,6},{5,7},{6,4},{7,5},{8,10},{9,11},{10,... | collective-permute-start | bytes 196616 | tf_op jit(solution)/shard_map/ppermute | solution.py:321
  56.2 4.7 %collective-permute-start.5 = (bf16[4,4,16,128]{3,2,1,0:T(8,128)(2,1)S(1)}, bf16[4,4,16,128]{3,2,1,0:T(8,128)(2,1)S(1)}, u32[]{:S(2)}, u32[]{:S(2)}) collective-permute-start(bf16[4,4,16,128]{3,2,1,0:T(8,128)(2,1)S(1)} %get-tuple-element.46.refs_0_), channel_id=1, source_target_pairs={{0,1},{1,0},{2,3},{3,2},{4,5},{5,4},{6,7},{7,6},{8,9},{9,8},{10,11... | collective-permute-start | bytes 196616 | tf_op jit(solution)/shard_map/ppermute | solution.py:321

commit v8 on v7

--- a/solution.py
+++ b/solution.py
@@ -403,7 +403,7 @@
 
     count = 4
     total = modes * QUAD * pencils // count
-    first_steps = total * 12 // 16
+    first_steps = total * 13 // 16
 
     def adam(begin, end, after, *before):
         steps = end - begin

time: 62.2 us -> 61.8 us (level)
  no operation moved by 1% of the time
where the time goes in v8:
time: 61.8 us; the launch traced here: 61.5 us
  blocking collectives  29.8 us (48%)
  Pallas kernels  19.6 us (32%)
  starting transfers between devices  9.32 us (15%)
  waiting for transfers between devices  2.06 us (3%)
  between operations  0.72 us (1%)
    all_to_all x1, blocking collectives, fast(): arrived = lax.all_to_all(partial, ('dp', 'half', 'quad'), 0, 0, tiled=True)  21.2 us
    pallas_call x2, Pallas kernels, adam(): pl.pallas_call(functools.partial(adam_kernel, begin), out_shape=[pltpu.HB...  10.8 us
    all_to_all x1, blocking collectives, fast(): lax.all_to_all(sent.reshape(per_half), ('dp', 'quad'), 0, 0, tiled=True)  8.65 us
    ppermute x6, starting transfers between devices, exchange(): lax.ppermute(blocks[r], 'quad', [(q, q ^ r) for q in range(QUAD)])  8.24 us
    pallas_call x1, Pallas kernels, fast(): pl.pallas_call(stage_kernel, out_shape=[vmem(big)] + [vmem(t) for t in st...  3.88 us
    ppermute x6, waiting for transfers between devices, exchange(): lax.ppermute(blocks[r], 'quad', [(q, q ^ r) for q in range(QUAD)])  1.95 us
    pallas_call x1, Pallas kernels, fast(): pl.pallas_call(yz_kernel, out_shape=[pltpu.VMEM((2, cells, owners * heigh...  1.75 us
    pallas_call x1, Pallas kernels, fast(): pl.pallas_call(modes_kernel, out_shape=[pltpu.VMEM((owners, QUAD, rows, C...  1.49 us
  transfers between devices with their start and end apart: 7, of which 3 were waited for; matrix products, arithmetic and copies ran while one was open for 0% of the time, Pallas kernels for 24%

profile of v8, /device:TPU:0, one launch (start us, length us, event | category | flops | bytes accessed | tf_op | source)
XLA Modules:
  0.0 61.5 jit_solution(13454095959705915756)
XLA Ops:
  0.6 1.8 %yz_modes.1 = (bf16[2,4,64,128]{3,2,1,0:T(8,128)(2,1)S(1)}, bf16[2,4,64,128]{3,2,1,0:T(8,128)(2,1)S(1)}, bf16[2,4,64,128]{3,2,1,0:T(8,128)(2,1)S(1)}, bf16[2,4,64,128]{3,2,1,0:T(8,128)(2,1)S(1)}) custom-call(bf16[4,512,128]{2,1,0:T(8,128)(2,1)} %bitcast.9, bf16[4,512,128]{2,1,0:T(8,128)(2,1)} %bitcast.10, bf16[4,64,512]{2,1,0:T(8,128)(2,1)} %constant.12.clone.table), custom_call_target="tpu_custom_call" | custom-call | tf_op jit(solution)/shard_map/yz_modes/pallas_call | solution.py:346
  2.4 4.0 %collective-permute-start = (bf16[2,4,64,128]{3,2,1,0:T(8,128)(2,1)S(1)}, bf16[2,4,64,128]{3,2,1,0:T(8,128)(2,1)S(1)}, u32[]{:S(2)}, u32[]{:S(2)}) collective-permute-start(bf16[2,4,64,128]{3,2,1,0:T(8,128)(2,1)S(1)} %get-tuple-element.31), channel_id=1, source_target_pairs={{0,3},{1,2},{2,1},{3,0},{4,7},{5,6},{6,5},{7,4},{8,11},{9,10},{10,... | collective-permute-start | bytes 393224 | tf_op jit(solution)/shard_map/ppermute | solution.py:321
  6.4 0.5 collective-permute-start.1
  6.9 0.1 collective-permute-start.2
  7.1 0.0 slice-start
  7.1 0.0 slice-start.1
  7.1 0.0 copy-start
  7.1 3.9 %stage.1 = (f32[2,32,2,128,128]{4,3,2,1,0:T(8,128)S(1)}, bf16[2,256,256]{2,1,0:T(8,128)(2,1)S(1)}, bf16[256,256]{1,0:T(8,128)(2,1)S(1)}, bf16[128,128]{1,0:T(8,1...) custom-call(bf16[2,4,64,128]{3,2,1,0:T(8,128)(2,1)S(1)} %get-tuple-e, ...), custom_call_target="tpu_custom_call" | custom-call | tf_op jit(solution)/shard_map/stage/pallas_call | solution.py:363
  11.0 0.0 collective-permute-done.refs_1_
  11.0 1.8 %collective-permute-done.1.refs_2_ = bf16[2,4,64,128]{3,2,1,0:T(8,128)(2,1)S(1)} collective-permute-done((bf16[2,4,64,128]{3,2,1,0:T(8,128)(2,1)S(1)}, bf16[2,4,64,128]{3,2,1,0:T(8,128)(2,1)S(1)}, u32[]{:S(2)}, u32[]{:S(2)}) %collective-permute-start.1) | collective-permute-done | bytes 131104 | tf_op jit(solution)/shard_map/ppermute | solution.py:321
  12.7 0.2 collective-permute-done.2.refs_3_
  12.9 0.3 x_modes.1
  13.3 21.2 %all_to_all.10 = bf16[32,2,32,128]{3,2,1,0:T(8,128)(2,1)S(1)} all-to-all(bf16[32,2,32,128]{3,2,1,0:T(8,128)(2,1)S(1)} %x_modes.1), channel_id=1, replica_groups=mesh['dp'=4,'half'=2,'quad'=4] {'dp','half','quad'}, dimensions={0} | all-to-all | bytes 1048576 | tf_op jit(solution)/shard_map/all_to_all | solution.py:386
  34.4 1.5 %mode_grads.1 = (bf16[4,4,32,128]{3,2,1,0:T(8,128)(2,1)S(1)}, bf16[4,128,128]{2,1,0:T(8,128)(2,1)S(1)}, bf16[4,128,256]{2,1,0:T(8,128)(2,1)S(1)}) custom-call(bf16[4,2,4,2,32,128]{5,4,3,2,1,0:T(8,128)(2,1)S(1)} %bitcast.7, bf16[2,32,128,256]{3,2,1,0:T(8,128)(2,1)S(1)} %get-tuple-element.35.weights, bf16[256,256]{1,0:T(8,128)(2,1)S(1)} %get-tuple-element.36.gather, ...), custom_call_target="tpu_custom_call" | custom-call | tf_op jit(solution)/shard_map/mode_grads/pallas_call | solution.py:389
  35.9 8.6 %all_to_all.11.refs_0_.own = bf16[16,32,128]{2,1,0:T(8,128)(2,1)S(1)} all-to-all(bf16[16,32,128]{2,1,0:T(8,128)(2,1)S(1)} %bitcast.8), channel_id=1, replica_groups=mesh['dp'=4,'half'=2,'quad'=4] {'dp','quad'}, dimensions={0} | all-to-all | bytes 262144 | tf_op jit(solution)/shard_map/all_to_all | solution.py:401
  44.6 1.1 %collective-permute-start.3 = (bf16[16,32,128]{2,1,0:T(8,128)(2,1)S(1)}, bf16[16,32,128]{2,1,0:T(8,128)(2,1)S(1)}, u32[]{:S(2)}, u32[]{:S(2)}) collective-permute-start(bf16[16,32,128]{2,1,0:T(8,128)(2,1)S(1)} %all_to_all.11.refs_0_.own), channel_id=1, source_target_pairs={{0,4},{4,0},{1,5},{5,1},{2,6},{6,2},{3,7},{7,3},{8,12},{12,8},{9,1... | collective-permute-start | bytes 393224 | tf_op jit(solution)/shard_map/ppermute | solution.py:326
  45.6 0.0 slice-done
  45.6 0.0 slice-done.1
  45.6 0.0 copy-done
  45.7 8.0 %adam.2 = (f32[2,32,2,128,128]{4,3,2,1,0:T(8,128)}, f32[2,32,2,128,128]{4,3,2,1,0:T(8,128)}, f32[2,32,2,128,128]{4,3,2,1,0:T(8,128)}, f32[8,128]{1,0:T(8,128)S(1)}) custom-call(bf16[4,128,128]{2,1,0:T(8,128)(2,1)S(1)} %get-tuple-element.40.inputs, bf16[4,128,256]{2,1,0:T(8,128)(2,1)S(1)} %get-tuple-element.41.pairs, ...), custom_call_target="tpu_custom_call" | custom-call | bytes 27262976 | tf_op jit(solution)/shard_map/adam/pallas_call | solution.py:410
  53.7 0.1 collective-permute-done.3.come
  53.8 0.3 back_x.1
  54.1 0.6 %collective-permute-start.4 = (bf16[4,4,16,128]{3,2,1,0:T(8,128)(2,1)S(1)}, bf16[4,4,16,128]{3,2,1,0:T(8,128)(2,1)S(1)}, u32[]{:S(2)}, u32[]{:S(2)}) collective-permute-start(bf16[4,4,16,128]{3,2,1,0:T(8,128)(2,1)S(1)} %get-tuple-element.45), channel_id=1, source_target_pairs={{0,3},{1,2},{2,1},{3,0},{4,7},{5,6},{6,5},{7,4},{8,11},{9,10},{10,... | collective-permute-start | bytes 196616 | tf_op jit(solution)/shard_map/ppermute | solution.py:321
  54.7 1.5 %collective-permute-start.6 = (bf16[4,4,16,128]{3,2,1,0:T(8,128)(2,1)S(1)}, bf16[4,4,16,128]{3,2,1,0:T(8,128)(2,1)S(1)}, u32[]{:S(2)}, u32[]{:S(2)}) collective-permute-start(bf16[4,4,16,128]{3,2,1,0:T(8,128)(2,1)S(1)} %get-tuple-element.47), channel_id=1, source_target_pairs={{0,2},{1,3},{2,0},{3,1},{4,6},{5,7},{6,4},{7,5},{8,10},{9,11},{10,... | collective-permute-start | bytes 196616 | tf_op jit(solution)/shard_map/ppermute | solution.py:321
  56.2 1.5 %collective-permute-start.5 = (bf16[4,4,16,128]{3,2,1,0:T(8,128)(2,1)S(1)}, bf16[4,4,16,128]{3,2,1,0:T(8,128)(2,1)S(1)}, u32[]{:S(2)}, u32[]{:S(2)}) collective-permute-start(bf16[4,4,16,128]{3,2,1,0:T(8,128)(2,1)S(1)} %get-tuple-element.46.refs_0_), channel_id=1, source_target_pairs={{0,1},{1,0},{2,3},{3,2},{4,5},{5,4},{6,7},{7,6},{8,9},{9,8},{10,11... | collective-permute-start | bytes 196616 | tf_op jit(solution)/shard_map/ppermute | solution.py:321
  57.6 2.7 %adam.3 = (f32[2,32,2,128,128]{4,3,2,1,0:T(8,128)}, f32[2,32,2,128,128]{4,3,2,1,0:T(8,128)}, f32[2,32,2,128,128]{4,3,2,1,0:T(8,128)}, f32[8,128]{1,0:T(8,128)S(1)}) custom-call(bf16[4,128,128]{2,1,0:T(8,128)(2,1)S(1)} %get-tuple-element.40.inputs, ...), custom_call_target="tpu_custom_call", output_to_operand_aliasing={{0}: (6, {}), {1}: (7, {}), {2}: (8, {})} | custom-call | bytes 6291456 | tf_op jit(solution)/shard_map/adam/pallas_call | solution.py:410
  60.4 0.0 collective-permute-done.4.refs_1_
  60.4 0.0 collective-permute-done.6.refs_3_
  60.4 0.0 collective-permute-done.5.refs_2_
  60.4 1.1 %back_yz.1 = bf16[4,512,128]{2,1,0:T(8,128)(2,1)} custom-call(bf16[4,4,16,128]{3,2,1,0:T(8,128)(2,1)S(1)} %get-tuple-element.44.refs_0_, bf16[4,4,16,128]{3,2,1,0:T(8,128)(2,1)S(1)} %collective-permute-done.4.refs_1_, bf16[4,4,16,128]{3,2,1,0:T(8,128)(2,1)S(1)} %collective-permute-done.5.refs_2_, bf16[4,4,16,128]{3,2,1,0:T(8,128)(2,1)S(1)} %collective-permute-done.6.refs_3_, ...), custom_call_target="tpu_custom_call" | custom-call | tf_op jit(solution)/shard_map/back_yz/pallas_call | solution.py:440
  (1 shorter events, 0.0 us)
Async XLA Ops:
  2.4 8.6 %collective-permute-start = (bf16[2,4,64,128]{3,2,1,0:T(8,128)(2,1)S(1)}, bf16[2,4,64,128]{3,2,1,0:T(8,128)(2,1)S(1)}, u32[]{:S(2)}, u32[]{:S(2)}) collective-permute-start(bf16[2,4,64,128]{3,2,1,0:T(8,128)(2,1)S(1)} %get-tuple-element.31), channel_id=1, source_target_pairs={{0,3},{1,2},{2,1},{3,0},{4,7},{5,6},{6,5},{7,4},{8,11},{9,10},{10,... | collective-permute-start | bytes 393224 | tf_op jit(solution)/shard_map/ppermute | solution.py:321
  6.4 6.3 %collective-permute-start.1 = (bf16[2,4,64,128]{3,2,1,0:T(8,128)(2,1)S(1)}, bf16[2,4,64,128]{3,2,1,0:T(8,128)(2,1)S(1)}, u32[]{:S(2)}, u32[]{:S(2)}) collective-permute-start(bf16[2,4,64,128]{3,2,1,0:T(8,128)(2,1)S(1)} %get-tuple-element.32), channel_id=1, source_target_pairs={{0,1},{1,0},{2,3},{3,2},{4,5},{5,4},{6,7},{7,6},{8,9},{9,8},{10,11... | collective-permute-start | bytes 393224 | tf_op jit(solution)/shard_map/ppermute | solution.py:321
  6.9 6.0 %collective-permute-start.2 = (bf16[2,4,64,128]{3,2,1,0:T(8,128)(2,1)S(1)}, bf16[2,4,64,128]{3,2,1,0:T(8,128)(2,1)S(1)}, u32[]{:S(2)}, u32[]{:S(2)}) collective-permute-start(bf16[2,4,64,128]{3,2,1,0:T(8,128)(2,1)S(1)} %get-tuple-element.33), channel_id=1, source_target_pairs={{0,2},{1,3},{2,0},{3,1},{4,6},{5,7},{6,4},{7,5},{8,10},{9,11},{10,... | collective-permute-start | bytes 393224 | tf_op jit(solution)/shard_map/ppermute | solution.py:321
  7.1 38.6 %slice-start = ((s8[8388608]{0:T(1024)(128)(4,1)}), s8[4194304]{0:T(1024)(128)(4,1)S(1)}, s32[]{:S(2)}) async-start(s8[8388608]{0:T(1024)(128)(4,1)} %bitcast.5), calls=%async_computation.2 | async-start | bytes 8388608
  7.1 38.6 %slice-start.1 = ((s8[8388608]{0:T(1024)(128)(4,1)}), s8[4194304]{0:T(1024)(128)(4,1)S(1)}, s32[]{:S(2)}) async-start(s8[8388608]{0:T(1024)(128)(4,1)} %bitcast.5), calls=%async_computation.3 | async-start | bytes 8388608
  7.1 38.6 %copy-start = (f32[2,32,2,128,128]{4,3,2,1,0:T(8,128)S(1)}, f32[2,32,2,128,128]{4,3,2,1,0:T(8,128)}, u32[]{:S(2)}) copy-start(f32[2,32,2,128,128]{4,3,2,1,0:T(8,128)} %second.3) | copy-start | bytes 25165828
  44.6 9.2 %collective-permute-start.3 = (bf16[16,32,128]{2,1,0:T(8,128)(2,1)S(1)}, bf16[16,32,128]{2,1,0:T(8,128)(2,1)S(1)}, u32[]{:S(2)}, u32[]{:S(2)}) collective-permute-start(bf16[16,32,128]{2,1,0:T(8,128)(2,1)S(1)} %all_to_all.11.refs_0_.own), channel_id=1, source_target_pairs={{0,4},{4,0},{1,5},{5,1},{2,6},{6,2},{3,7},{7,3},{8,12},{12,8},{9,1... | collective-permute-start | bytes 393224 | tf_op jit(solution)/shard_map/ppermute | solution.py:326
  54.1 6.3 %collective-permute-start.4 = (bf16[4,4,16,128]{3,2,1,0:T(8,128)(2,1)S(1)}, bf16[4,4,16,128]{3,2,1,0:T(8,128)(2,1)S(1)}, u32[]{:S(2)}, u32[]{:S(2)}) collective-permute-start(bf16[4,4,16,128]{3,2,1,0:T(8,128)(2,1)S(1)} %get-tuple-element.45), channel_id=1, source_target_pairs={{0,3},{1,2},{2,1},{3,0},{4,7},{5,6},{6,5},{7,4},{8,11},{9,10},{10,... | collective-permute-start | bytes 196616 | tf_op jit(solution)/shard_map/ppermute | solution.py:321
  54.7 5.7 %collective-permute-start.6 = (bf16[4,4,16,128]{3,2,1,0:T(8,128)(2,1)S(1)}, bf16[4,4,16,128]{3,2,1,0:T(8,128)(2,1)S(1)}, u32[]{:S(2)}, u32[]{:S(2)}) collective-permute-start(bf16[4,4,16,128]{3,2,1,0:T(8,128)(2,1)S(1)} %get-tuple-element.47), channel_id=1, source_target_pairs={{0,2},{1,3},{2,0},{3,1},{4,6},{5,7},{6,4},{7,5},{8,10},{9,11},{10,... | collective-permute-start | bytes 196616 | tf_op jit(solution)/shard_map/ppermute | solution.py:321
  56.2 4.3 %collective-permute-start.5 = (bf16[4,4,16,128]{3,2,1,0:T(8,128)(2,1)S(1)}, bf16[4,4,16,128]{3,2,1,0:T(8,128)(2,1)S(1)}, u32[]{:S(2)}, u32[]{:S(2)}) collective-permute-start(bf16[4,4,16,128]{3,2,1,0:T(8,128)(2,1)S(1)} %get-tuple-element.46.refs_0_), channel_id=1, source_target_pairs={{0,1},{1,0},{2,3},{3,2},{4,5},{5,4},{6,7},{7,6},{8,9},{9,8},{10,11... | collective-permute-start | bytes 196616 | tf_op jit(solution)/shard_map/ppermute | solution.py:321

commit v9 on v8

--- a/solution.py
+++ b/solution.py
@@ -185,12 +185,12 @@
     modes, pencils = weights.shape[0], weights.shape[1] // quad
     height = batch * 2
     columns_out = []
+    wide = [arrived[:, :, q, f].reshape(-1, C) for q in range(quad) for f in range(2)]
+    gathered = dot(gather[...], jnp.concatenate(wide, axis=1)).astype(half)
+    count = gathered.shape[0] // 2
     all_pairs = []
     for q in range(quad):
-        field = arrived[:, :, q, 0].reshape(-1, C)
-        cot = arrived[:, :, q, 1].reshape(-1, C)
-        both = dot(gather[...], jnp.concatenate([field, cot], axis=1)).astype(half)
-        count = both.shape[0] // 2
+        both = gathered[:, q * 2 * C : (q + 1) * 2 * C]
         inputs[q] = both[:count, :C]
         pair = jnp.concatenate([both[:count, C:], both[count:, C:]], axis=1)
         pairs[q] = pair

time: 61.8 us -> 61.8 us (level)
  no operation moved by 1% of the time
where the time goes in v9:
time: 61.8 us; the launch traced here: 61.5 us
  blocking collectives  29.8 us (48%)
  Pallas kernels  19.6 us (32%)
  starting transfers between devices  9.32 us (15%)
  waiting for transfers between devices  2.06 us (3%)
  between operations  0.72 us (1%)
    all_to_all x1, blocking collectives, fast(): arrived = lax.all_to_all(partial, ('dp', 'half', 'quad'), 0, 0, tiled=True)  21.2 us
    pallas_call x2, Pallas kernels, adam(): pl.pallas_call(functools.partial(adam_kernel, begin), out_shape=[pltpu.HB...  10.8 us
    all_to_all x1, blocking collectives, fast(): lax.all_to_all(sent.reshape(per_half), ('dp', 'quad'), 0, 0, tiled=True)  8.65 us
    ppermute x6, starting transfers between devices, exchange(): lax.ppermute(blocks[r], 'quad', [(q, q ^ r) for q in range(QUAD)])  8.24 us
    pallas_call x1, Pallas kernels, fast(): pl.pallas_call(stage_kernel, out_shape=[vmem(big)] + [vmem(t) for t in st...  3.88 us
    ppermute x6, waiting for transfers between devices, exchange(): lax.ppermute(blocks[r], 'quad', [(q, q ^ r) for q in range(QUAD)])  1.95 us
    pallas_call x1, Pallas kernels, fast(): pl.pallas_call(yz_kernel, out_shape=[pltpu.VMEM((2, cells, owners * heigh...  1.75 us
    pallas_call x1, Pallas kernels, fast(): pl.pallas_call(modes_kernel, out_shape=[pltpu.VMEM((owners, QUAD, rows, C...  1.49 us
  transfers between devices with their start and end apart: 7, of which 3 were waited for; matrix products, arithmetic and copies ran while one was open for 0% of the time, Pallas kernels for 24%

profile of v9, /device:TPU:0, one launch (start us, length us, event | category | flops | bytes accessed | tf_op | source)
XLA Modules:
  0.0 61.5 jit_solution(5549989815483510684)
XLA Ops:
  0.6 1.8 %yz_modes.1 = (bf16[2,4,64,128]{3,2,1,0:T(8,128)(2,1)S(1)}, bf16[2,4,64,128]{3,2,1,0:T(8,128)(2,1)S(1)}, bf16[2,4,64,128]{3,2,1,0:T(8,128)(2,1)S(1)}, bf16[2,4,64,128]{3,2,1,0:T(8,128)(2,1)S(1)}) custom-call(bf16[4,512,128]{2,1,0:T(8,128)(2,1)} %bitcast.9, bf16[4,512,128]{2,1,0:T(8,128)(2,1)} %bitcast.10, bf16[4,64,512]{2,1,0:T(8,128)(2,1)} %constant.12.clone.table), custom_call_target="tpu_custom_call" | custom-call | tf_op jit(solution)/shard_map/yz_modes/pallas_call | solution.py:346
  2.4 4.0 %collective-permute-start = (bf16[2,4,64,128]{3,2,1,0:T(8,128)(2,1)S(1)}, bf16[2,4,64,128]{3,2,1,0:T(8,128)(2,1)S(1)}, u32[]{:S(2)}, u32[]{:S(2)}) collective-permute-start(bf16[2,4,64,128]{3,2,1,0:T(8,128)(2,1)S(1)} %get-tuple-element.31), channel_id=1, source_target_pairs={{0,3},{1,2},{2,1},{3,0},{4,7},{5,6},{6,5},{7,4},{8,11},{9,10},{10,... | collective-permute-start | bytes 393224 | tf_op jit(solution)/shard_map/ppermute | solution.py:321
  6.4 0.5 collective-permute-start.1
  6.9 0.1 collective-permute-start.2
  7.1 0.0 slice-start
  7.1 0.0 slice-start.1
  7.1 0.0 copy-start
  7.1 3.9 %stage.1 = (f32[2,32,2,128,128]{4,3,2,1,0:T(8,128)S(1)}, bf16[2,256,256]{2,1,0:T(8,128)(2,1)S(1)}, bf16[256,256]{1,0:T(8,128)(2,1)S(1)}, bf16[128,128]{1,0:T(8,1...) custom-call(bf16[2,4,64,128]{3,2,1,0:T(8,128)(2,1)S(1)} %get-tuple-e, ...), custom_call_target="tpu_custom_call" | custom-call | tf_op jit(solution)/shard_map/stage/pallas_call | solution.py:363
  11.0 0.0 collective-permute-done.refs_1_
  11.0 1.8 %collective-permute-done.1.refs_2_ = bf16[2,4,64,128]{3,2,1,0:T(8,128)(2,1)S(1)} collective-permute-done((bf16[2,4,64,128]{3,2,1,0:T(8,128)(2,1)S(1)}, bf16[2,4,64,128]{3,2,1,0:T(8,128)(2,1)S(1)}, u32[]{:S(2)}, u32[]{:S(2)}) %collective-permute-start.1) | collective-permute-done | bytes 131104 | tf_op jit(solution)/shard_map/ppermute | solution.py:321
  12.7 0.2 collective-permute-done.2.refs_3_
  12.9 0.3 x_modes.1
  13.3 21.2 %all_to_all.10 = bf16[32,2,32,128]{3,2,1,0:T(8,128)(2,1)S(1)} all-to-all(bf16[32,2,32,128]{3,2,1,0:T(8,128)(2,1)S(1)} %x_modes.1), channel_id=1, replica_groups=mesh['dp'=4,'half'=2,'quad'=4] {'dp','half','quad'}, dimensions={0} | all-to-all | bytes 1048576 | tf_op jit(solution)/shard_map/all_to_all | solution.py:386
  34.4 1.5 %mode_grads.1 = (bf16[4,4,32,128]{3,2,1,0:T(8,128)(2,1)S(1)}, bf16[4,128,128]{2,1,0:T(8,128)(2,1)S(1)}, bf16[4,128,256]{2,1,0:T(8,128)(2,1)S(1)}) custom-call(bf16[4,2,4,2,32,128]{5,4,3,2,1,0:T(8,128)(2,1)S(1)} %bitcast.7, bf16[2,32,128,256]{3,2,1,0:T(8,128)(2,1)S(1)} %get-tuple-element.35.weights, bf16[256,256]{1,0:T(8,128)(2,1)S(1)} %get-tuple-element.36.gather, ...), custom_call_target="tpu_custom_call" | custom-call | tf_op jit(solution)/shard_map/mode_grads/pallas_call | solution.py:389
  35.9 8.6 %all_to_all.11.refs_0_.own = bf16[16,32,128]{2,1,0:T(8,128)(2,1)S(1)} all-to-all(bf16[16,32,128]{2,1,0:T(8,128)(2,1)S(1)} %bitcast.8), channel_id=1, replica_groups=mesh['dp'=4,'half'=2,'quad'=4] {'dp','quad'}, dimensions={0} | all-to-all | bytes 262144 | tf_op jit(solution)/shard_map/all_to_all | solution.py:401
  44.6 1.1 %collective-permute-start.3 = (bf16[16,32,128]{2,1,0:T(8,128)(2,1)S(1)}, bf16[16,32,128]{2,1,0:T(8,128)(2,1)S(1)}, u32[]{:S(2)}, u32[]{:S(2)}) collective-permute-start(bf16[16,32,128]{2,1,0:T(8,128)(2,1)S(1)} %all_to_all.11.refs_0_.own), channel_id=1, source_target_pairs={{0,4},{4,0},{1,5},{5,1},{2,6},{6,2},{3,7},{7,3},{8,12},{12,8},{9,1... | collective-permute-start | bytes 393224 | tf_op jit(solution)/shard_map/ppermute | solution.py:326
  45.6 0.0 slice-done
  45.6 0.0 slice-done.1
  45.6 0.0 copy-done
  45.7 8.0 %adam.2 = (f32[2,32,2,128,128]{4,3,2,1,0:T(8,128)}, f32[2,32,2,128,128]{4,3,2,1,0:T(8,128)}, f32[2,32,2,128,128]{4,3,2,1,0:T(8,128)}, f32[8,128]{1,0:T(8,128)S(1)}) custom-call(bf16[4,128,128]{2,1,0:T(8,128)(2,1)S(1)} %get-tuple-element.40.inputs, bf16[4,128,256]{2,1,0:T(8,128)(2,1)S(1)} %get-tuple-element.41.pairs, ...), custom_call_target="tpu_custom_call" | custom-call | bytes 27262976 | tf_op jit(solution)/shard_map/adam/pallas_call | solution.py:410
  53.7 0.1 collective-permute-done.3.come
  53.8 0.3 back_x.1
  54.1 0.6 %collective-permute-start.4 = (bf16[4,4,16,128]{3,2,1,0:T(8,128)(2,1)S(1)}, bf16[4,4,16,128]{3,2,1,0:T(8,128)(2,1)S(1)}, u32[]{:S(2)}, u32[]{:S(2)}) collective-permute-start(bf16[4,4,16,128]{3,2,1,0:T(8,128)(2,1)S(1)} %get-tuple-element.45), channel_id=1, source_target_pairs={{0,3},{1,2},{2,1},{3,0},{4,7},{5,6},{6,5},{7,4},{8,11},{9,10},{10,... | collective-permute-start | bytes 196616 | tf_op jit(solution)/shard_map/ppermute | solution.py:321
  54.7 1.5 %collective-permute-start.6 = (bf16[4,4,16,128]{3,2,1,0:T(8,128)(2,1)S(1)}, bf16[4,4,16,128]{3,2,1,0:T(8,128)(2,1)S(1)}, u32[]{:S(2)}, u32[]{:S(2)}) collective-permute-start(bf16[4,4,16,128]{3,2,1,0:T(8,128)(2,1)S(1)} %get-tuple-element.47), channel_id=1, source_target_pairs={{0,2},{1,3},{2,0},{3,1},{4,6},{5,7},{6,4},{7,5},{8,10},{9,11},{10,... | collective-permute-start | bytes 196616 | tf_op jit(solution)/shard_map/ppermute | solution.py:321
  56.2 1.5 %collective-permute-start.5 = (bf16[4,4,16,128]{3,2,1,0:T(8,128)(2,1)S(1)}, bf16[4,4,16,128]{3,2,1,0:T(8,128)(2,1)S(1)}, u32[]{:S(2)}, u32[]{:S(2)}) collective-permute-start(bf16[4,4,16,128]{3,2,1,0:T(8,128)(2,1)S(1)} %get-tuple-element.46.refs_0_), channel_id=1, source_target_pairs={{0,1},{1,0},{2,3},{3,2},{4,5},{5,4},{6,7},{7,6},{8,9},{9,8},{10,11... | collective-permute-start | bytes 196616 | tf_op jit(solution)/shard_map/ppermute | solution.py:321
  57.6 2.7 %adam.3 = (f32[2,32,2,128,128]{4,3,2,1,0:T(8,128)}, f32[2,32,2,128,128]{4,3,2,1,0:T(8,128)}, f32[2,32,2,128,128]{4,3,2,1,0:T(8,128)}, f32[8,128]{1,0:T(8,128)S(1)}) custom-call(bf16[4,128,128]{2,1,0:T(8,128)(2,1)S(1)} %get-tuple-element.40.inputs, ...), custom_call_target="tpu_custom_call", output_to_operand_aliasing={{0}: (6, {}), {1}: (7, {}), {2}: (8, {})} | custom-call | bytes 6291456 | tf_op jit(solution)/shard_map/adam/pallas_call | solution.py:410
  60.4 0.0 collective-permute-done.4.refs_1_
  60.4 0.0 collective-permute-done.6.refs_3_
  60.4 0.0 collective-permute-done.5.refs_2_
  60.4 1.1 %back_yz.1 = bf16[4,512,128]{2,1,0:T(8,128)(2,1)} custom-call(bf16[4,4,16,128]{3,2,1,0:T(8,128)(2,1)S(1)} %get-tuple-element.44.refs_0_, bf16[4,4,16,128]{3,2,1,0:T(8,128)(2,1)S(1)} %collective-permute-done.4.refs_1_, bf16[4,4,16,128]{3,2,1,0:T(8,128)(2,1)S(1)} %collective-permute-done.5.refs_2_, bf16[4,4,16,128]{3,2,1,0:T(8,128)(2,1)S(1)} %collective-permute-done.6.refs_3_, ...), custom_call_target="tpu_custom_call" | custom-call | tf_op jit(solution)/shard_map/back_yz/pallas_call | solution.py:440
  (1 shorter events, 0.0 us)
Async XLA Ops:
  2.4 8.6 %collective-permute-start = (bf16[2,4,64,128]{3,2,1,0:T(8,128)(2,1)S(1)}, bf16[2,4,64,128]{3,2,1,0:T(8,128)(2,1)S(1)}, u32[]{:S(2)}, u32[]{:S(2)}) collective-permute-start(bf16[2,4,64,128]{3,2,1,0:T(8,128)(2,1)S(1)} %get-tuple-element.31), channel_id=1, source_target_pairs={{0,3},{1,2},{2,1},{3,0},{4,7},{5,6},{6,5},{7,4},{8,11},{9,10},{10,... | collective-permute-start | bytes 393224 | tf_op jit(solution)/shard_map/ppermute | solution.py:321
  6.4 6.3 %collective-permute-start.1 = (bf16[2,4,64,128]{3,2,1,0:T(8,128)(2,1)S(1)}, bf16[2,4,64,128]{3,2,1,0:T(8,128)(2,1)S(1)}, u32[]{:S(2)}, u32[]{:S(2)}) collective-permute-start(bf16[2,4,64,128]{3,2,1,0:T(8,128)(2,1)S(1)} %get-tuple-element.32), channel_id=1, source_target_pairs={{0,1},{1,0},{2,3},{3,2},{4,5},{5,4},{6,7},{7,6},{8,9},{9,8},{10,11... | collective-permute-start | bytes 393224 | tf_op jit(solution)/shard_map/ppermute | solution.py:321
  6.9 6.0 %collective-permute-start.2 = (bf16[2,4,64,128]{3,2,1,0:T(8,128)(2,1)S(1)}, bf16[2,4,64,128]{3,2,1,0:T(8,128)(2,1)S(1)}, u32[]{:S(2)}, u32[]{:S(2)}) collective-permute-start(bf16[2,4,64,128]{3,2,1,0:T(8,128)(2,1)S(1)} %get-tuple-element.33), channel_id=1, source_target_pairs={{0,2},{1,3},{2,0},{3,1},{4,6},{5,7},{6,4},{7,5},{8,10},{9,11},{10,... | collective-permute-start | bytes 393224 | tf_op jit(solution)/shard_map/ppermute | solution.py:321
  7.1 38.6 %slice-start = ((s8[8388608]{0:T(1024)(128)(4,1)}), s8[4194304]{0:T(1024)(128)(4,1)S(1)}, s32[]{:S(2)}) async-start(s8[8388608]{0:T(1024)(128)(4,1)} %bitcast.5), calls=%async_computation.2 | async-start | bytes 8388608
  7.1 38.6 %slice-start.1 = ((s8[8388608]{0:T(1024)(128)(4,1)}), s8[4194304]{0:T(1024)(128)(4,1)S(1)}, s32[]{:S(2)}) async-start(s8[8388608]{0:T(1024)(128)(4,1)} %bitcast.5), calls=%async_computation.3 | async-start | bytes 8388608
  7.1 38.6 %copy-start = (f32[2,32,2,128,128]{4,3,2,1,0:T(8,128)S(1)}, f32[2,32,2,128,128]{4,3,2,1,0:T(8,128)}, u32[]{:S(2)}) copy-start(f32[2,32,2,128,128]{4,3,2,1,0:T(8,128)} %second.3) | copy-start | bytes 25165828
  44.6 9.2 %collective-permute-start.3 = (bf16[16,32,128]{2,1,0:T(8,128)(2,1)S(1)}, bf16[16,32,128]{2,1,0:T(8,128)(2,1)S(1)}, u32[]{:S(2)}, u32[]{:S(2)}) collective-permute-start(bf16[16,32,128]{2,1,0:T(8,128)(2,1)S(1)} %all_to_all.11.refs_0_.own), channel_id=1, source_target_pairs={{0,4},{4,0},{1,5},{5,1},{2,6},{6,2},{3,7},{7,3},{8,12},{12,8},{9,1... | collective-permute-start | bytes 393224 | tf_op jit(solution)/shard_map/ppermute | solution.py:326
  54.1 6.3 %collective-permute-start.4 = (bf16[4,4,16,128]{3,2,1,0:T(8,128)(2,1)S(1)}, bf16[4,4,16,128]{3,2,1,0:T(8,128)(2,1)S(1)}, u32[]{:S(2)}, u32[]{:S(2)}) collective-permute-start(bf16[4,4,16,128]{3,2,1,0:T(8,128)(2,1)S(1)} %get-tuple-element.45), channel_id=1, source_target_pairs={{0,3},{1,2},{2,1},{3,0},{4,7},{5,6},{6,5},{7,4},{8,11},{9,10},{10,... | collective-permute-start | bytes 196616 | tf_op jit(solution)/shard_map/ppermute | solution.py:321
  54.7 5.7 %collective-permute-start.6 = (bf16[4,4,16,128]{3,2,1,0:T(8,128)(2,1)S(1)}, bf16[4,4,16,128]{3,2,1,0:T(8,128)(2,1)S(1)}, u32[]{:S(2)}, u32[]{:S(2)}) collective-permute-start(bf16[4,4,16,128]{3,2,1,0:T(8,128)(2,1)S(1)} %get-tuple-element.47), channel_id=1, source_target_pairs={{0,2},{1,3},{2,0},{3,1},{4,6},{5,7},{6,4},{7,5},{8,10},{9,11},{10,... | collective-permute-start | bytes 196616 | tf_op jit(solution)/shard_map/ppermute | solution.py:321
  56.2 4.3 %collective-permute-start.5 = (bf16[4,4,16,128]{3,2,1,0:T(8,128)(2,1)S(1)}, bf16[4,4,16,128]{3,2,1,0:T(8,128)(2,1)S(1)}, u32[]{:S(2)}, u32[]{:S(2)}) collective-permute-start(bf16[4,4,16,128]{3,2,1,0:T(8,128)(2,1)S(1)} %get-tuple-element.46.refs_0_), channel_id=1, source_target_pairs={{0,1},{1,0},{2,3},{3,2},{4,5},{5,4},{6,7},{7,6},{8,9},{9,8},{10,11... | collective-permute-start | bytes 196616 | tf_op jit(solution)/shard_map/ppermute | solution.py:321
